TPU v7x, 32 devices: a whole 2x2x4 slice. The times are simulated.
32 devices in a mesh: row: 4 (over x, core), col: 8 (over z, y).
Axes of the slice: x: 2, y: 2, z: 4, core: 2. Of those that a mesh axis runs over, the one named last changes fastest.
Arguments:
- start_block: float32 [65536, 128], P(('row', 'col')), may hold values from -6 to 6
- block_values: float32 [4, 16, 512, 512], P('row', 'col'), may hold values from -0.25 to 0.25
- block_rows: int32 [4, 16], P('row', 'col'), may hold values from 0 to 31, as said below
- block_cols: int32 [4, 16], P('row', 'col'), may hold values from 0 to 15
- block_count: int32 [4, 8], P('row', 'col'), may hold values from 1 to 2, as said below
- center: float32 [1], replicated, may hold values from 0.5 to 1
- radius: float32 [1], replicated, may hold values from 0.8 to 1.2
Outputs:
- basis_block: float32 [65536, 128], P(('row', 'col'))
- projected: float32 [128, 128], replicated
Inputs may be any that keep to these rules, and one draw needn't show every extreme that they name: `block_rows`: block row within the tile; the used slots of one tile name distinct block positions. `block_count`: some tile holds exactly 2 used slots in every draw.
All inputs are finite; a program needn't handle non-finite values.
Results may differ from a plain program's by a relative error of at most 0.0003.
Values sent between devices are 32-bit elements; how exact they have to be, the bound alone decides.
No kernel may reach another device: no remote copies, remote signals or barrier semaphores. Data moves between devices by JAX's collectives and lax.ppermute only.
A program may use at most 64 MiB of HBM per device.

v0:
```python
import jax
import jax.numpy as jnp
from jax import lax
from jax.sharding import PartitionSpec as P

ORDER = 65536
BS = 512


HIGHEST_PRECISION = lax.Precision.HIGHEST


def move_blocks(source, values, take_index, put_index, live_count, put_blocks, transpose):
    block_size = values.shape[-1]
    vec_width = source.shape[-1]
    picked = source.reshape(-1, block_size, vec_width)[take_index]
    pattern = "sba,sbv->sav" if transpose else "sab,sbv->sav"
    products = jnp.einsum(pattern, values, picked, precision=HIGHEST_PRECISION)
    live_mask = jnp.arange(values.shape[0]) < live_count
    onehot = ((put_index[None, :] == jnp.arange(put_blocks)[:, None]) & live_mask[None, :]).astype(
        jnp.float32
    )
    placed = jnp.einsum("ts,sav->tav", onehot, products, precision=HIGHEST_PRECISION)
    return placed.reshape(put_blocks * block_size, vec_width)


def body(start_block, block_values, block_rows, block_cols, block_count, center, radius):
    values = block_values[0]
    rows_local = block_rows[0]
    cols_local = block_cols[0]
    live_count = block_count[0, 0]
    tile_rows = ORDER // (BS * lax.axis_size("row"))
    tile_cols = ORDER // (BS * lax.axis_size("col"))
    shift = center[0]
    spread = radius[0]

    def transpose_half(vectors):
        gathered = lax.all_gather(vectors, "col", axis=0, tiled=True)
        return move_blocks(gathered, values, rows_local, cols_local, live_count, tile_cols, True)

    def column_share(partial_cols):
        return lax.psum_scatter(partial_cols, "row", scatter_dimension=0, tiled=True)

    def apply_scaled(vectors):
        partial_cols = transpose_half(vectors)
        whole_cols = lax.all_gather(column_share(partial_cols), "row", axis=0, tiled=True)
        partial_rows = move_blocks(
            whole_cols, values, cols_local, rows_local, live_count, tile_rows, False
        )
        system = lax.psum_scatter(partial_rows, "col", scatter_dimension=0, tiled=True)
        return (system - shift * vectors) / spread

    current = apply_scaled(start_block)
    following = 2.0 * apply_scaled(current) - start_block
    image_block = column_share(transpose_half(following))
    gram_local = jnp.dot(following.T, following, precision=HIGHEST_PRECISION)
    inner_local = jnp.dot(image_block.T, image_block, precision=HIGHEST_PRECISION)
    gram_matrix, inner_matrix = lax.psum((gram_local, inner_local), ("row", "col"))
    lower_factor = jnp.linalg.cholesky(gram_matrix)
    basis_block = jax.scipy.linalg.solve_triangular(lower_factor, following.T, lower=True).T
    left_solved = jax.scipy.linalg.solve_triangular(lower_factor, inner_matrix, lower=True)
    projected = jax.scipy.linalg.solve_triangular(lower_factor, left_solved.T, lower=True).T
    return (basis_block, projected)


def solution(mesh):
    in_specs = (
        P(("row", "col"), None),
        P("row", "col", None, None),
        P("row", "col"),
        P("row", "col"),
        P("row", "col"),
        P(),
        P(),
    )
    out_specs = (P(("row", "col"), None), P())
    return jax.shard_map(body, mesh=mesh, in_specs=in_specs, out_specs=out_specs, check_vma=False)
```

profile of v0, /device:TPU:0, one launch (start us, length us, event | category | flops | bytes accessed | tf_op | source)
XLA Modules:
  0.0 1134.1 jit_solution(13084960177903234737)
XLA Ops:
  9.3 128.5 %all-gather.6.cloned.1.call-done = f32[16384,128]{1,0:T(8,128)} async-done(((f32[2048,128]{1,0:T(8,128)}), f32[16384,128]{1,0:T(8,128)}) %all-gather.6.cloned.1.call-update) | async-done | bytes 8388624 | tf_op jit(solution)/shard_map/all_gather | solution.py:38
  137.8 4.0 gather_fusion
  145.5 3.2 copy.12
  148.8 42.8 %reduce-scatter.6.cloned.1.call-done = f32[2048,128]{1,0:T(8,128)} async-done(((f32[8192,128]{1,0:T(8,128)}), f32[2048,128]{1,0:T(8,128)}) %reduce-scatter.6.cloned.1.call-update) | async-done | bytes 1048592 | tf_op jit(solution)/shard_map/reduce_scatter | solution.py:42
  191.9 35.9 %all-gather.8.cloned.1.call-done = f32[8192,128]{1,0:T(8,128)} async-done(((f32[2048,128]{1,0:T(8,128)}), f32[8192,128]{1,0:T(8,128)}) %all-gather.8.cloned.1.call-update) | async-done | bytes 4194320 | tf_op jit(solution)/shard_map/all_gather | solution.py:46
  227.8 2.8 gather_fusion.1
  230.5 2.3 fusion.6
  233.1 3.8 fusion.16
  236.9 8.1 copy.13
  246.4 147.7 %reduce-scatter.8.cloned.1.call-done = f32[2048,128]{1,0:T(8,128)} async-done(((f32[16384,128]{1,0:T(8,128)}), f32[2048,128]{1,0:T(8,128)}) %reduce-scatter.8.cloned.1.call-update) | async-done | bytes 1048592 | tf_op jit(solution)/shard_map/reduce_scatter | solution.py:50
  397.0 123.7 %all-gather.10.cloned.1.call-done = f32[16384,128]{1,0:T(8,128)} async-done(((f32[2048,128]{1,0:T(8,128)}), f32[16384,128]{1,0:T(8,128)}) %all-gather.10.cloned.1.call-update) | async-done | bytes 8388624 | tf_op jit(solution)/shard_map/all_gather | solution.py:38
  520.7 4.8 gather_fusion.2
  525.4 3.2 fusion.4
  530.7 3.1 fusion.14
  533.8 3.2 copy.14
  537.1 42.8 %reduce-scatter.10.cloned.1.call-done = f32[2048,128]{1,0:T(8,128)} async-done(((f32[8192,128]{1,0:T(8,128)}), f32[2048,128]{1,0:T(8,128)}) %reduce-scatter.10.cloned.1.call-update) | async-done | bytes 1048592 | tf_op jit(solution)/shard_map/reduce_scatter | solution.py:42
  580.0 36.1 %all-gather.12.cloned.1.call-done = f32[8192,128]{1,0:T(8,128)} async-done(((f32[2048,128]{1,0:T(8,128)}), f32[8192,128]{1,0:T(8,128)}) %all-gather.12.cloned.1.call-update) | async-done | bytes 4194320 | tf_op jit(solution)/shard_map/all_gather | solution.py:46
  616.0 3.6 gather_fusion.3
  619.6 4.2 fusion.2
  625.8 4.8 fusion.12
  630.6 8.1 copy.15
  638.8 149.1 %reduce-scatter.12.cloned.1.call-done = f32[2048,128]{1,0:T(8,128)} async-done(((f32[16384,128]{1,0:T(8,128)}), f32[2048,128]{1,0:T(8,128)}) %reduce-scatter.12.cloned.1.call-update) | async-done | bytes 1048592 | tf_op jit(solution)/shard_map/reduce_scatter | solution.py:50
  787.9 2.8 multiply_subtract_fusion
  790.9 123.9 %all-gather.14.cloned.1.call-done = f32[16384,128]{1,0:T(8,128)} async-done(((f32[2048,128]{1,0:T(8,128)}), f32[16384,128]{1,0:T(8,128)}) %all-gather.14.cloned.1.call-update) | async-done | bytes 8388624 | tf_op jit(solution)/shard_map/all_gather | solution.py:38
  914.8 4.0 gather_fusion.4
  922.4 3.2 copy.18
  926.9 2.4 fusion.37
  929.3 39.2 %reduce-scatter.14.cloned.1.call-done = f32[2048,128]{1,0:T(8,128)} async-done(((f32[8192,128]{1,0:T(8,128)}), f32[2048,128]{1,0:T(8,128)}) %reduce-scatter.14.cloned.1.call-update) | async-done | bytes 1048592 | tf_op jit(solution)/shard_map/reduce_scatter | solution.py:42
  968.5 4.0 fusion.38
  972.5 126.1 %all-reduce.3.cloned.1.call-done = (f32[128,128]{0,1:T(8,128)}, f32[128,128]{1,0:T(8,128)}) async-done(((f32[128,128]{0,1:T(8,128)}, f32[128,128]{1,0:T(8,128)}), (f32[128,128]{0,1:T(8,128)}, f32[128,128]{1,0:T(8,128)})) %all-reduce.3.cloned.1.call-update) | async-done | bytes 131088 | tf_op jit(solution)/shard_map/psum | solution.py:58
  1100.4 11.7 %cholesky.16 = f32[128,128]{1,0:T(8,128)S(1)} custom-call(f32[128,128]{1,0:T(8,128)S(1)} %fusion.25), custom_call_target="Cholesky" | custom-call | tf_op jit(solution)/shard_map/jit(cholesky)/cholesky | solution.py:59
  1113.5 9.8 custom-call.10
  (56 shorter events, 25.1 us)
Async XLA Ops:
  7.2 134.6 %copy-start = (f32[1,2,512,512]{3,2,1,0:T(8,128)S(1)}, f32[1,2,512,512]{3,2,1,0:T(8,128)}, u32[]{:S(2)}) copy-start(f32[1,2,512,512]{3,2,1,0:T(8,128)} %param.10) | copy-start | bytes 6291460
  7.2 136.2 %copy-start.3 = (s32[1,2]{1,0:T(1,128)S(1)}, s32[1,2]{1,0:T(1,128)}, u32[]{:S(2)}) copy-start(s32[1,2]{1,0:T(1,128)} %param.12) | copy-start | bytes 28
  7.2 130.6 %all-gather.6.cloned.1.call-start = ((), (), s32[]{:S(2)}) async-start(), calls=%async_computation.5 | async-start | bytes 9437184 | tf_op jit(solution)/shard_map/all_gather | solution.py:38
  7.9 183.7 %reduce-scatter.6.cloned.1.call-start = ((), (), s32[]{:S(2)}) async-start(), calls=%async_computation.6 | async-start | bytes 5242880 | tf_op jit(solution)/shard_map/reduce_scatter | solution.py:42
  148.8 84.4 %copy-start.4 = (s32[1,2]{1,0:T(1,128)S(1)}, s32[1,2]{1,0:T(1,128)}, u32[]{:S(2)}) copy-start(s32[1,2]{1,0:T(1,128)} %param.11) | copy-start | bytes 28
  148.8 79.0 %all-gather.8.cloned.1.call-start = ((), (), s32[]{:S(2)}) async-start(), calls=%async_computation.7 | async-start | bytes 5242880 | tf_op jit(solution)/shard_map/all_gather | solution.py:46
  191.6 202.5 %reduce-scatter.8.cloned.1.call-start = ((), (), s32[]{:S(2)}) async-start(), calls=%async_computation.8 | async-start | bytes 9437184 | tf_op jit(solution)/shard_map/reduce_scatter | solution.py:50
  245.0 149.2 %copy-start.2 = (f32[2048,128]{1,0:T(8,128)S(1)}, f32[2048,128]{1,0:T(8,128)}, u32[]{:S(2)}) copy-start(f32[2048,128]{1,0:T(8,128)} %param.9) | copy-start | bytes 3145732
  245.0 275.7 %all-gather.10.cloned.1.call-start = ((), (), s32[]{:S(2)}) async-start(), calls=%async_computation.9 | async-start | bytes 9437184 | tf_op jit(solution)/shard_map/all_gather | solution.py:38
  396.5 183.4 %reduce-scatter.10.cloned.1.call-start = ((), (), s32[]{:S(2)}) async-start(), calls=%async_computation.10 | async-start | bytes 5242880 | tf_op jit(solution)/shard_map/reduce_scatter | solution.py:42
  537.0 79.0 %all-gather.12.cloned.1.call-start = ((), (), s32[]{:S(2)}) async-start(), calls=%async_computation.11 | async-start | bytes 5242880 | tf_op jit(solution)/shard_map/all_gather | solution.py:46
  579.9 207.9 %reduce-scatter.12.cloned.1.call-start = ((), (), s32[]{:S(2)}) async-start(), calls=%async_computation.12 | async-start | bytes 9437184 | tf_op jit(solution)/shard_map/reduce_scatter | solution.py:50
  638.7 276.1 %all-gather.14.cloned.1.call-start = ((), (), s32[]{:S(2)}) async-start(), calls=%async_computation.13 | async-start | bytes 9437184 | tf_op jit(solution)/shard_map/all_gather | solution.py:38
  790.7 177.9 %reduce-scatter.14.cloned.1.call-start = ((), (), s32[]{:S(2)}) async-start(), calls=%async_computation.14 | async-start | bytes 5242880 | tf_op jit(solution)/shard_map/reduce_scatter | solution.py:42
  925.7 1.2 copy-start.1
  925.7 172.9 %all-reduce.3.cloned.1.call-start = ((), (), s32[]{:S(2)}) async-start(), calls=%async_computation.15 | async-start | bytes 262144 | tf_op jit(solution)/shard_map/psum | solution.py:58
Sparse Core Ops, SparseCore 0:
  10.1 127.6 all-gather.5
  148.9 42.6 reduce-scatter.5
  193.2 34.4 all-gather.7
  245.1 148.9 reduce-scatter.7
  396.7 123.9 all-gather.9
  537.2 42.6 reduce-scatter.9
  581.5 34.4 all-gather.11
  638.8 148.9 reduce-scatter.11
  790.8 123.9 all-gather.13
  925.8 42.6 reduce-scatter.13
  975.8 122.8 all-reduce.2
where the time goes:
time: 1140 us; the launch traced here: 1130 us
  waiting for transfers between devices  997 us (87%)
  local copies, waits for them, and re-layouts  52.5 us (5%)
  matrix products  38 us (3%)
  other arithmetic  29.5 us (3%)
  between operations  16.3 us (1%)
    all_gather x3, waiting for transfers between devices, transpose_half(): gathered = lax.all_gather(vectors, 'col', axis=0, tiled=True)  376 us
    reduce_scatter x2, waiting for transfers between devices, apply_scaled(): lax.psum_scatter(partial_rows, 'col', scatter_dimension=0, tiled=True)  297 us
    psum x1, waiting for transfers between devices, body(): lax.psum((gram_local, inner_local), ('row', 'col'))  126 us
    reduce_scatter x3, waiting for transfers between devices, column_share(): lax.psum_scatter(partial_cols, 'row', scatter_dimension=0, tiled=True)  125 us
    all_gather x2, waiting for transfers between devices, apply_scaled(): lax.all_gather(column_share(partial_cols), 'row', axis=0, tiled=True)  71.9 us
    dot_general x5, local copies, waits for them, and re-layouts, move_blocks(): jnp.einsum('ts,sav->tav', onehot, products, precision=HIGHEST_PRECISION)  25.9 us
  transfers between devices with their start and end apart: 11, of which 11 were waited for; matrix products, arithmetic and copies ran while one was open for 0% of the time, Pallas kernels for 0%

commit v1 on v0

v1 whole, which is shorter than its diff:
```python
import functools

import jax
import jax.numpy as jnp
import numpy as np
from jax import lax
from jax.experimental import pallas as pl
from jax.experimental.pallas import tpu as pltpu
from jax.sharding import PartitionSpec as P

HIGHEST = lax.Precision.HIGHEST
PANEL = 8
VMEM = pl.BlockSpec(memory_space=pltpu.VMEM)
SMEM = pl.BlockSpec(memory_space=pltpu.SMEM)
ANY = pl.BlockSpec(memory_space=pl.ANY)


def call(kernel, out_shape, in_specs, out_specs, args, scratch=(), flops=0, name=None):
    moved = sum(a.size * a.dtype.itemsize for a in args)
    return pl.pallas_call(
        kernel,
        out_shape=out_shape,
        in_specs=in_specs,
        out_specs=out_specs,
        scratch_shapes=list(scratch),
        compiler_params=pltpu.CompilerParams(vmem_limit_bytes=40 * 1024 * 1024),
        cost_estimate=pl.CostEstimate(flops=flops, bytes_accessed=moved, transcendentals=0),
        name=name,
    )(*args)


def split(value):
    high = value.astype(jnp.bfloat16)
    return high, (value - high.astype(jnp.float32)).astype(jnp.bfloat16)


def dot3(left_high, left_low, right):
    right_high, right_low = split(right)
    dot = functools.partial(jnp.dot, preferred_element_type=jnp.float32)
    return dot(left_high, right_high) + (dot(left_high, right_low) + dot(left_low, right_high))


def self_product(value):
    high, low = split(value)

    def dot(left, right):
        return lax.dot_general(left, right, (((0,), (0,)), ((), ())), preferred_element_type=jnp.float32)

    mixed = dot(high, low)
    return dot(high, high) + (dot(low, low) + (mixed + mixed.T))


def prepare_kernel(values, high, low, high_t, low_t):
    for s in range(values.shape[0]):
        block = values[s]
        high[s], low[s] = split(block)
        high_t[s], low_t[s] = split(block.T)


def table_row(table, places, entry, slots, slot):
    place = places[entry]
    return jnp.where(place >= 0, table[jnp.maximum(place, 0) * slots + slot], -1)


def pick(row, held, first, piece, out, s, base):
    size = out.shape[1]
    count = held.shape[0] // piece
    for i in range(size // piece):
        rows = slice(i * piece, (i + 1) * piece)
        value = jnp.zeros((piece, out.shape[2]), out.dtype)
        for ref, slot in base:
            value = value + ref[slot, rows, :]
        local = row * (size // piece) + i - first
        valid = (row >= 0) & (local >= 0) & (local < count)
        at = pl.multiple_of(jnp.clip(local, 0, count - 1) * piece, piece)
        out[s, rows, :] = jnp.where(valid, held[pl.ds(at, piece), :], value)


def ring_kernel(entry, slots, offset, before_offset, piece, table, places, held, *refs):
    before, out = refs[:-1], refs[-1]
    for s in range(out.shape[0]):
        slot = s + offset
        base = [(ref, slot - before_offset) for ref in before if 0 <= slot - before_offset < ref.shape[0]]
        pick(table_row(table, places, entry, slots, slot), held, places[0], piece, out, s, base)


def first_kernel(entry, slots, offsets, piece, table, places, held, high_t, low_t, *refs):
    arrived, (x_out, p_out) = refs[:-2], refs[-2:]
    for s in range(slots):
        base = [(ref, s - off) for ref, off in zip(arrived, offsets) if 0 <= s - off < ref.shape[0]]
        pick(table_row(table, places, entry, slots, s), held, places[0], piece, x_out, s, base)
        p_out[s] = dot3(high_t[s], low_t[s], x_out[s])


def column_kernel(slots, last, columns, scalars, high, low, *refs):
    refs = list(refs)
    older = refs.pop(0) if last else None
    arrived, q_out, total = refs[:-2], refs[-2], refs[-1]
    center, radius = scalars[0], scalars[1]
    for s in range(slots):
        mine = columns[s]
        total[s] = arrived[0][s]
        for j, held in enumerate(arrived):
            for t in range(slots):
                if (j, t) != (0, s):

                    @pl.when((columns[j * slots + t] == mine) & (mine >= 0))
                    def _():
                        total[s] += held[t]

        q = dot3(high[s], low[s], total[s])
        if last:
            q = (2.0 / radius) * (q - (center / radius) * older[s])
        q_out[s] = q


def row_kernel(slots, entries, last, table, places, scalars, high_t, low_t, mine, vectors, *refs):
    count = len(entries)
    arrived = refs[:count]
    p_out, total, landing, sems = refs[count:]
    center, radius = scalars[0], scalars[1]

    def each(action):
        for b, (entry, offset) in enumerate(entries):
            for t in range(arrived[b].shape[0]):
                row = table_row(table, places, entry, slots, offset + t)
                hit = row < -1
                for s in range(slots):
                    hit = hit | ((row == table[s]) & (row >= 0))

                @pl.when(hit)
                def _():
                    action(b, t, row)

    def copy(b, t):
        return pltpu.make_async_copy(arrived[b].at[t], landing.at[b * slots + t], sems.at[b * slots + t])

    each(lambda b, t, row: copy(b, t).start())
    for s in range(slots):
        total[s] = mine[s]
        for t in range(slots):
            if t != s:

                @pl.when((table[t] == table[s]) & (table[s] >= 0))
                def _():
                    total[s] += mine[t]

    def add(b, t, row):
        copy(b, t).wait()
        for s in range(slots):

            @pl.when(row == table[s])
            def _():
                total[s] += landing[b * slots + t]

    each(add)
    for s in range(slots):
        if last:
            y = total[s] + (2.0 * (center / radius) * (center / radius) - 1.0) * vectors[s]
        else:
            y = (total[s] - center * vectors[s]) / radius
        p_out[s] = dot3(high_t[s], low_t[s], y)


def owner_kernel(slots, entries, piece, table, places, scalars, start, *refs):
    count = len(entries)
    arrived = refs[:count]
    y_out, gram_out, landing, sems = refs[count:]
    center, radius = scalars[0], scalars[1]
    subs = landing.shape[1] // piece
    held = y_out.shape[0] // piece
    first = places[0]

    def each(action):
        for b, (entry, offset) in enumerate(entries):
            for t in range(arrived[b].shape[0]):
                row = table_row(table, places, entry, slots, offset + t)
                begin = row * subs - first

                @pl.when((row >= 0) & (begin + subs > 0) & (begin < held))
                def _():
                    action(b, t, begin)

    def copy(b, t):
        return pltpu.make_async_copy(arrived[b].at[t], landing.at[b * slots + t], sems.at[b * slots + t])

    each(lambda b, t, begin: copy(b, t).start())
    y_out[...] = (2.0 * (center / radius) * (center / radius) - 1.0) * start[...]

    def add(b, t, begin):
        copy(b, t).wait()
        for i in range(subs):
            local = begin + i

            @pl.when((local >= 0) & (local < held))
            def _():
                at = pl.multiple_of(jnp.clip(local, 0, held - 1) * piece, piece)
                y_out[pl.ds(at, piece), :] += landing[b * slots + t, i * piece : (i + 1) * piece, :]

    each(add)
    gram_out[...] = self_product(y_out[...])


def inner_kernel(slots, columns, place, *refs):
    arrived, out, order, total = refs[:-3], refs[-3], refs[-2], refs[-1]
    count = len(arrived)
    size = order.shape[1]
    for j, held in enumerate(arrived):
        at = lax.bitwise_xor(place[0], j)
        for t in range(slots):
            order[at * slots + t] = held[t]

    def column(i):
        return columns[lax.bitwise_xor(place[0], i // slots) * slots + i % slots]

    ids = [column(i) for i in range(count * slots)]
    for i in range(count * slots):
        earlier = ids[i] < 0
        for k in range(i):
            earlier = earlier | (ids[k] == ids[i])
        total[i * size : (i + 1) * size, :] = jnp.where(earlier, 0.0, order[i])
        for k in range(i + 1, count * slots):

            @pl.when((ids[k] == ids[i]) & jnp.logical_not(earlier))
            def _():
                total[i * size : (i + 1) * size, :] += order[k]

    out[...] = self_product(total[...])


def factor_kernel(gram, following, basis_out, inverse_out):
    order = gram.shape[0]
    blocks = order // PANEL
    shape = (PANEL, order)
    below = lax.broadcasted_iota(jnp.int32, shape, 0)
    lane = lax.broadcasted_iota(jnp.int32, shape, 1)
    left = [gram[b * PANEL : (b + 1) * PANEL, :] for b in range(blocks)]
    right = [jnp.where(lane == below + b * PANEL, 1.0, 0.0) for b in range(blocks)]

    def spread(block, k):
        return jnp.broadcast_to(block[k : k + 1, :], shape)

    for b in range(blocks):
        rest = range(b, blocks)
        panel = [
            {i: jnp.broadcast_to(left[i][:, b * PANEL + j : b * PANEL + j + 1], shape) for i in rest}
            for j in range(PANEL)
        ]
        scale = jnp.ones(shape, jnp.float32)
        for k in range(PANEL):
            pivot = spread(panel[k][b], k)
            inverse = 1.0 / pivot
            scale = jnp.where(below == k, lax.rsqrt(pivot), scale)
            factor = {i: panel[k][i] * inverse for i in rest}
            factor[b] = jnp.where(below > k, factor[b], 0.0)
            left_row, right_row = spread(left[b], k), spread(right[b], k)
            for j in range(k + 1, PANEL):
                row = spread(panel[j][b], k)
                for i in rest:
                    panel[j][i] = panel[j][i] - factor[i] * row
            for i in rest:
                left[i] = left[i] - factor[i] * left_row
                right[i] = right[i] - factor[i] * right_row
        inverse_out[b * PANEL : (b + 1) * PANEL, :] = right[b] * scale
    basis_out[...] = lax.dot_general(
        following[...], inverse_out[...], (((1,), (1,)), ((), ())), precision=HIGHEST, preferred_element_type=jnp.float32
    )


def project_kernel(inverse, inner, out):
    half = jnp.dot(inverse[...], inner[...], precision=HIGHEST, preferred_element_type=jnp.float32)
    out[...] = lax.dot_general(
        half, inverse[...], (((1,), (1,)), ((), ())), precision=HIGHEST, preferred_element_type=jnp.float32
    )


def solution(mesh):
    n_row, n_col = mesh.shape["row"], mesh.shape["col"]
    tie = lax.optimization_barrier
    far = n_col // 2

    ring = list(range(0, n_col, 2)) + list(range(1, n_col, 2))[::-1]
    position = {col: k for k, col in enumerate(ring)}

    place_lines = np.array(
        [[0] + [col ^ ring[(position[col] + d) % n_col] for d in range(-far, far + 1)] for col in range(n_col)], np.int32
    )

    def at(distance):
        return far + 1 + distance

    def forward(value, step):
        return lax.ppermute(value, "col", [(col, ring[(k + step) % n_col]) for k, col in enumerate(ring)])

    def shares(distance, slots):
        if 2 * distance < n_col:
            return (0, slots), (0, slots)
        if slots % 2:
            return (0, slots), (0, 0)
        return (0, slots // 2), (slots // 2, slots)

    def flip(value, axis, bit):
        size = n_row if axis == "row" else n_col
        return lax.ppermute(value, axis, [(i, i ^ bit) for i in range(size)])

    def table_over(own, axis):
        for bit in powers(n_row if axis == "row" else n_col):
            own = jnp.concatenate([own, flip(own, axis, bit)])
        return own

    def gather_row(own):
        held = {0: own}
        bit = n_row // 2
        while bit:
            held.update({j ^ bit: flip(v, "row", bit) for j, v in list(held.items())})
            bit //= 2
        return [held[j] for j in range(n_row)]

    def sum_over(value, axis, bits):
        for bit in bits:
            value = value + flip(value, axis, bit)
        return value

    def powers(size):
        return [1 << k for k in range(size.bit_length() - 1)]

    def gather_col(own):
        slots = own.shape[0]
        held = {1: (own, 0), -1: (own, 0)}
        got = []
        for distance in range(1, far + 1):
            for step, (first, end) in zip((1, -1), shares(distance, slots)):
                if first == end:
                    continue
                chunk, _ = held[step]
                if (first, end) != (0, slots):
                    chunk = chunk[first:end]
                held[step] = (forward(chunk, step), first)
                got.append(((at(-step * distance), first), held[step][0]))
        return [g[0] for g in got], [g[1] for g in got]

    def body(start_block, block_values, block_rows, block_cols, block_count, center, radius):
        values = block_values[0]
        slots, size, _ = values.shape
        held_rows, vec = start_block.shape
        piece = min(size, held_rows)
        live = jnp.arange(slots) < block_count[0, 0]
        rows = jnp.where(live, block_rows[0], -1)
        cols = jnp.where(live, block_cols[0], -1)
        col = lax.axis_index("col")
        with jax.named_scope("tables"):
            table = table_over(rows, "col")
            columns = table_over(cols, "row")
        places = jnp.asarray(place_lines)[col]
        held_pieces = held_rows // piece
        places = places.at[0].set(col * held_pieces)
        scalars = jnp.concatenate([center, radius])

        chunk = jax.ShapeDtypeStruct((slots, size, vec), jnp.float32)
        square = jax.ShapeDtypeStruct((vec, vec), jnp.float32)
        half_block = jax.ShapeDtypeStruct(values.shape, jnp.bfloat16)
        high, low, high_t, low_t = call(
            prepare_kernel, [half_block] * 4, [VMEM], [VMEM] * 4, [values], name="split_blocks"
        )
        flops = 6 * slots * size * size * vec

        before = {1: [], -1: []}
        for distance in range(far, 0, -1):
            for step, (first, end) in zip((1, -1), shares(distance, slots)):
                if first == end:
                    continue
                value = call(
                    functools.partial(
                        ring_kernel, at(step * distance), slots, first, sum(b[1] for b in before[step]), piece
                    ),
                    jax.ShapeDtypeStruct((end - first, size, vec), jnp.float32),
                    [SMEM, SMEM] + [VMEM] * (1 + len(before[step])),
                    VMEM,
                    [table, places, start_block] + [b[0] for b in before[step]],
                    name="pick_rows",
                )
                before[step] = [(forward(value, step), first)]
            if distance == 2:
                (first_value, offset) = before[1][0]
                first_value, columns, high, low, high_t, low_t = tie((first_value, columns, high, low, high_t, low_t))
                before[1] = [(first_value, offset)]
        arrived = before[1] + before[-1]
        x, p = call(
            functools.partial(first_kernel, at(0), slots, [b[1] for b in arrived], piece),
            [chunk] * 2,
            [SMEM, SMEM] + [VMEM] * (3 + len(arrived)),
            [VMEM] * 2,
            [table, places, start_block, high_t, low_t] + [b[0] for b in arrived],
            flops=flops,
            name="first_product",
        )

        def column_step(parts, older=None):
            more = [] if older is None else [older]
            return call(
                functools.partial(column_kernel, slots, older is not None),
                chunk,
                [SMEM, SMEM] + [VMEM] * (2 + len(more) + n_row),
                VMEM,
                [columns, scalars, high, low] + more + parts,
                scratch=[pltpu.VMEM(chunk.shape, jnp.float32)],
                flops=flops,
                name="column_product",
            )

        def row_step(last, mine, entries, got, vectors):
            count = len(got)
            return call(
                functools.partial(row_kernel, slots, entries, last),
                chunk,
                [SMEM] * 3 + [VMEM] * 4 + [ANY] * count,
                VMEM,
                [table, places, scalars, high_t, low_t, mine, vectors] + got,
                scratch=[
                    pltpu.VMEM(chunk.shape, jnp.float32),
                    pltpu.VMEM((count * slots, size, vec), jnp.float32),
                    pltpu.SemaphoreType.DMA((count * slots,)),
                ],
                flops=flops,
                name="row_product",
            )

        q = column_step(gather_row(p))
        p = row_step(False, q, *gather_col(q), x)
        g = column_step(gather_row(p), q)
        entries, got = gather_col(g)
        count = len(got)

        following, gram_local = call(
            functools.partial(owner_kernel, slots, [(at(0), 0)] + entries, piece),
            [jax.ShapeDtypeStruct(start_block.shape, jnp.float32), square],
            [SMEM] * 3 + [VMEM] + [ANY] * (count + 1),
            [VMEM] * 2,
            [table, places, scalars, start_block, g] + got,
            scratch=[
                pltpu.VMEM(((count + 1) * slots, size, vec), jnp.float32),
                pltpu.SemaphoreType.DMA(((count + 1) * slots,)),
            ],
            flops=6 * held_rows * vec * vec,
            name="owner_rows",
        )
        gram_matrix, g = tie((gram_local, g))
        p = row_step(True, g, entries, got, x)
        gram_matrix = sum_over(gram_matrix, "row", powers(n_row)[:1])
        gram_matrix = sum_over(gram_matrix, "col", powers(n_col))
        gram_matrix = sum_over(gram_matrix, "row", powers(n_row)[1:])
        inner_local = call(
            functools.partial(inner_kernel, slots),
            square,
            [SMEM, SMEM] + [VMEM] * n_row,
            VMEM,
            [columns, lax.axis_index("row").reshape(1)] + gather_row(p),
            scratch=[
                pltpu.VMEM((n_row * slots, size, vec), jnp.float32),
                pltpu.VMEM((n_row * slots * size, vec), jnp.float32),
            ],
            flops=6 * n_row * slots * size * vec * vec,
            name="inner_product",
        )
        inner_matrix = sum_over(inner_local, "col", powers(n_col))
        basis_block, inverse = call(
            factor_kernel,
            [jax.ShapeDtypeStruct(start_block.shape, jnp.float32), square],
            [VMEM] * 2,
            [VMEM] * 2,
            [gram_matrix, following],
            flops=12 * held_rows * vec * vec,
            name="factor_and_basis",
        )
        projected = call(project_kernel, square, [VMEM] * 2, VMEM, [inverse, inner_matrix], name="project")
        return (basis_block, projected)

    in_specs = (
        P(("row", "col"), None),
        P("row", "col", None, None),
        P("row", "col"),
        P("row", "col"),
        P("row", "col"),
        P(),
        P(),
    )
    out_specs = (P(("row", "col"), None), P())
    return jax.shard_map(body, mesh=mesh, in_specs=in_specs, out_specs=out_specs, check_vma=False)
```

time: 1140 us -> 232 us (0.20)
  waiting for transfers between devices: 997 us -> 150 us
  local copies, waits for them, and re-layouts: 52.5 us -> 2.02 us
  starting transfers between devices: 1.3 us -> 48.2 us
  matrix products: 38 us -> 0 us
  other arithmetic: 29.5 us -> 1.19 us
  Pallas kernels: 0 us -> 28.1 us
  between operations: 16.3 us -> 2.83 us
    all_gather x5 -> x0, waiting for transfers between devices: 448 us -> none  [the longest x3 376 us: transpose_half(): gathered = lax.all_gather(vectors, 'col', axis=0, tiled=True)]
    reduce_scatter x5 -> x0, waiting for transfers between devices: 422 us -> none  [the longest x2 297 us: apply_scaled(): lax.psum_scatter(partial_rows, 'col', scatter_dimension=0, tiled=True)]
    ppermute x0 -> x46, waiting for transfers between devices: none -> 150 us  [the longest x24 105 us: forward(): lax.ppermute(value, 'col', [(col, ring[(k + step) % n_col]) for k, col in...]
    psum x1 -> x0, waiting for transfers between devices: 126 us -> none  [body(): lax.psum((gram_local, inner_local), ('row', 'col'))]
    ppermute x0 -> x46, starting transfers between devices: none -> 48.2 us  [the longest x24 25.5 us: forward(): lax.ppermute(value, 'col', [(col, ring[(k + step) % n_col]) for k, col in...]
    dot_general x12 -> x0, matrix products: 34.6 us -> none  [the longest x5 15.7 us: move_blocks(): jnp.einsum('ts,sav->tav', onehot, products, precision=HIGHEST_PRECISION)]
    dot_general x10 -> x0, local copies, waits for them, and re-layouts: 30.7 us -> none  [the longest x5 25.9 us: move_blocks(): jnp.einsum('ts,sav->tav', onehot, products, precision=HIGHEST_PRECISION)]
    pallas_call x0 -> x18, Pallas kernels: none -> 28.1 us  [call(): pl.pallas_call(kernel, out_shape=out_shape, in_specs=in_specs, out_specs=...]
  transfers between devices with their start and end apart: 11 -> 46, of which waited for: 11 -> 32; matrix products, arithmetic and copies ran while one was open for 0% -> 0% of each run, Pallas kernels for 0% -> 6%
where the time goes in v1:
time: 232 us
  waiting for transfers between devices  150 us (65%)
  starting transfers between devices  48.2 us (21%)
  Pallas kernels  28.1 us (12%)
  between operations  2.83 us (1%)
    ppermute x24, waiting for transfers between devices, forward(): lax.ppermute(value, 'col', [(col, ring[(k + step) % n_col]) for k, col in...  105 us
    ppermute x22, waiting for transfers between devices, flip(): return lax.ppermute(value, axis, [(i, i ^ bit) for i in range(size)])  44.8 us
    pallas_call x18, Pallas kernels, call(): pl.pallas_call(kernel, out_shape=out_shape, in_specs=in_specs, out_specs=...  28.1 us
    ppermute x24, starting transfers between devices, forward(): lax.ppermute(value, 'col', [(col, ring[(k + step) % n_col]) for k, col in...  25.5 us
    ppermute x22, starting transfers between devices, flip(): return lax.ppermute(value, axis, [(i, i ^ bit) for i in range(size)])  22.7 us
  transfers between devices with their start and end apart: 46, of which 32 were waited for; matrix products, arithmetic and copies ran while one was open for 0% of the time, Pallas kernels for 6%

profile of v1, /device:TPU:0, one launch (start us, length us, event | category | flops | bytes accessed | tf_op | source)
XLA Modules:
  0.0 231.9 jit_solution(4036431660060314500)
XLA Ops:
  1.9 3.0 %collective-permute-start = (s32[2]{0:T(128)S(1)}, s32[2]{0:T(128)S(1)}, u32[]{:S(2)}, u32[]{:S(2)}) collective-permute-start(s32[2]{0:T(128)S(1)} %compare_select_fusion.1), channel_id=1, source_target_pairs={{0,1},{1,0},{2,3},{3,2},{4,5},{5,4},{6,7},{7,6},{8,9},{9,8},{10,11... | collective-permute-start | bytes 32 | tf_op jit(solution)/shard_map/tables/ppermute | solution.py:304
  6.5 2.1 collective-permute-start.1
  10.2 3.0 %collective-permute-start.2 = (s32[8]{0:T(128)S(1)}, s32[8]{0:T(128)S(1)}, u32[]{:S(2)}, u32[]{:S(2)}) collective-permute-start(s32[8]{0:T(128)S(1)} %pad_add_fusion.1), channel_id=1, source_target_pairs={{0,4},{1,5},{2,6},{3,7},{4,0},{5,1},{6,2},{7,3},{8,12},{9,13},{10,... | collective-permute-start | bytes 104 | tf_op jit(solution)/shard_map/tables/ppermute | solution.py:304
  19.4 4.8 %collective-permute-done.9.refs_0_ = f32[1,512,128]{2,1,0:T(8,128)S(1)} collective-permute-done((f32[1,512,128]{2,1,0:T(8,128)S(1)}, f32[1,512,128]{2,1,0:T(8,128)S(1)}, u32[]{:S(2)}, u32[]{:S(2)}) %collective-permute-start.9) | collective-permute-done | bytes 262176 | tf_op jit(solution)/shard_map/ppermute | solution.py:293
  24.8 2.2 collective-permute-start.10
  27.8 8.8 %collective-permute-done.10.refs_0_ = f32[2,512,128]{2,1,0:T(8,128)S(1)} collective-permute-done((f32[2,512,128]{2,1,0:T(8,128)S(1)}, f32[2,512,128]{2,1,0:T(8,128)S(1)}, u32[]{:S(2)}, u32[]{:S(2)}) %collective-permute-start.10) | collective-permute-done | bytes 524320 | tf_op jit(solution)/shard_map/ppermute | solution.py:293
  37.2 2.2 collective-permute-start.11
  41.4 2.0 collective-permute-start.7
  47.3 2.0 collective-permute-start.12
  50.0 9.4 %collective-permute-done.12.refs_1_ = f32[2,512,128]{2,1,0:T(8,128)S(1)} collective-permute-done((f32[2,512,128]{2,1,0:T(8,128)S(1)}, f32[2,512,128]{2,1,0:T(8,128)S(1)}, u32[]{:S(2)}, u32[]{:S(2)}) %collective-permute-start.12) | collective-permute-done | bytes 524320 | tf_op jit(solution)/shard_map/ppermute | solution.py:293
  64.3 8.8 %collective-permute-done.14.refs_2_ = f32[2,512,128]{2,1,0:T(8,128)S(1)} collective-permute-done((f32[2,512,128]{2,1,0:T(8,128)S(1)}, f32[2,512,128]{2,1,0:T(8,128)S(1)}, u32[]{:S(2)}, u32[]{:S(2)}) %collective-permute-start.14) | collective-permute-done | bytes 524320 | tf_op jit(solution)/shard_map/ppermute | solution.py:304
  75.1 2.6 %column_product.2.mine.refs_0_ = f32[2,512,128]{2,1,0:T(8,128)S(1)} custom-call(s32[8]{0:T(128)S(1)} %pad_add_fusion.4.columns, f32[2]{0:T(128)S(1)} %pad_maximum_fusion.scalars, bf16[2,512,512]{2,1,0:T(8,128)(2,1)S(1)} %get-tuple-element.37.high, bf16[2,512,512]{2,1,0:T(8,128)(2,1)S(1)} %get-tuple-element.38.low, ...), custom_call_target="tpu_custom_call" | custom-call | flops 402653184 | bytes 4194344 | tf_op jit(solution)/shard_map/column_product/pallas_call | solution.py:20
  79.7 11.9 %collective-permute-done.17.refs_1_ = f32[2,512,128]{2,1,0:T(8,128)S(1)} collective-permute-done((f32[2,512,128]{2,1,0:T(8,128)S(1)}, f32[2,512,128]{2,1,0:T(8,128)S(1)}, u32[]{:S(2)}, u32[]{:S(2)}) %collective-permute-start.17) | collective-permute-done | bytes 524320 | tf_op jit(solution)/shard_map/ppermute | solution.py:293
  93.7 11.1 %collective-permute-done.19.refs_3_ = f32[2,512,128]{2,1,0:T(8,128)S(1)} collective-permute-done((f32[2,512,128]{2,1,0:T(8,128)S(1)}, f32[2,512,128]{2,1,0:T(8,128)S(1)}, u32[]{:S(2)}, u32[]{:S(2)}) %collective-permute-start.19) | collective-permute-done | bytes 524320 | tf_op jit(solution)/shard_map/ppermute | solution.py:293
  106.8 10.2 %collective-permute-done.21.refs_5_ = f32[2,512,128]{2,1,0:T(8,128)S(1)} collective-permute-done((f32[2,512,128]{2,1,0:T(8,128)S(1)}, f32[2,512,128]{2,1,0:T(8,128)S(1)}, u32[]{:S(2)}, u32[]{:S(2)}) %collective-permute-start.21) | collective-permute-done | bytes 524320 | tf_op jit(solution)/shard_map/ppermute | solution.py:293
  119.2 4.3 %collective-permute-done.23.refs_7_ = f32[1,512,128]{2,1,0:T(8,128)S(1)} collective-permute-done((f32[1,512,128]{2,1,0:T(8,128)S(1)}, f32[1,512,128]{2,1,0:T(8,128)S(1)}, u32[]{:S(2)}, u32[]{:S(2)}) %collective-permute-start.23) | collective-permute-done | bytes 262176 | tf_op jit(solution)/shard_map/ppermute | solution.py:293
  125.1 2.3 row_product.2.refs_1_
  128.9 8.7 %collective-permute-done.25.refs_3_ = f32[2,512,128]{2,1,0:T(8,128)S(1)} collective-permute-done((f32[2,512,128]{2,1,0:T(8,128)S(1)}, f32[2,512,128]{2,1,0:T(8,128)S(1)}, u32[]{:S(2)}, u32[]{:S(2)}) %collective-permute-start.25) | collective-permute-done | bytes 524320 | tf_op jit(solution)/shard_map/ppermute | solution.py:304
  137.6 1.9 collective-permute-done.26.refs_4_
  139.5 2.6 %column_product.3.refs_0_.mine = f32[2,512,128]{2,1,0:T(8,128)S(1)} custom-call(s32[8]{0:T(128)S(1)} %pad_add_fusion.4.columns, f32[2]{0:T(128)S(1)} %pad_maximum_fusion.scalars, bf16[2,512,512]{2,1,0:T(8,128)(2,1)S(1)} %get-tuple-element.37.high, bf16[2,512,512]{2,1,0:T(8,128)(2,1)S(1)} %get-tuple-element.38.low, ...), custom_call_target="tpu_custom_call" | custom-call | flops 402653184 | bytes 4718632 | tf_op jit(solution)/shard_map/column_product/pallas_call | solution.py:20
  144.2 11.9 %collective-permute-done.28.refs_2_.refs_1_ = f32[2,512,128]{2,1,0:T(8,128)S(1)} collective-permute-done((f32[2,512,128]{2,1,0:T(8,128)S(1)}, f32[2,512,128]{2,1,0:T(8,128)S(1)}, u32[]{:S(2)}, u32[]{:S(2)}) %collective-permute-start.28) | collective-permute-done | bytes 524320 | tf_op jit(solution)/shard_map/ppermute | solution.py:293
  158.2 11.1 %collective-permute-done.30.refs_4_.refs_3_ = f32[2,512,128]{2,1,0:T(8,128)S(1)} collective-permute-done((f32[2,512,128]{2,1,0:T(8,128)S(1)}, f32[2,512,128]{2,1,0:T(8,128)S(1)}, u32[]{:S(2)}, u32[]{:S(2)}) %collective-permute-start.30) | collective-permute-done | bytes 524320 | tf_op jit(solution)/shard_map/ppermute | solution.py:293
  171.3 10.2 %collective-permute-done.32.refs_6_.refs_5_ = f32[2,512,128]{2,1,0:T(8,128)S(1)} collective-permute-done((f32[2,512,128]{2,1,0:T(8,128)S(1)}, f32[2,512,128]{2,1,0:T(8,128)S(1)}, u32[]{:S(2)}, u32[]{:S(2)}) %collective-permute-start.32) | collective-permute-done | bytes 524320 | tf_op jit(solution)/shard_map/ppermute | solution.py:293
  183.7 4.3 %collective-permute-done.34.refs_8_.refs_7_ = f32[1,512,128]{2,1,0:T(8,128)S(1)} collective-permute-done((f32[1,512,128]{2,1,0:T(8,128)S(1)}, f32[1,512,128]{2,1,0:T(8,128)S(1)}, u32[]{:S(2)}, u32[]{:S(2)}) %collective-permute-start.34) | collective-permute-done | bytes 262176 | tf_op jit(solution)/shard_map/ppermute | solution.py:293
  189.6 2.1 owner_rows.1
  191.8 2.3 %row_product.3.refs_0_ = f32[2,512,128]{2,1,0:T(8,128)S(1)} custom-call(s32[16]{0:T(128)S(1)} %pad_add_fusion.2.table, s32[10]{0:T(128)S(1)} %constant_dynamic-update-slice_fusion.places, f32[2]{0:T(128)S(1)} %pad_maximum_fusion.scalars, bf16[2,512,512]{2,1,0:T(8,128)(2,1)S(1)} %get-tuple-element.39.high_t, ...), custom_call_target="tpu_custom_call" | custom-call | flops 402653184 | bytes 6815856 | tf_op jit(solution)/shard_map/row_product/pallas_call | solution.py:20
  195.8 8.6 %collective-permute-done.41.refs_2_ = f32[2,512,128]{2,1,0:T(8,128)S(1)} collective-permute-done((f32[2,512,128]{2,1,0:T(8,128)S(1)}, f32[2,512,128]{2,1,0:T(8,128)S(1)}, u32[]{:S(2)}, u32[]{:S(2)}) %collective-permute-start.41) | collective-permute-done | bytes 524320 | tf_op jit(solution)/shard_map/ppermute | solution.py:304
  208.0 2.7 %collective-permute-done.36 = f32[128,128]{1,0:T(8,128)S(1)} collective-permute-done((f32[128,128]{1,0:T(8,128)S(1)}, f32[128,128]{1,0:T(8,128)S(1)}, u32[]{:S(2)}, u32[]{:S(2)}) %collective-permute-start.36) | collective-permute-done | bytes 65568 | tf_op jit(solution)/shard_map/ppermute | solution.py:304
  211.2 2.0 inner_product.1
  215.2 2.3 %collective-permute-done.43 = f32[128,128]{1,0:T(8,128)S(1)} collective-permute-done((f32[128,128]{1,0:T(8,128)S(1)}, f32[128,128]{1,0:T(8,128)S(1)}, u32[]{:S(2)}, u32[]{:S(2)}) %collective-permute-start.43) | collective-permute-done | bytes 65568 | tf_op jit(solution)/shard_map/ppermute | solution.py:304
  222.6 2.1 collective-permute-done.39
  224.7 6.0 %factor_and_basis.1 = (f32[2048,128]{1,0:T(8,128)}, f32[128,128]{1,0:T(8,128)S(1)}) custom-call(f32[128,128]{1,0:T(8,128)S(1)} %add.36.gram, f32[2048,128]{1,0:T(8,128)S(1)} %get-tuple-element.46.following), custom_call_target="tpu_custom_call" | custom-call | flops 402653184 | bytes 1114112 | tf_op jit(solution)/shard_map/factor_and_basis/pallas_call | solution.py:20
  (108 shorter events, 59.4 us)
Async XLA Ops:
  16.6 7.6 %collective-permute-start.9 = (f32[1,512,128]{2,1,0:T(8,128)S(1)}, f32[1,512,128]{2,1,0:T(8,128)S(1)}, u32[]{:S(2)}, u32[]{:S(2)}) collective-permute-start(f32[1,512,128]{2,1,0:T(8,128)S(1)} %pick_rows.12), channel_id=1, source_target_pairs={{0,1},{2,0},{4,2},{6,4},{7,6},{5,7},{3,5},{1,3},{8,9},{10,8},{12,1... | collective-permute-start | bytes 786440 | tf_op jit(solution)/shard_map/ppermute | solution.py:293
  19.1 7.9 %collective-permute-start.3 = (f32[1,512,128]{2,1,0:T(8,128)S(1)}, f32[1,512,128]{2,1,0:T(8,128)S(1)}, u32[]{:S(2)}, u32[]{:S(2)}) collective-permute-start(f32[1,512,128]{2,1,0:T(8,128)S(1)} %pick_rows.8), channel_id=1, source_target_pairs={{0,2},{2,4},{4,6},{6,7},{7,5},{5,3},{3,1},{1,0},{8,10},{10,12},{12... | collective-permute-start | bytes 786440 | tf_op jit(solution)/shard_map/ppermute | solution.py:293
  24.8 11.8 %collective-permute-start.10 = (f32[2,512,128]{2,1,0:T(8,128)S(1)}, f32[2,512,128]{2,1,0:T(8,128)S(1)}, u32[]{:S(2)}, u32[]{:S(2)}) collective-permute-start(f32[2,512,128]{2,1,0:T(8,128)S(1)} %pick_rows.13), channel_id=1, source_target_pairs={{0,1},{2,0},{4,2},{6,4},{7,6},{5,7},{3,5},{1,3},{8,9},{10,8},{12,1... | collective-permute-start | bytes 1572872 | tf_op jit(solution)/shard_map/ppermute | solution.py:293
  27.7 11.7 %collective-permute-start.4 = (f32[2,512,128]{2,1,0:T(8,128)S(1)}, f32[2,512,128]{2,1,0:T(8,128)S(1)}, u32[]{:S(2)}, u32[]{:S(2)}) collective-permute-start(f32[2,512,128]{2,1,0:T(8,128)S(1)} %pick_rows.9), channel_id=1, source_target_pairs={{0,2},{2,4},{4,6},{6,7},{7,5},{5,3},{3,1},{1,0},{8,10},{10,12},{12... | collective-permute-start | bytes 1572872 | tf_op jit(solution)/shard_map/ppermute | solution.py:293
  37.2 9.4 %collective-permute-start.11 = (f32[2,512,128]{2,1,0:T(8,128)S(1)}, f32[2,512,128]{2,1,0:T(8,128)S(1)}, u32[]{:S(2)}, u32[]{:S(2)}) collective-permute-start(f32[2,512,128]{2,1,0:T(8,128)S(1)} %pick_rows.14), channel_id=1, source_target_pairs={{0,1},{2,0},{4,2},{6,4},{7,6},{5,7},{3,5},{1,3},{8,9},{10,8},{12,1... | collective-permute-start | bytes 1572872 | tf_op jit(solution)/shard_map/ppermute | solution.py:293
  40.0 9.2 %collective-permute-start.5 = (f32[2,512,128]{2,1,0:T(8,128)S(1)}, f32[2,512,128]{2,1,0:T(8,128)S(1)}, u32[]{:S(2)}, u32[]{:S(2)}) collective-permute-start(f32[2,512,128]{2,1,0:T(8,128)S(1)} %pick_rows.10), channel_id=1, source_target_pairs={{0,2},{2,4},{4,6},{6,7},{7,5},{5,3},{3,1},{1,0},{8,10},{10,12},{12... | collective-permute-start | bytes 1572872 | tf_op jit(solution)/shard_map/ppermute | solution.py:293
  47.3 12.1 %collective-permute-start.12 = (f32[2,512,128]{2,1,0:T(8,128)S(1)}, f32[2,512,128]{2,1,0:T(8,128)S(1)}, u32[]{:S(2)}, u32[]{:S(2)}) collective-permute-start(f32[2,512,128]{2,1,0:T(8,128)S(1)} %pick_rows.15), channel_id=1, source_target_pairs={{0,1},{2,0},{4,2},{6,4},{7,6},{5,7},{3,5},{1,3},{8,9},{10,8},{12,1... | collective-permute-start | bytes 1572872 | tf_op jit(solution)/shard_map/ppermute | solution.py:293
  49.9 11.3 %collective-permute-start.8 = (f32[2,512,128]{2,1,0:T(8,128)S(1)}, f32[2,512,128]{2,1,0:T(8,128)S(1)}, u32[]{:S(2)}, u32[]{:S(2)}) collective-permute-start(f32[2,512,128]{2,1,0:T(8,128)S(1)} %pick_rows.11), channel_id=1, source_target_pairs={{0,2},{2,4},{4,6},{6,7},{7,5},{5,3},{3,1},{1,0},{8,10},{10,12},{12... | collective-permute-start | bytes 1572872 | tf_op jit(solution)/shard_map/ppermute | solution.py:293
  62.8 10.4 %collective-permute-start.14 = (f32[2,512,128]{2,1,0:T(8,128)S(1)}, f32[2,512,128]{2,1,0:T(8,128)S(1)}, u32[]{:S(2)}, u32[]{:S(2)}) collective-permute-start(f32[2,512,128]{2,1,0:T(8,128)S(1)} %get-tuple-element.42.refs_0_), channel_id=1, source_target_pairs={{0,16},{8,24},{16,0},{24,8},{1,17},{9,25},{17,1},{25,9},{2,18},{10... | collective-permute-start | bytes 1572872 | tf_op jit(solution)/shard_map/ppermute | solution.py:304
  64.3 10.2 %collective-permute-start.13 = (f32[2,512,128]{2,1,0:T(8,128)S(1)}, f32[2,512,128]{2,1,0:T(8,128)S(1)}, u32[]{:S(2)}, u32[]{:S(2)}) collective-permute-start(f32[2,512,128]{2,1,0:T(8,128)S(1)} %get-tuple-element.42.refs_0_), channel_id=1, source_target_pairs={{0,8},{8,0},{16,24},{24,16},{1,9},{9,1},{17,25},{25,17},{2,10},{10... | collective-permute-start | bytes 1572872 | tf_op jit(solution)/shard_map/ppermute | solution.py:304
  77.6 14.0 %collective-permute-start.17 = (f32[2,512,128]{2,1,0:T(8,128)S(1)}, f32[2,512,128]{2,1,0:T(8,128)S(1)}, u32[]{:S(2)}, u32[]{:S(2)}) collective-permute-start(f32[2,512,128]{2,1,0:T(8,128)S(1)} %column_product.2.mine.refs_0_), channel_id=1, source_target_pairs={{0,1},{2,0},{4,2},{6,4},{7,6},{5,7},{3,5},{1,3},{8,9},{10,8},{12,1... | collective-permute-start | bytes 1572872 | tf_op jit(solution)/shard_map/ppermute | solution.py:293
  79.3 14.0 %collective-permute-start.16 = (f32[2,512,128]{2,1,0:T(8,128)S(1)}, f32[2,512,128]{2,1,0:T(8,128)S(1)}, u32[]{:S(2)}, u32[]{:S(2)}) collective-permute-start(f32[2,512,128]{2,1,0:T(8,128)S(1)} %column_product.2.mine.refs_0_), channel_id=1, source_target_pairs={{0,2},{2,4},{4,6},{6,7},{7,5},{5,3},{3,1},{1,0},{8,10},{10,12},{12... | collective-permute-start | bytes 1572872 | tf_op jit(solution)/shard_map/ppermute | solution.py:293
  91.6 13.1 %collective-permute-start.19 = (f32[2,512,128]{2,1,0:T(8,128)S(1)}, f32[2,512,128]{2,1,0:T(8,128)S(1)}, u32[]{:S(2)}, u32[]{:S(2)}) collective-permute-start(f32[2,512,128]{2,1,0:T(8,128)S(1)} %collective-permute-done.17.refs_1_), channel_id=1, source_target_pairs={{0,1},{2,0},{4,2},{6,4},{7,6},{5,7},{3,5},{1,3},{8,9},{10,8},{12,1... | collective-permute-start | bytes 1572872 | tf_op jit(solution)/shard_map/ppermute | solution.py:293
  93.2 13.1 %collective-permute-start.18 = (f32[2,512,128]{2,1,0:T(8,128)S(1)}, f32[2,512,128]{2,1,0:T(8,128)S(1)}, u32[]{:S(2)}, u32[]{:S(2)}) collective-permute-start(f32[2,512,128]{2,1,0:T(8,128)S(1)} %collective-permute-done.16.refs_0_), channel_id=1, source_target_pairs={{0,2},{2,4},{4,6},{6,7},{7,5},{5,3},{3,1},{1,0},{8,10},{10,12},{12... | collective-permute-start | bytes 1572872 | tf_op jit(solution)/shard_map/ppermute | solution.py:293
  104.8 12.2 %collective-permute-start.21 = (f32[2,512,128]{2,1,0:T(8,128)S(1)}, f32[2,512,128]{2,1,0:T(8,128)S(1)}, u32[]{:S(2)}, u32[]{:S(2)}) collective-permute-start(f32[2,512,128]{2,1,0:T(8,128)S(1)} %collective-permute-done.19.refs_3_), channel_id=1, source_target_pairs={{0,1},{2,0},{4,2},{6,4},{7,6},{5,7},{3,5},{1,3},{8,9},{10,8},{12,1... | collective-permute-start | bytes 1572872 | tf_op jit(solution)/shard_map/ppermute | solution.py:293
  106.4 12.3 %collective-permute-start.20 = (f32[2,512,128]{2,1,0:T(8,128)S(1)}, f32[2,512,128]{2,1,0:T(8,128)S(1)}, u32[]{:S(2)}, u32[]{:S(2)}) collective-permute-start(f32[2,512,128]{2,1,0:T(8,128)S(1)} %collective-permute-done.18.refs_2_), channel_id=1, source_target_pairs={{0,2},{2,4},{4,6},{6,7},{7,5},{5,3},{3,1},{1,0},{8,10},{10,12},{12... | collective-permute-start | bytes 1572872 | tf_op jit(solution)/shard_map/ppermute | solution.py:293
  117.0 6.4 %collective-permute-start.23 = (f32[1,512,128]{2,1,0:T(8,128)S(1)}, f32[1,512,128]{2,1,0:T(8,128)S(1)}, u32[]{:S(2)}, u32[]{:S(2)}) collective-permute-start(f32[1,512,128]{2,1,0:T(8,128)S(1)} %slice.26), channel_id=1, source_target_pairs={{0,1},{2,0},{4,2},{6,4},{7,6},{5,7},{3,5},{1,3},{8,9},{10,8},{12,1... | collective-permute-start | bytes 786440 | tf_op jit(solution)/shard_map/ppermute | solution.py:293
  118.7 6.4 %collective-permute-start.22 = (f32[1,512,128]{2,1,0:T(8,128)S(1)}, f32[1,512,128]{2,1,0:T(8,128)S(1)}, u32[]{:S(2)}, u32[]{:S(2)}) collective-permute-start(f32[1,512,128]{2,1,0:T(8,128)S(1)} %slice.25), channel_id=1, source_target_pairs={{0,2},{2,4},{4,6},{6,7},{7,5},{5,3},{3,1},{1,0},{8,10},{10,12},{12... | collective-permute-start | bytes 786440 | tf_op jit(solution)/shard_map/ppermute | solution.py:293
  127.4 10.2 %collective-permute-start.25 = (f32[2,512,128]{2,1,0:T(8,128)S(1)}, f32[2,512,128]{2,1,0:T(8,128)S(1)}, u32[]{:S(2)}, u32[]{:S(2)}) collective-permute-start(f32[2,512,128]{2,1,0:T(8,128)S(1)} %row_product.2.refs_1_), channel_id=1, source_target_pairs={{0,16},{8,24},{16,0},{24,8},{1,17},{9,25},{17,1},{25,9},{2,18},{10... | collective-permute-start | bytes 1572872 | tf_op jit(solution)/shard_map/ppermute | solution.py:304
  128.9 8.7 %collective-permute-start.24 = (f32[2,512,128]{2,1,0:T(8,128)S(1)}, f32[2,512,128]{2,1,0:T(8,128)S(1)}, u32[]{:S(2)}, u32[]{:S(2)}) collective-permute-start(f32[2,512,128]{2,1,0:T(8,128)S(1)} %row_product.2.refs_1_), channel_id=1, source_target_pairs={{0,8},{8,0},{16,24},{24,16},{1,9},{9,1},{17,25},{25,17},{2,10},{10... | collective-permute-start | bytes 1572872 | tf_op jit(solution)/shard_map/ppermute | solution.py:304
  142.1 14.0 %collective-permute-start.28 = (f32[2,512,128]{2,1,0:T(8,128)S(1)}, f32[2,512,128]{2,1,0:T(8,128)S(1)}, u32[]{:S(2)}, u32[]{:S(2)}) collective-permute-start(f32[2,512,128]{2,1,0:T(8,128)S(1)} %column_product.3.refs_0_.mine), channel_id=1, source_target_pairs={{0,1},{2,0},{4,2},{6,4},{7,6},{5,7},{3,5},{1,3},{8,9},{10,8},{12,1... | collective-permute-start | bytes 1572872 | tf_op jit(solution)/shard_map/ppermute | solution.py:293
  143.8 14.0 %collective-permute-start.27 = (f32[2,512,128]{2,1,0:T(8,128)S(1)}, f32[2,512,128]{2,1,0:T(8,128)S(1)}, u32[]{:S(2)}, u32[]{:S(2)}) collective-permute-start(f32[2,512,128]{2,1,0:T(8,128)S(1)} %column_product.3.refs_0_.mine), channel_id=1, source_target_pairs={{0,2},{2,4},{4,6},{6,7},{7,5},{5,3},{3,1},{1,0},{8,10},{10,12},{12... | collective-permute-start | bytes 1572872 | tf_op jit(solution)/shard_map/ppermute | solution.py:293
  156.1 13.1 %collective-permute-start.30 = (f32[2,512,128]{2,1,0:T(8,128)S(1)}, f32[2,512,128]{2,1,0:T(8,128)S(1)}, u32[]{:S(2)}, u32[]{:S(2)}) collective-permute-start(f32[2,512,128]{2,1,0:T(8,128)S(1)} %collective-permute-done.28.refs_2_.refs_1_), channel_id=1, source_target_pairs={{0,1},{2,0},{4,2},{6,4},{7,6},{5,7},{3,5},{1,3},{8,9},{10,8},{12,1... | collective-permute-start | bytes 1572872 | tf_op jit(solution)/shard_map/ppermute | solution.py:293
  157.8 13.1 %collective-permute-start.29 = (f32[2,512,128]{2,1,0:T(8,128)S(1)}, f32[2,512,128]{2,1,0:T(8,128)S(1)}, u32[]{:S(2)}, u32[]{:S(2)}) collective-permute-start(f32[2,512,128]{2,1,0:T(8,128)S(1)} %collective-permute-done.27.refs_1_.refs_0_), channel_id=1, source_target_pairs={{0,2},{2,4},{4,6},{6,7},{7,5},{5,3},{3,1},{1,0},{8,10},{10,12},{12... | collective-permute-start | bytes 1572872 | tf_op jit(solution)/shard_map/ppermute | solution.py:293
  169.3 12.2 %collective-permute-start.32 = (f32[2,512,128]{2,1,0:T(8,128)S(1)}, f32[2,512,128]{2,1,0:T(8,128)S(1)}, u32[]{:S(2)}, u32[]{:S(2)}) collective-permute-start(f32[2,512,128]{2,1,0:T(8,128)S(1)} %collective-permute-done.30.refs_4_.refs_3_), channel_id=1, source_target_pairs={{0,1},{2,0},{4,2},{6,4},{7,6},{5,7},{3,5},{1,3},{8,9},{10,8},{12,1... | collective-permute-start | bytes 1572872 | tf_op jit(solution)/shard_map/ppermute | solution.py:293
  170.9 12.3 %collective-permute-start.31 = (f32[2,512,128]{2,1,0:T(8,128)S(1)}, f32[2,512,128]{2,1,0:T(8,128)S(1)}, u32[]{:S(2)}, u32[]{:S(2)}) collective-permute-start(f32[2,512,128]{2,1,0:T(8,128)S(1)} %collective-permute-done.29.refs_3_.refs_2_), channel_id=1, source_target_pairs={{0,2},{2,4},{4,6},{6,7},{7,5},{5,3},{3,1},{1,0},{8,10},{10,12},{12... | collective-permute-start | bytes 1572872 | tf_op jit(solution)/shard_map/ppermute | solution.py:293
  181.5 6.4 %collective-permute-start.34 = (f32[1,512,128]{2,1,0:T(8,128)S(1)}, f32[1,512,128]{2,1,0:T(8,128)S(1)}, u32[]{:S(2)}, u32[]{:S(2)}) collective-permute-start(f32[1,512,128]{2,1,0:T(8,128)S(1)} %slice.28), channel_id=1, source_target_pairs={{0,1},{2,0},{4,2},{6,4},{7,6},{5,7},{3,5},{1,3},{8,9},{10,8},{12,1... | collective-permute-start | bytes 786440 | tf_op jit(solution)/shard_map/ppermute | solution.py:293
  183.2 6.4 %collective-permute-start.33 = (f32[1,512,128]{2,1,0:T(8,128)S(1)}, f32[1,512,128]{2,1,0:T(8,128)S(1)}, u32[]{:S(2)}, u32[]{:S(2)}) collective-permute-start(f32[1,512,128]{2,1,0:T(8,128)S(1)} %slice.27), channel_id=1, source_target_pairs={{0,2},{2,4},{4,6},{6,7},{7,5},{5,3},{3,1},{1,0},{8,10},{10,12},{12... | collective-permute-start | bytes 786440 | tf_op jit(solution)/shard_map/ppermute | solution.py:293
  194.1 10.3 %collective-permute-start.41 = (f32[2,512,128]{2,1,0:T(8,128)S(1)}, f32[2,512,128]{2,1,0:T(8,128)S(1)}, u32[]{:S(2)}, u32[]{:S(2)}) collective-permute-start(f32[2,512,128]{2,1,0:T(8,128)S(1)} %row_product.3.refs_0_), channel_id=1, source_target_pairs={{0,16},{8,24},{16,0},{24,8},{1,17},{9,25},{17,1},{25,9},{2,18},{10... | collective-permute-start | bytes 1572872 | tf_op jit(solution)/shard_map/ppermute | solution.py:304
  195.8 15.4 %collective-permute-start.40 = (f32[2,512,128]{2,1,0:T(8,128)S(1)}, f32[2,512,128]{2,1,0:T(8,128)S(1)}, u32[]{:S(2)}, u32[]{:S(2)}) collective-permute-start(f32[2,512,128]{2,1,0:T(8,128)S(1)} %row_product.3.refs_0_), channel_id=1, source_target_pairs={{0,8},{8,0},{16,24},{24,16},{1,9},{9,1},{17,25},{25,17},{2,10},{10... | collective-permute-start | bytes 1572872 | tf_op jit(solution)/shard_map/ppermute | solution.py:304
  204.4 6.8 %collective-permute-start.42 = (f32[2,512,128]{2,1,0:T(8,128)S(1)}, f32[2,512,128]{2,1,0:T(8,128)S(1)}, u32[]{:S(2)}, u32[]{:S(2)}) collective-permute-start(f32[2,512,128]{2,1,0:T(8,128)S(1)} %collective-permute-done.41.refs_2_), channel_id=1, source_target_pairs={{0,8},{8,0},{16,24},{24,16},{1,9},{9,1},{17,25},{25,17},{2,10},{10... | collective-permute-start | bytes 1572872 | tf_op jit(solution)/shard_map/ppermute | solution.py:304
  221.9 8.9 %collective-permute-start.45 = (f32[128,128]{1,0:T(8,128)S(1)}, f32[128,128]{1,0:T(8,128)S(1)}, u32[]{:S(2)}, u32[]{:S(2)}) collective-permute-start(f32[128,128]{1,0:T(8,128)S(1)} %add.38), channel_id=1, source_target_pairs={{0,4},{1,5},{2,6},{3,7},{4,0},{5,1},{6,2},{7,3},{8,12},{9,13},{10,... | collective-permute-start | bytes 196616 | tf_op jit(solution)/shard_map/ppermute | solution.py:304
  (18 other events, 85.8 us)

commit v2 on v1

v2 whole, which is shorter than its diff:
```python
import functools

import jax
import jax.numpy as jnp
import numpy as np
from jax import lax
from jax.experimental import pallas as pl
from jax.experimental.pallas import tpu as pltpu
from jax.sharding import PartitionSpec as P

HIGHEST = lax.Precision.HIGHEST
PANEL = 8
VMEM = pl.BlockSpec(memory_space=pltpu.VMEM)
SMEM = pl.BlockSpec(memory_space=pltpu.SMEM)
ANY = pl.BlockSpec(memory_space=pl.ANY)


def call(kernel, out_shape, in_specs, out_specs, args, scratch=(), flops=0, name=None):
    moved = sum(a.size * a.dtype.itemsize for a in args)
    return pl.pallas_call(
        kernel,
        out_shape=out_shape,
        in_specs=in_specs,
        out_specs=out_specs,
        scratch_shapes=list(scratch),
        compiler_params=pltpu.CompilerParams(vmem_limit_bytes=40 * 1024 * 1024),
        cost_estimate=pl.CostEstimate(flops=flops, bytes_accessed=moved, transcendentals=0),
        name=name,
    )(*args)


def split(value):
    high = value.astype(jnp.bfloat16)
    return high, (value - high.astype(jnp.float32)).astype(jnp.bfloat16)


def dot3(left_high, left_low, right):
    right_high, right_low = split(right)
    dot = functools.partial(jnp.dot, preferred_element_type=jnp.float32)
    return dot(left_high, right_high) + (dot(left_high, right_low) + dot(left_low, right_high))


def self_product(value):
    high, low = split(value)

    def dot(left, right):
        return lax.dot_general(left, right, (((0,), (0,)), ((), ())), preferred_element_type=jnp.float32)

    mixed = dot(high, low)
    return dot(high, high) + (dot(low, low) + (mixed + mixed.T))


def prepare_kernel(slots, values, *outs):
    for s in range(slots):
        high, low, high_t, low_t = outs[4 * s : 4 * s + 4]
        high[...], low[...] = split(values[s])
        high_t[...], low_t[...] = split(values[s].T)


def table_row(table, places, entry, slots, slot):
    place = places[entry]
    return jnp.where(place >= 0, table[jnp.maximum(place, 0) * slots + slot], -1)


def pick(row, held, first_unit, unit, per_block, out, begin, base):
    vec = out.shape[1]
    count = held.shape[0] // unit
    for i in range(out.shape[0] // unit):
        value = jnp.zeros((unit, vec), out.dtype)
        for ref, ref_begin in base:
            at = begin + i * unit - ref_begin
            if 0 <= at < ref.shape[0]:
                value = value + ref[at : at + unit, :]
        local = row * per_block + begin // unit + i - first_unit
        valid = (row >= 0) & (local >= 0) & (local < count)
        rows = pl.ds(pl.multiple_of(jnp.clip(local, 0, count - 1) * unit, unit), unit)
        out[i * unit : (i + 1) * unit, :] = jnp.where(valid, held[rows, :], value)


def ring_kernel(entry, slots, slot, begin, befores, unit, per_block, table, places, held, *refs):
    base, out = list(zip(refs[:-1], befores)), refs[-1]
    pick(table_row(table, places, entry, slots, slot), held, places[0], unit, per_block, out, begin, base)


def first_kernel(entry, slots, slot, befores, unit, per_block, table, places, held, high_t, low_t, *refs):
    base, (x_out, p_out) = list(zip(refs[:-2], befores)), refs[-2:]
    pick(table_row(table, places, entry, slots, slot), held, places[0], unit, per_block, x_out, 0, base)
    p_out[...] = dot3(high_t[...], low_t[...], x_out[...])


def add_matching(hits, copies, total):
    for hit, (copy, _, _) in zip(hits, copies):

        @pl.when(hit)
        def _():
            copy.start()

    for hit, (copy, landing, rows) in zip(hits, copies):

        @pl.when(hit)
        def _():
            copy.wait()
            total[rows, :] += landing[...]


def column_kernel(slots, slot, last, columns, scalars, high, low, *refs):
    refs = list(refs)
    older = refs.pop(0) if last else None
    mine = refs.pop(0)
    arrived, (q_out, total, landing, sems) = refs[:-4], refs[-4:]
    center, radius = scalars[0], scalars[1]
    column = columns[slot]
    others = [k for k in range(len(arrived) + 1) if k != slot]
    hits, copies = [], []
    for i, k in enumerate(others):
        hits.append((columns[k] == column) & (column >= 0))
        copies.append(
            (pltpu.make_async_copy(arrived[i], landing.at[i], sems.at[i]), landing.at[i], slice(0, total.shape[0]))
        )
    total[...] = mine[...]
    add_matching(hits, copies, total)
    q = dot3(high[...], low[...], total[...])
    if last:
        q = (2.0 / radius) * (q - (center / radius) * older[...])
    q_out[...] = q


def row_kernel(slots, pieces, last, table, places, scalars, *refs):
    refs = list(refs)
    high_t, low_t, mine, vectors = [[refs.pop(0) for _ in range(slots)] for _ in range(4)]
    arrived, p_out, (total, landing, sems) = refs[: len(pieces)], refs[len(pieces) : -3], refs[-3:]
    center, radius = scalars[0], scalars[1]
    rows = [table_row(table, places, entry, slots, slot) for entry, slot, _ in pieces]

    def copy(b):
        return pltpu.make_async_copy(arrived[b], landing.at[b, pl.ds(0, arrived[b].shape[0])], sems.at[b])

    def each(action):
        for b in range(len(pieces)):
            hit = rows[b] < -1
            for s in range(slots):
                hit = hit | ((rows[b] == table[s]) & (rows[b] >= 0))

            @pl.when(hit)
            def _():
                action(b)

    each(lambda b: copy(b).start())
    for s in range(slots):
        total[s] = mine[s][...]
        for t in range(slots):
            if t != s:

                @pl.when((table[t] == table[s]) & (table[s] >= 0))
                def _():
                    total[s] += mine[t][...]

    def add(b):
        copy(b).wait()
        first, count = pieces[b][2], arrived[b].shape[0]
        for s in range(slots):

            @pl.when(rows[b] == table[s])
            def _():
                total[s, first : first + count, :] += landing[b, :count, :]

    each(add)
    for s in range(slots):
        if last:
            y = total[s] + (2.0 * (center / radius) * (center / radius) - 1.0) * vectors[s][...]
        else:
            y = (total[s] - center * vectors[s][...]) / radius
        p_out[s][...] = dot3(high_t[s][...], low_t[s][...], y)


def owner_kernel(slots, pieces, unit, per_block, table, places, scalars, start, *refs):
    arrived, (y_out, gram_out, landing, sems) = refs[:-4], refs[-4:]
    center, radius = scalars[0], scalars[1]
    held = y_out.shape[0] // unit

    def copy(b):
        return pltpu.make_async_copy(arrived[b], landing.at[b, pl.ds(0, arrived[b].shape[0])], sems.at[b])

    def each(action):
        for b, (entry, slot, first) in enumerate(pieces):
            row = table_row(table, places, entry, slots, slot)
            count = arrived[b].shape[0] // unit
            begin = row * per_block + first // unit - places[0]

            @pl.when((row >= 0) & (begin + count > 0) & (begin < held))
            def _():
                action(b, begin, count)

    each(lambda b, begin, count: copy(b).start())
    y_out[...] = (2.0 * (center / radius) * (center / radius) - 1.0) * start[...]

    def add(b, begin, count):
        copy(b).wait()
        for i in range(count):
            local = begin + i

            @pl.when((local >= 0) & (local < held))
            def _():
                rows = pl.ds(pl.multiple_of(jnp.clip(local, 0, held - 1) * unit, unit), unit)
                y_out[rows, :] += landing[b, i * unit : (i + 1) * unit, :]

    each(add)
    gram_out[...] = self_product(y_out[...])


def inner_kernel(slots, columns, place, *refs):
    arrived, out, order, total = refs[:-3], refs[-3], refs[-2], refs[-1]
    count, size = len(arrived), order.shape[1]
    for k, held in enumerate(arrived):
        order[lax.bitwise_xor(place[0], k // slots) * slots + k % slots] = held[...]
    ids = [columns[lax.bitwise_xor(place[0], i // slots) * slots + i % slots] for i in range(count)]
    for i in range(count):
        earlier = ids[i] < 0
        for k in range(i):
            earlier = earlier | (ids[k] == ids[i])
        total[i * size : (i + 1) * size, :] = jnp.where(earlier, 0.0, order[i])
        for k in range(i + 1, count):

            @pl.when((ids[k] == ids[i]) & jnp.logical_not(earlier))
            def _():
                total[i * size : (i + 1) * size, :] += order[k]

    out[...] = self_product(total[...])


def factor_kernel(gram, following, basis_out, inverse_out):
    order = gram.shape[0]
    blocks = order // PANEL
    shape = (PANEL, order)
    below = lax.broadcasted_iota(jnp.int32, shape, 0)
    lane = lax.broadcasted_iota(jnp.int32, shape, 1)
    left = [gram[b * PANEL : (b + 1) * PANEL, :] for b in range(blocks)]
    right = [jnp.where(lane == below + b * PANEL, 1.0, 0.0) for b in range(blocks)]

    def spread(block, k):
        return jnp.broadcast_to(block[k : k + 1, :], shape)

    for b in range(blocks):
        rest = range(b, blocks)
        panel = [
            {i: jnp.broadcast_to(left[i][:, b * PANEL + j : b * PANEL + j + 1], shape) for i in rest}
            for j in range(PANEL)
        ]
        scale = jnp.ones(shape, jnp.float32)
        for k in range(PANEL):
            pivot = spread(panel[k][b], k)
            inverse = 1.0 / pivot
            scale = jnp.where(below == k, lax.rsqrt(pivot), scale)
            factor = {i: panel[k][i] * inverse for i in rest}
            factor[b] = jnp.where(below > k, factor[b], 0.0)
            left_row, right_row = spread(left[b], k), spread(right[b], k)
            for j in range(k + 1, PANEL):
                row = spread(panel[j][b], k)
                for i in rest:
                    panel[j][i] = panel[j][i] - factor[i] * row
            for i in rest:
                left[i] = left[i] - factor[i] * left_row
                right[i] = right[i] - factor[i] * right_row
        inverse_out[b * PANEL : (b + 1) * PANEL, :] = right[b] * scale
    basis_out[...] = lax.dot_general(
        following[...], inverse_out[...], (((1,), (1,)), ((), ())), precision=HIGHEST, preferred_element_type=jnp.float32
    )


def project_kernel(inverse, inner, out):
    half = jnp.dot(inverse[...], inner[...], precision=HIGHEST, preferred_element_type=jnp.float32)
    out[...] = lax.dot_general(
        half, inverse[...], (((1,), (1,)), ((), ())), precision=HIGHEST, preferred_element_type=jnp.float32
    )


def solution(mesh):
    n_row, n_col = mesh.shape["row"], mesh.shape["col"]
    tie = lax.optimization_barrier
    far = n_col // 2

    ring = list(range(0, n_col, 2)) + list(range(1, n_col, 2))[::-1]
    position = {col: k for k, col in enumerate(ring)}

    place_lines = np.array(
        [[0] + [col ^ ring[(position[col] + d) % n_col] for d in range(-far, far + 1)] for col in range(n_col)], np.int32
    )

    def at(distance):
        return far + 1 + distance

    def forward(value, step):
        return lax.ppermute(value, "col", [(col, ring[(k + step) % n_col]) for k, col in enumerate(ring)])

    def shares(distance, size):
        if 2 * distance < n_col:
            return (1, 0, size), (-1, 0, size)
        return (1, 0, size // 2), (-1, size // 2, size)

    def flip(value, axis, bit):
        size = n_row if axis == "row" else n_col
        return lax.ppermute(value, axis, [(i, i ^ bit) for i in range(size)])

    def table_over(own, axis):
        for bit in powers(n_row if axis == "row" else n_col):
            own = jnp.concatenate([own, flip(own, axis, bit)])
        return own

    def gather_rest(own, across):
        top = powers(n_row)[-1]
        held = {0: own, top: across}
        bit = top // 2
        while bit:
            held.update({j ^ bit: [flip(v, "row", bit) for v in values] for j, values in list(held.items())})
            bit //= 2
        return sum([held[j] for j in range(n_row)], [])

    def gather_row(own):
        return gather_rest(own, [flip(value, "row", powers(n_row)[-1]) for value in own])

    def sum_over(value, axis, bits):
        for bit in bits:
            value = value + flip(value, axis, bit)
        return value

    def powers(size):
        return [1 << k for k in range(size.bit_length() - 1)]

    def gather_col(own):
        held = [{1: value, -1: value} for value in own]
        pieces, got = [], []
        for distance in range(1, far + 1):
            for slot, value in enumerate(own):
                for step, first, end in shares(distance, value.shape[0]):
                    chunk = held[slot][step]
                    if end - first < chunk.shape[0]:
                        chunk = chunk[first:end]
                    held[slot][step] = forward(chunk, step)
                    pieces.append((at(-step * distance), slot, first))
                    got.append(held[slot][step])
        return pieces, got

    def body(start_block, block_values, block_rows, block_cols, block_count, center, radius):
        values = block_values[0]
        slots, size, _ = values.shape
        held_rows, vec = start_block.shape
        unit = min(size // 2, held_rows)
        per_block = size // unit
        live = jnp.arange(slots) < block_count[0, 0]
        rows = jnp.where(live, block_rows[0], -1)
        cols = jnp.where(live, block_cols[0], -1)
        col = lax.axis_index("col")
        with jax.named_scope("tables"):
            table = table_over(rows, "col")
            columns = table_over(cols, "row")
        places = jnp.asarray(place_lines)[col]
        places = places.at[0].set(col * (held_rows // unit))
        scalars = jnp.concatenate([center, radius])
        row_bits, col_bits = powers(n_row), powers(n_col)

        chunk = jax.ShapeDtypeStruct((size, vec), jnp.float32)
        square = jax.ShapeDtypeStruct((vec, vec), jnp.float32)
        half_block = jax.ShapeDtypeStruct((size, size), jnp.bfloat16)
        blocks = call(
            functools.partial(prepare_kernel, slots),
            [half_block] * (4 * slots),
            [VMEM],
            [VMEM] * (4 * slots),
            [values],
            name="split_blocks",
        )
        flops = 6 * size * size * vec

        before = [{1: [], -1: []} for _ in range(slots)]
        for distance in range(far, 0, -1):
            for slot in range(slots):
                for step, first, end in shares(distance, size):
                    prior = before[slot][step]
                    value = call(
                        functools.partial(
                            ring_kernel, at(step * distance), slots, slot, first, [b[1] for b in prior], unit, per_block
                        ),
                        jax.ShapeDtypeStruct((end - first, vec), jnp.float32),
                        [SMEM, SMEM] + [VMEM] * (1 + len(prior)),
                        VMEM,
                        [table, places, start_block] + [b[0] for b in prior],
                        name="pick_rows",
                    )
                    before[slot][step] = [(forward(value, step), first)]
            if distance == 2:
                value, first = before[0][1][0]
                value, columns, blocks = tie((value, columns, blocks))
                before[0][1] = [(value, first)]
        high, low, high_t, low_t = [[blocks[4 * s + k] for s in range(slots)] for k in range(4)]

        def first_step(slot):
            arrived = before[slot][1] + before[slot][-1]
            return call(
                functools.partial(first_kernel, at(0), slots, slot, [b[1] for b in arrived], unit, per_block),
                [chunk] * 2,
                [SMEM, SMEM] + [VMEM] * (3 + len(arrived)),
                [VMEM] * 2,
                [table, places, start_block, high_t[slot], low_t[slot]] + [b[0] for b in arrived],
                flops=flops,
                name="first_product",
            )

        def column_step(chunks, older=None):
            out = []
            for slot in range(slots):
                others = chunks[:slot] + chunks[slot + 1 :]
                more = [] if older is None else [older[slot]]
                out.append(
                    call(
                        functools.partial(column_kernel, slots, slot, older is not None),
                        chunk,
                        [SMEM, SMEM] + [VMEM] * (3 + len(more)) + [ANY] * len(others),
                        VMEM,
                        [columns, scalars, high[slot], low[slot]] + more + [chunks[slot]] + others,
                        scratch=[
                            pltpu.VMEM(chunk.shape, jnp.float32),
                            pltpu.VMEM((len(others), size, vec), jnp.float32),
                            pltpu.SemaphoreType.DMA((len(others),)),
                        ],
                        flops=flops,
                        name="column_product",
                    )
                )
            return out

        def row_step(last, mine, pieces, got, vectors):
            return call(
                functools.partial(row_kernel, slots, pieces, last),
                [chunk] * slots,
                [SMEM] * 3 + [VMEM] * (4 * slots) + [ANY] * len(got),
                [VMEM] * slots,
                [table, places, scalars] + high_t + low_t + mine + vectors + got,
                scratch=[
                    pltpu.VMEM((slots, size, vec), jnp.float32),
                    pltpu.VMEM((len(got), size, vec), jnp.float32),
                    pltpu.SemaphoreType.DMA((len(got),)),
                ],
                flops=flops * slots,
                name="row_product",
            )

        xs, ps = zip(*[first_step(slot) for slot in range(slots)])
        xs, ps = list(xs), list(ps)
        qs = column_step(gather_row(ps))
        ps = list(row_step(False, qs, *gather_col(qs), xs))
        gs = column_step(gather_row(ps), qs)
        pieces, got = gather_col(gs)

        owner_pieces = [(at(0), slot, 0) for slot in range(slots)] + pieces
        following, gram_matrix = call(
            functools.partial(owner_kernel, slots, owner_pieces, unit, per_block),
            [jax.ShapeDtypeStruct(start_block.shape, jnp.float32), square],
            [SMEM] * 3 + [VMEM] + [ANY] * len(owner_pieces),
            [VMEM] * 2,
            [table, places, scalars, start_block] + gs + got,
            scratch=[
                pltpu.VMEM((len(owner_pieces), size, vec), jnp.float32),
                pltpu.SemaphoreType.DMA((len(owner_pieces),)),
            ],
            flops=6 * held_rows * vec * vec,
            name="owner_rows",
        )
        gram_matrix, gs = tie((gram_matrix, gs))
        ps = list(row_step(True, gs, pieces, got, xs))
        gram_matrix = sum_over(gram_matrix, "row", row_bits[:-1])
        across = [flip(p, "row", row_bits[-1]) for p in ps]
        gram_matrix = sum_over(gram_matrix, "col", col_bits[:2])
        gram_matrix, across = tie((gram_matrix, across))
        images = gather_rest(ps, across)
        gram_matrix = sum_over(gram_matrix, "col", col_bits[2:])
        gram_matrix = sum_over(gram_matrix, "row", row_bits[-1:])
        inner_local = call(
            functools.partial(inner_kernel, slots),
            square,
            [SMEM, SMEM] + [VMEM] * len(images),
            VMEM,
            [columns, lax.axis_index("row").reshape(1)] + images,
            scratch=[
                pltpu.VMEM((len(images), size, vec), jnp.float32),
                pltpu.VMEM((len(images) * size, vec), jnp.float32),
            ],
            flops=6 * len(images) * size * vec * vec,
            name="inner_product",
        )
        inner_matrix = sum_over(inner_local, "col", col_bits)
        basis_block, inverse = call(
            factor_kernel,
            [jax.ShapeDtypeStruct(start_block.shape, jnp.float32), square],
            [VMEM] * 2,
            [VMEM] * 2,
            [gram_matrix, following],
            flops=12 * held_rows * vec * vec,
            name="factor_and_basis",
        )
        projected = call(project_kernel, square, [VMEM] * 2, VMEM, [inverse, inner_matrix], name="project")
        return (basis_block, projected)

    in_specs = (
        P(("row", "col"), None),
        P("row", "col", None, None),
        P("row", "col"),
        P("row", "col"),
        P("row", "col"),
        P(),
        P(),
    )
    out_specs = (P(("row", "col"), None), P())
    return jax.shard_map(body, mesh=mesh, in_specs=in_specs, out_specs=out_specs, check_vma=False)
```

time: 232 us -> 218 us (0.940)
  waiting for transfers between devices: 150 us -> 105 us
  starting transfers between devices: 48.2 us -> 72.8 us
  Pallas kernels: 28.1 us -> 33.8 us
    ppermute x24 -> x48, waiting for transfers between devices: 105 us -> 66.1 us  [forward(): lax.ppermute(value, 'col', [(col, ring[(k + step) % n_col]) for k, col in...]
    ppermute x24 -> x48, starting transfers between devices: 25.5 us -> 50.1 us  [forward(): lax.ppermute(value, 'col', [(col, ring[(k + step) % n_col]) for k, col in...]
    ppermute x22 -> x31, waiting for transfers between devices: 44.8 us -> 39 us  [flip(): return lax.ppermute(value, axis, [(i, i ^ bit) for i in range(size)])]
    pallas_call x18 -> x29, Pallas kernels: 28.1 us -> 33.8 us  [call(): pl.pallas_call(kernel, out_shape=out_shape, in_specs=in_specs, out_specs=...]
    ppermute x22 -> x31, starting transfers between devices: 22.7 us -> 22.7 us  [flip(): return lax.ppermute(value, axis, [(i, i ^ bit) for i in range(size)])]
  transfers between devices with their start and end apart: 46 -> 79, of which waited for: 32 -> 45; matrix products, arithmetic and copies ran while one was open for 0% -> 0% of each run, Pallas kernels for 6% -> 10%
where the time goes in v2:
time: 218 us
  waiting for transfers between devices  105 us (48%)
  starting transfers between devices  72.8 us (33%)
  Pallas kernels  33.8 us (16%)
  between operations  3 us (1%)
    ppermute x48, waiting for transfers between devices, forward(): lax.ppermute(value, 'col', [(col, ring[(k + step) % n_col]) for k, col in...  66.1 us
    ppermute x48, starting transfers between devices, forward(): lax.ppermute(value, 'col', [(col, ring[(k + step) % n_col]) for k, col in...  50.1 us
    ppermute x31, waiting for transfers between devices, flip(): return lax.ppermute(value, axis, [(i, i ^ bit) for i in range(size)])  39 us
    pallas_call x29, Pallas kernels, call(): pl.pallas_call(kernel, out_shape=out_shape, in_specs=in_specs, out_specs=...  33.8 us
    ppermute x31, starting transfers between devices, flip(): return lax.ppermute(value, axis, [(i, i ^ bit) for i in range(size)])  22.7 us
  transfers between devices with their start and end apart: 79, of which 45 were waited for; matrix products, arithmetic and copies ran while one was open for 0% of the time, Pallas kernels for 10%

profile of v2, /device:TPU:0, one launch (start us, length us, event | category | flops | bytes accessed | tf_op | source)
XLA Modules:
  0.0 217.9 jit_solution(7298572082751022881)
XLA Ops:
  1.9 3.0 %collective-permute-start = (s32[2]{0:T(128)S(1)}, s32[2]{0:T(128)S(1)}, u32[]{:S(2)}, u32[]{:S(2)}) collective-permute-start(s32[2]{0:T(128)S(1)} %compare_select_fusion.1), channel_id=1, source_target_pairs={{0,1},{1,0},{2,3},{3,2},{4,5},{5,4},{6,7},{7,6},{8,9},{9,8},{10,11... | collective-permute-start | bytes 32 | tf_op jit(solution)/shard_map/tables/ppermute | solution.py:302
  6.5 2.1 collective-permute-start.1
  10.2 3.0 %collective-permute-start.2 = (s32[8]{0:T(128)S(1)}, s32[8]{0:T(128)S(1)}, u32[]{:S(2)}, u32[]{:S(2)}) collective-permute-start(s32[8]{0:T(128)S(1)} %pad_add_fusion.1), channel_id=1, source_target_pairs={{0,4},{1,5},{2,6},{3,7},{4,0},{5,1},{6,2},{7,3},{8,12},{9,13},{10,... | collective-permute-start | bytes 104 | tf_op jit(solution)/shard_map/tables/ppermute | solution.py:302
  29.7 2.8 %collective-permute-done.18.refs_0_ = f32[512,128]{1,0:T(8,128)S(1)} collective-permute-done((f32[512,128]{1,0:T(8,128)S(1)}, f32[512,128]{1,0:T(8,128)S(1)}, u32[]{:S(2)}, u32[]{:S(2)}) %collective-permute-start.18) | collective-permute-done | bytes 262176 | tf_op jit(solution)/shard_map/ppermute | solution.py:293
  35.9 2.3 %collective-permute-done.10.refs_0_ = f32[512,128]{1,0:T(8,128)S(1)} collective-permute-done((f32[512,128]{1,0:T(8,128)S(1)}, f32[512,128]{1,0:T(8,128)S(1)}, u32[]{:S(2)}, u32[]{:S(2)}) %collective-permute-start.10) | collective-permute-done | bytes 262176 | tf_op jit(solution)/shard_map/ppermute | solution.py:293
  51.3 3.1 %collective-permute-done.20.refs_1_ = f32[512,128]{1,0:T(8,128)S(1)} collective-permute-done((f32[512,128]{1,0:T(8,128)S(1)}, f32[512,128]{1,0:T(8,128)S(1)}, u32[]{:S(2)}, u32[]{:S(2)}) %collective-permute-start.20) | collective-permute-done | bytes 262176 | tf_op jit(solution)/shard_map/ppermute | solution.py:293
  54.4 2.2 %collective-permute-done.16.refs_0_ = f32[512,128]{1,0:T(8,128)S(1)} collective-permute-done((f32[512,128]{1,0:T(8,128)S(1)}, f32[512,128]{1,0:T(8,128)S(1)}, u32[]{:S(2)}, u32[]{:S(2)}) %collective-permute-start.16) | collective-permute-done | bytes 262176 | tf_op jit(solution)/shard_map/ppermute | solution.py:293
  64.3 5.5 %collective-permute-done.23.refs_4_ = f32[512,128]{1,0:T(8,128)S(1)} collective-permute-done((f32[512,128]{1,0:T(8,128)S(1)}, f32[512,128]{1,0:T(8,128)S(1)}, u32[]{:S(2)}, u32[]{:S(2)}) %collective-permute-start.23) | collective-permute-done | bytes 262176 | tf_op jit(solution)/shard_map/ppermute | solution.py:302
  78.0 3.8 %collective-permute-done.28.refs_9_ = f32[512,128]{1,0:T(8,128)S(1)} collective-permute-done((f32[512,128]{1,0:T(8,128)S(1)}, f32[512,128]{1,0:T(8,128)S(1)}, u32[]{:S(2)}, u32[]{:S(2)}) %collective-permute-start.28) | collective-permute-done | bytes 262176 | tf_op jit(solution)/shard_map/ppermute | solution.py:293
  83.8 3.5 %collective-permute-done.30.refs_11_ = f32[512,128]{1,0:T(8,128)S(1)} collective-permute-done((f32[512,128]{1,0:T(8,128)S(1)}, f32[512,128]{1,0:T(8,128)S(1)}, u32[]{:S(2)}, u32[]{:S(2)}) %collective-permute-start.30) | collective-permute-done | bytes 262176 | tf_op jit(solution)/shard_map/ppermute | solution.py:293
  89.5 3.5 %collective-permute-done.32.refs_13_ = f32[512,128]{1,0:T(8,128)S(1)} collective-permute-done((f32[512,128]{1,0:T(8,128)S(1)}, f32[512,128]{1,0:T(8,128)S(1)}, u32[]{:S(2)}, u32[]{:S(2)}) %collective-permute-start.32) | collective-permute-done | bytes 262176 | tf_op jit(solution)/shard_map/ppermute | solution.py:293
  95.1 3.5 %collective-permute-done.34.refs_15_ = f32[512,128]{1,0:T(8,128)S(1)} collective-permute-done((f32[512,128]{1,0:T(8,128)S(1)}, f32[512,128]{1,0:T(8,128)S(1)}, u32[]{:S(2)}, u32[]{:S(2)}) %collective-permute-start.34) | collective-permute-done | bytes 262176 | tf_op jit(solution)/shard_map/ppermute | solution.py:293
  100.7 3.5 %collective-permute-done.36.refs_17_ = f32[512,128]{1,0:T(8,128)S(1)} collective-permute-done((f32[512,128]{1,0:T(8,128)S(1)}, f32[512,128]{1,0:T(8,128)S(1)}, u32[]{:S(2)}, u32[]{:S(2)}) %collective-permute-start.36) | collective-permute-done | bytes 262176 | tf_op jit(solution)/shard_map/ppermute | solution.py:293
  106.4 3.5 %collective-permute-done.38.refs_19_ = f32[512,128]{1,0:T(8,128)S(1)} collective-permute-done((f32[512,128]{1,0:T(8,128)S(1)}, f32[512,128]{1,0:T(8,128)S(1)}, u32[]{:S(2)}, u32[]{:S(2)}) %collective-permute-start.38) | collective-permute-done | bytes 262176 | tf_op jit(solution)/shard_map/ppermute | solution.py:293
  116.6 2.1 row_product.2
  121.3 6.7 %collective-permute-done.45.refs_5_ = f32[512,128]{1,0:T(8,128)S(1)} collective-permute-done((f32[512,128]{1,0:T(8,128)S(1)}, f32[512,128]{1,0:T(8,128)S(1)}, u32[]{:S(2)}, u32[]{:S(2)}) %collective-permute-start.45) | collective-permute-done | bytes 262176 | tf_op jit(solution)/shard_map/ppermute | solution.py:302
  128.0 2.9 %collective-permute-done.46.refs_6_ = f32[512,128]{1,0:T(8,128)S(1)} collective-permute-done((f32[512,128]{1,0:T(8,128)S(1)}, f32[512,128]{1,0:T(8,128)S(1)}, u32[]{:S(2)}, u32[]{:S(2)}) %collective-permute-start.46) | collective-permute-done | bytes 262176 | tf_op jit(solution)/shard_map/ppermute | solution.py:302
  139.4 3.8 %collective-permute-done.50.refs_3_.refs_9_ = f32[512,128]{1,0:T(8,128)S(1)} collective-permute-done((f32[512,128]{1,0:T(8,128)S(1)}, f32[512,128]{1,0:T(8,128)S(1)}, u32[]{:S(2)}, u32[]{:S(2)}) %collective-permute-start.50) | collective-permute-done | bytes 262176 | tf_op jit(solution)/shard_map/ppermute | solution.py:293
  145.2 3.6 %collective-permute-done.52.refs_5_.refs_11_ = f32[512,128]{1,0:T(8,128)S(1)} collective-permute-done((f32[512,128]{1,0:T(8,128)S(1)}, f32[512,128]{1,0:T(8,128)S(1)}, u32[]{:S(2)}, u32[]{:S(2)}) %collective-permute-start.52) | collective-permute-done | bytes 262176 | tf_op jit(solution)/shard_map/ppermute | solution.py:293
  150.8 3.6 %collective-permute-done.54.refs_7_.refs_13_ = f32[512,128]{1,0:T(8,128)S(1)} collective-permute-done((f32[512,128]{1,0:T(8,128)S(1)}, f32[512,128]{1,0:T(8,128)S(1)}, u32[]{:S(2)}, u32[]{:S(2)}) %collective-permute-start.54) | collective-permute-done | bytes 262176 | tf_op jit(solution)/shard_map/ppermute | solution.py:293
  156.4 3.6 %collective-permute-done.56.refs_9_.refs_15_ = f32[512,128]{1,0:T(8,128)S(1)} collective-permute-done((f32[512,128]{1,0:T(8,128)S(1)}, f32[512,128]{1,0:T(8,128)S(1)}, u32[]{:S(2)}, u32[]{:S(2)}) %collective-permute-start.56) | collective-permute-done | bytes 262176 | tf_op jit(solution)/shard_map/ppermute | solution.py:293
  162.1 3.6 %collective-permute-done.58.refs_11_.refs_17_ = f32[512,128]{1,0:T(8,128)S(1)} collective-permute-done((f32[512,128]{1,0:T(8,128)S(1)}, f32[512,128]{1,0:T(8,128)S(1)}, u32[]{:S(2)}, u32[]{:S(2)}) %collective-permute-start.58) | collective-permute-done | bytes 262176 | tf_op jit(solution)/shard_map/ppermute | solution.py:293
  167.8 3.5 %collective-permute-done.60.refs_13_.refs_19_ = f32[512,128]{1,0:T(8,128)S(1)} collective-permute-done((f32[512,128]{1,0:T(8,128)S(1)}, f32[512,128]{1,0:T(8,128)S(1)}, u32[]{:S(2)}, u32[]{:S(2)}) %collective-permute-start.60) | collective-permute-done | bytes 262176 | tf_op jit(solution)/shard_map/ppermute | solution.py:293
  178.1 2.2 %owner_rows.1 = (f32[2048,128]{1,0:T(8,128)S(1)}, f32[128,128]{1,0:T(8,128)S(1)}) custom-call(s32[16]{0:T(128)S(1)} %pad_add_fusion.2.table, s32[10]{0:T(128)S(1)} %constant_dynamic-update-slice_fusion.places, f32[2]{0:T(128)S(1)} %pad_maximum_fusion.scalars, f32[2048,128]{1,0:T(8,128)S(1)} %copy-done.1, f32[512,128]{1,0:T(8,128)S(1)} %column_product.6.refs_0_.refs_4_, ...), custom_call_target="tpu_custom_call" | custom-call | flops 201326592 | bytes 5242992 | tf_op jit(solution)/shard_map/owner_rows/pallas_call | solution.py:20
  180.3 2.2 row_product.3
  187.3 2.8 %collective-permute-done.66 = f32[128,128]{1,0:T(8,128)S(1)} collective-permute-done((f32[128,128]{1,0:T(8,128)S(1)}, f32[128,128]{1,0:T(8,128)S(1)}, u32[]{:S(2)}, u32[]{:S(2)}) %collective-permute-start.66) | collective-permute-done | bytes 65568 | tf_op jit(solution)/shard_map/ppermute | solution.py:302
  191.3 3.2 %collective-permute-done.67 = f32[128,128]{1,0:T(8,128)S(1)} collective-permute-done((f32[128,128]{1,0:T(8,128)S(1)}, f32[128,128]{1,0:T(8,128)S(1)}, u32[]{:S(2)}, u32[]{:S(2)}) %collective-permute-start.67) | collective-permute-done | bytes 65568 | tf_op jit(solution)/shard_map/ppermute | solution.py:302
  196.5 2.2 %inner_product.1 = f32[128,128]{1,0:T(8,128)S(1)} custom-call(s32[8]{0:T(128)S(1)} %pad_add_fusion.4.columns, s32[1]{0:T(128)} %bitcast.6.place, f32[512,128]{1,0:T(8,128)S(1)} %get-tuple-element.78.refs_0_, f32[512,128]{1,0:T(8,128)S(1)} %get-tuple-element.79.refs_1_, f32[512,128]{1,0:T(8,128)S(1)} %collective-permute-done.72.refs_2_, ...), custom_call_target="tpu_custom_call" | custom-call | flops 402653184 | bytes 2097188 | tf_op jit(solution)/shard_map/inner_product/pallas_call | solution.py:20
  200.5 2.5 %collective-permute-done.76 = f32[128,128]{1,0:T(8,128)S(1)} collective-permute-done((f32[128,128]{1,0:T(8,128)S(1)}, f32[128,128]{1,0:T(8,128)S(1)}, u32[]{:S(2)}, u32[]{:S(2)}) %collective-permute-start.76) | collective-permute-done | bytes 65568 | tf_op jit(solution)/shard_map/ppermute | solution.py:302
  203.8 2.6 %collective-permute-done.70 = f32[128,128]{1,0:T(8,128)S(1)} collective-permute-done((f32[128,128]{1,0:T(8,128)S(1)}, f32[128,128]{1,0:T(8,128)S(1)}, u32[]{:S(2)}, u32[]{:S(2)}) %collective-permute-start.70) | collective-permute-done | bytes 65568 | tf_op jit(solution)/shard_map/ppermute | solution.py:302
  207.9 2.9 %collective-permute-done.71 = f32[128,128]{1,0:T(8,128)S(1)} collective-permute-done((f32[128,128]{1,0:T(8,128)S(1)}, f32[128,128]{1,0:T(8,128)S(1)}, u32[]{:S(2)}, u32[]{:S(2)}) %collective-permute-start.71) | collective-permute-done | bytes 65568 | tf_op jit(solution)/shard_map/ppermute | solution.py:302
  210.7 6.1 %factor_and_basis.1 = (f32[2048,128]{1,0:T(8,128)}, f32[128,128]{1,0:T(8,128)S(1)}) custom-call(f32[128,128]{1,0:T(8,128)S(1)} %add.36.gram, f32[2048,128]{1,0:T(8,128)S(1)} %get-tuple-element.81.following), custom_call_target="tpu_custom_call" | custom-call | flops 402653184 | bytes 1114112 | tf_op jit(solution)/shard_map/factor_and_basis/pallas_call | solution.py:20
  (189 shorter events, 109.7 us)
Async XLA Ops:
  27.0 11.1 %collective-permute-start.10 = (f32[512,128]{1,0:T(8,128)S(1)}, f32[512,128]{1,0:T(8,128)S(1)}, u32[]{:S(2)}, u32[]{:S(2)}) collective-permute-start(f32[512,128]{1,0:T(8,128)S(1)} %pick_rows.21), channel_id=1, source_target_pairs={{0,1},{2,0},{4,2},{6,4},{7,6},{5,7},{3,5},{1,3},{8,9},{10,8},{12,1... | collective-permute-start | bytes 786440 | tf_op jit(solution)/shard_map/ppermute | solution.py:293
  29.5 11.2 %collective-permute-start.4 = (f32[512,128]{1,0:T(8,128)S(1)}, f32[512,128]{1,0:T(8,128)S(1)}, u32[]{:S(2)}, u32[]{:S(2)}) collective-permute-start(f32[512,128]{1,0:T(8,128)S(1)} %pick_rows.17), channel_id=1, source_target_pairs={{0,2},{2,4},{4,6},{6,7},{7,5},{5,3},{3,1},{1,0},{8,10},{10,12},{12... | collective-permute-start | bytes 786440 | tf_op jit(solution)/shard_map/ppermute | solution.py:293
  33.1 11.4 %collective-permute-start.19 = (f32[512,128]{1,0:T(8,128)S(1)}, f32[512,128]{1,0:T(8,128)S(1)}, u32[]{:S(2)}, u32[]{:S(2)}) collective-permute-start(f32[512,128]{1,0:T(8,128)S(1)} %pick_rows.30), channel_id=1, source_target_pairs={{0,1},{2,0},{4,2},{6,4},{7,6},{5,7},{3,5},{1,3},{8,9},{10,8},{12,1... | collective-permute-start | bytes 786440 | tf_op jit(solution)/shard_map/ppermute | solution.py:293
  35.6 11.1 %collective-permute-start.15 = (f32[512,128]{1,0:T(8,128)S(1)}, f32[512,128]{1,0:T(8,128)S(1)}, u32[]{:S(2)}, u32[]{:S(2)}) collective-permute-start(f32[512,128]{1,0:T(8,128)S(1)} %pick_rows.26), channel_id=1, source_target_pairs={{0,2},{2,4},{4,6},{6,7},{7,5},{5,3},{3,1},{1,0},{8,10},{10,12},{12... | collective-permute-start | bytes 786440 | tf_op jit(solution)/shard_map/ppermute | solution.py:293
  48.6 10.7 %collective-permute-start.12 = (f32[512,128]{1,0:T(8,128)S(1)}, f32[512,128]{1,0:T(8,128)S(1)}, u32[]{:S(2)}, u32[]{:S(2)}) collective-permute-start(f32[512,128]{1,0:T(8,128)S(1)} %pick_rows.23), channel_id=1, source_target_pairs={{0,1},{2,0},{4,2},{6,4},{7,6},{5,7},{3,5},{1,3},{8,9},{10,8},{12,1... | collective-permute-start | bytes 786440 | tf_op jit(solution)/shard_map/ppermute | solution.py:293
  50.7 10.4 %collective-permute-start.8 = (f32[512,128]{1,0:T(8,128)S(1)}, f32[512,128]{1,0:T(8,128)S(1)}, u32[]{:S(2)}, u32[]{:S(2)}) collective-permute-start(f32[512,128]{1,0:T(8,128)S(1)} %pick_rows.19), channel_id=1, source_target_pairs={{0,2},{2,4},{4,6},{6,7},{7,5},{5,3},{3,1},{1,0},{8,10},{10,12},{12... | collective-permute-start | bytes 786440 | tf_op jit(solution)/shard_map/ppermute | solution.py:293
  75.9 11.5 %collective-permute-start.30 = (f32[512,128]{1,0:T(8,128)S(1)}, f32[512,128]{1,0:T(8,128)S(1)}, u32[]{:S(2)}, u32[]{:S(2)}) collective-permute-start(f32[512,128]{1,0:T(8,128)S(1)} %column_product.5.refs_5_.refs_0_), channel_id=1, source_target_pairs={{0,1},{2,0},{4,2},{6,4},{7,6},{5,7},{3,5},{1,3},{8,9},{10,8},{12,1... | collective-permute-start | bytes 786440 | tf_op jit(solution)/shard_map/ppermute | solution.py:293
  77.6 11.4 %collective-permute-start.29 = (f32[512,128]{1,0:T(8,128)S(1)}, f32[512,128]{1,0:T(8,128)S(1)}, u32[]{:S(2)}, u32[]{:S(2)}) collective-permute-start(f32[512,128]{1,0:T(8,128)S(1)} %column_product.5.refs_5_.refs_0_), channel_id=1, source_target_pairs={{0,2},{2,4},{4,6},{6,7},{7,5},{5,3},{3,1},{1,0},{8,10},{10,12},{12... | collective-permute-start | bytes 786440 | tf_op jit(solution)/shard_map/ppermute | solution.py:293
  81.8 11.2 %collective-permute-start.32 = (f32[512,128]{1,0:T(8,128)S(1)}, f32[512,128]{1,0:T(8,128)S(1)}, u32[]{:S(2)}, u32[]{:S(2)}) collective-permute-start(f32[512,128]{1,0:T(8,128)S(1)} %collective-permute-done.28.refs_9_), channel_id=1, source_target_pairs={{0,1},{2,0},{4,2},{6,4},{7,6},{5,7},{3,5},{1,3},{8,9},{10,8},{12,1... | collective-permute-start | bytes 786440 | tf_op jit(solution)/shard_map/ppermute | solution.py:293
  83.4 11.2 %collective-permute-start.31 = (f32[512,128]{1,0:T(8,128)S(1)}, f32[512,128]{1,0:T(8,128)S(1)}, u32[]{:S(2)}, u32[]{:S(2)}) collective-permute-start(f32[512,128]{1,0:T(8,128)S(1)} %collective-permute-done.27.refs_8_), channel_id=1, source_target_pairs={{0,2},{2,4},{4,6},{6,7},{7,5},{5,3},{3,1},{1,0},{8,10},{10,12},{12... | collective-permute-start | bytes 786440 | tf_op jit(solution)/shard_map/ppermute | solution.py:293
  87.4 11.2 %collective-permute-start.34 = (f32[512,128]{1,0:T(8,128)S(1)}, f32[512,128]{1,0:T(8,128)S(1)}, u32[]{:S(2)}, u32[]{:S(2)}) collective-permute-start(f32[512,128]{1,0:T(8,128)S(1)} %collective-permute-done.30.refs_11_), channel_id=1, source_target_pairs={{0,1},{2,0},{4,2},{6,4},{7,6},{5,7},{3,5},{1,3},{8,9},{10,8},{12,1... | collective-permute-start | bytes 786440 | tf_op jit(solution)/shard_map/ppermute | solution.py:293
  89.0 11.2 %collective-permute-start.33 = (f32[512,128]{1,0:T(8,128)S(1)}, f32[512,128]{1,0:T(8,128)S(1)}, u32[]{:S(2)}, u32[]{:S(2)}) collective-permute-start(f32[512,128]{1,0:T(8,128)S(1)} %collective-permute-done.29.refs_10_), channel_id=1, source_target_pairs={{0,2},{2,4},{4,6},{6,7},{7,5},{5,3},{3,1},{1,0},{8,10},{10,12},{12... | collective-permute-start | bytes 786440 | tf_op jit(solution)/shard_map/ppermute | solution.py:293
  93.0 11.2 %collective-permute-start.36 = (f32[512,128]{1,0:T(8,128)S(1)}, f32[512,128]{1,0:T(8,128)S(1)}, u32[]{:S(2)}, u32[]{:S(2)}) collective-permute-start(f32[512,128]{1,0:T(8,128)S(1)} %collective-permute-done.32.refs_13_), channel_id=1, source_target_pairs={{0,1},{2,0},{4,2},{6,4},{7,6},{5,7},{3,5},{1,3},{8,9},{10,8},{12,1... | collective-permute-start | bytes 786440 | tf_op jit(solution)/shard_map/ppermute | solution.py:293
  94.7 11.3 %collective-permute-start.35 = (f32[512,128]{1,0:T(8,128)S(1)}, f32[512,128]{1,0:T(8,128)S(1)}, u32[]{:S(2)}, u32[]{:S(2)}) collective-permute-start(f32[512,128]{1,0:T(8,128)S(1)} %collective-permute-done.31.refs_12_), channel_id=1, source_target_pairs={{0,2},{2,4},{4,6},{6,7},{7,5},{5,3},{3,1},{1,0},{8,10},{10,12},{12... | collective-permute-start | bytes 786440 | tf_op jit(solution)/shard_map/ppermute | solution.py:293
  98.6 11.2 %collective-permute-start.38 = (f32[512,128]{1,0:T(8,128)S(1)}, f32[512,128]{1,0:T(8,128)S(1)}, u32[]{:S(2)}, u32[]{:S(2)}) collective-permute-start(f32[512,128]{1,0:T(8,128)S(1)} %collective-permute-done.34.refs_15_), channel_id=1, source_target_pairs={{0,1},{2,0},{4,2},{6,4},{7,6},{5,7},{3,5},{1,3},{8,9},{10,8},{12,1... | collective-permute-start | bytes 786440 | tf_op jit(solution)/shard_map/ppermute | solution.py:293
  100.3 11.3 %collective-permute-start.37 = (f32[512,128]{1,0:T(8,128)S(1)}, f32[512,128]{1,0:T(8,128)S(1)}, u32[]{:S(2)}, u32[]{:S(2)}) collective-permute-start(f32[512,128]{1,0:T(8,128)S(1)} %collective-permute-done.33.refs_14_), channel_id=1, source_target_pairs={{0,2},{2,4},{4,6},{6,7},{7,5},{5,3},{3,1},{1,0},{8,10},{10,12},{12... | collective-permute-start | bytes 786440 | tf_op jit(solution)/shard_map/ppermute | solution.py:293
  119.3 11.6 %collective-permute-start.46 = (f32[512,128]{1,0:T(8,128)S(1)}, f32[512,128]{1,0:T(8,128)S(1)}, u32[]{:S(2)}, u32[]{:S(2)}) collective-permute-start(f32[512,128]{1,0:T(8,128)S(1)} %get-tuple-element.73.refs_2_.refs_1_), channel_id=1, source_target_pairs={{0,16},{8,24},{16,0},{24,8},{1,17},{9,25},{17,1},{25,9},{2,18},{10... | collective-permute-start | bytes 786440 | tf_op jit(solution)/shard_map/ppermute | solution.py:302
  120.8 10.2 %collective-permute-start.43 = (f32[512,128]{1,0:T(8,128)S(1)}, f32[512,128]{1,0:T(8,128)S(1)}, u32[]{:S(2)}, u32[]{:S(2)}) collective-permute-start(f32[512,128]{1,0:T(8,128)S(1)} %get-tuple-element.72.refs_1_.refs_2_), channel_id=1, source_target_pairs={{0,8},{8,0},{16,24},{24,16},{1,9},{9,1},{17,25},{25,17},{2,10},{10... | collective-permute-start | bytes 786440 | tf_op jit(solution)/shard_map/ppermute | solution.py:302
  120.8 10.2 %collective-permute-start.44 = (f32[512,128]{1,0:T(8,128)S(1)}, f32[512,128]{1,0:T(8,128)S(1)}, u32[]{:S(2)}, u32[]{:S(2)}) collective-permute-start(f32[512,128]{1,0:T(8,128)S(1)} %get-tuple-element.73.refs_2_.refs_1_), channel_id=1, source_target_pairs={{0,8},{8,0},{16,24},{24,16},{1,9},{9,1},{17,25},{25,17},{2,10},{10... | collective-permute-start | bytes 786440 | tf_op jit(solution)/shard_map/ppermute | solution.py:302
  137.3 11.5 %collective-permute-start.52 = (f32[512,128]{1,0:T(8,128)S(1)}, f32[512,128]{1,0:T(8,128)S(1)}, u32[]{:S(2)}, u32[]{:S(2)}) collective-permute-start(f32[512,128]{1,0:T(8,128)S(1)} %column_product.7.refs_1_.refs_5_), channel_id=1, source_target_pairs={{0,1},{2,0},{4,2},{6,4},{7,6},{5,7},{3,5},{1,3},{8,9},{10,8},{12,1... | collective-permute-start | bytes 786440 | tf_op jit(solution)/shard_map/ppermute | solution.py:293
  139.1 11.5 %collective-permute-start.51 = (f32[512,128]{1,0:T(8,128)S(1)}, f32[512,128]{1,0:T(8,128)S(1)}, u32[]{:S(2)}, u32[]{:S(2)}) collective-permute-start(f32[512,128]{1,0:T(8,128)S(1)} %column_product.7.refs_1_.refs_5_), channel_id=1, source_target_pairs={{0,2},{2,4},{4,6},{6,7},{7,5},{5,3},{3,1},{1,0},{8,10},{10,12},{12... | collective-permute-start | bytes 786440 | tf_op jit(solution)/shard_map/ppermute | solution.py:293
  143.1 11.2 %collective-permute-start.54 = (f32[512,128]{1,0:T(8,128)S(1)}, f32[512,128]{1,0:T(8,128)S(1)}, u32[]{:S(2)}, u32[]{:S(2)}) collective-permute-start(f32[512,128]{1,0:T(8,128)S(1)} %collective-permute-done.50.refs_3_.refs_9_), channel_id=1, source_target_pairs={{0,1},{2,0},{4,2},{6,4},{7,6},{5,7},{3,5},{1,3},{8,9},{10,8},{12,1... | collective-permute-start | bytes 786440 | tf_op jit(solution)/shard_map/ppermute | solution.py:293
  144.9 11.2 %collective-permute-start.53 = (f32[512,128]{1,0:T(8,128)S(1)}, f32[512,128]{1,0:T(8,128)S(1)}, u32[]{:S(2)}, u32[]{:S(2)}) collective-permute-start(f32[512,128]{1,0:T(8,128)S(1)} %collective-permute-done.49.refs_2_.refs_8_), channel_id=1, source_target_pairs={{0,2},{2,4},{4,6},{6,7},{7,5},{5,3},{3,1},{1,0},{8,10},{10,12},{12... | collective-permute-start | bytes 786440 | tf_op jit(solution)/shard_map/ppermute | solution.py:293
  148.8 11.2 %collective-permute-start.56 = (f32[512,128]{1,0:T(8,128)S(1)}, f32[512,128]{1,0:T(8,128)S(1)}, u32[]{:S(2)}, u32[]{:S(2)}) collective-permute-start(f32[512,128]{1,0:T(8,128)S(1)} %collective-permute-done.52.refs_5_.refs_11_), channel_id=1, source_target_pairs={{0,1},{2,0},{4,2},{6,4},{7,6},{5,7},{3,5},{1,3},{8,9},{10,8},{12,1... | collective-permute-start | bytes 786440 | tf_op jit(solution)/shard_map/ppermute | solution.py:293
  150.5 11.2 %collective-permute-start.55 = (f32[512,128]{1,0:T(8,128)S(1)}, f32[512,128]{1,0:T(8,128)S(1)}, u32[]{:S(2)}, u32[]{:S(2)}) collective-permute-start(f32[512,128]{1,0:T(8,128)S(1)} %collective-permute-done.51.refs_4_.refs_10_), channel_id=1, source_target_pairs={{0,2},{2,4},{4,6},{6,7},{7,5},{5,3},{3,1},{1,0},{8,10},{10,12},{12... | collective-permute-start | bytes 786440 | tf_op jit(solution)/shard_map/ppermute | solution.py:293
  154.4 11.2 %collective-permute-start.58 = (f32[512,128]{1,0:T(8,128)S(1)}, f32[512,128]{1,0:T(8,128)S(1)}, u32[]{:S(2)}, u32[]{:S(2)}) collective-permute-start(f32[512,128]{1,0:T(8,128)S(1)} %collective-permute-done.54.refs_7_.refs_13_), channel_id=1, source_target_pairs={{0,1},{2,0},{4,2},{6,4},{7,6},{5,7},{3,5},{1,3},{8,9},{10,8},{12,1... | collective-permute-start | bytes 786440 | tf_op jit(solution)/shard_map/ppermute | solution.py:293
  156.1 11.3 %collective-permute-start.57 = (f32[512,128]{1,0:T(8,128)S(1)}, f32[512,128]{1,0:T(8,128)S(1)}, u32[]{:S(2)}, u32[]{:S(2)}) collective-permute-start(f32[512,128]{1,0:T(8,128)S(1)} %collective-permute-done.53.refs_6_.refs_12_), channel_id=1, source_target_pairs={{0,2},{2,4},{4,6},{6,7},{7,5},{5,3},{3,1},{1,0},{8,10},{10,12},{12... | collective-permute-start | bytes 786440 | tf_op jit(solution)/shard_map/ppermute | solution.py:293
  160.0 11.2 %collective-permute-start.60 = (f32[512,128]{1,0:T(8,128)S(1)}, f32[512,128]{1,0:T(8,128)S(1)}, u32[]{:S(2)}, u32[]{:S(2)}) collective-permute-start(f32[512,128]{1,0:T(8,128)S(1)} %collective-permute-done.56.refs_9_.refs_15_), channel_id=1, source_target_pairs={{0,1},{2,0},{4,2},{6,4},{7,6},{5,7},{3,5},{1,3},{8,9},{10,8},{12,1... | collective-permute-start | bytes 786440 | tf_op jit(solution)/shard_map/ppermute | solution.py:293
  161.8 11.3 %collective-permute-start.59 = (f32[512,128]{1,0:T(8,128)S(1)}, f32[512,128]{1,0:T(8,128)S(1)}, u32[]{:S(2)}, u32[]{:S(2)}) collective-permute-start(f32[512,128]{1,0:T(8,128)S(1)} %collective-permute-done.55.refs_8_.refs_14_), channel_id=1, source_target_pairs={{0,2},{2,4},{4,6},{6,7},{7,5},{5,3},{3,1},{1,0},{8,10},{10,12},{12... | collective-permute-start | bytes 786440 | tf_op jit(solution)/shard_map/ppermute | solution.py:293
  182.4 12.1 %collective-permute-start.68 = (f32[512,128]{1,0:T(8,128)S(1)}, f32[512,128]{1,0:T(8,128)S(1)}, u32[]{:S(2)}, u32[]{:S(2)}) collective-permute-start(f32[512,128]{1,0:T(8,128)S(1)} %get-tuple-element.78.refs_0_), channel_id=1, source_target_pairs={{0,16},{8,24},{16,0},{24,8},{1,17},{9,25},{17,1},{25,9},{2,18},{10... | collective-permute-start | bytes 786440 | tf_op jit(solution)/shard_map/ppermute | solution.py:302
  182.9 11.6 %collective-permute-start.69 = (f32[512,128]{1,0:T(8,128)S(1)}, f32[512,128]{1,0:T(8,128)S(1)}, u32[]{:S(2)}, u32[]{:S(2)}) collective-permute-start(f32[512,128]{1,0:T(8,128)S(1)} %get-tuple-element.79.refs_1_), channel_id=1, source_target_pairs={{0,16},{8,24},{16,0},{24,8},{1,17},{9,25},{17,1},{25,9},{2,18},{10... | collective-permute-start | bytes 786440 | tf_op jit(solution)/shard_map/ppermute | solution.py:302
  207.4 9.4 %collective-permute-start.78 = (f32[128,128]{1,0:T(8,128)S(1)}, f32[128,128]{1,0:T(8,128)S(1)}, u32[]{:S(2)}, u32[]{:S(2)}) collective-permute-start(f32[128,128]{1,0:T(8,128)S(1)} %add.38), channel_id=1, source_target_pairs={{0,4},{1,5},{2,6},{3,7},{4,0},{5,1},{6,2},{7,3},{8,12},{9,13},{10,... | collective-permute-start | bytes 196616 | tf_op jit(solution)/shard_map/ppermute | solution.py:302
  (51 other events, 306.6 us)

commit v3 on v2

--- a/solution.py
+++ b/solution.py
@@ -58,8 +58,7 @@
 
 
 def table_row(table, places, entry, slots, slot):
-    place = places[entry]
-    return jnp.where(place >= 0, table[jnp.maximum(place, 0) * slots + slot], -1)
+    return table[places[entry] * slots + slot]
 
 
 def pick(row, held, first_unit, unit, per_block, out, begin, base):
@@ -228,7 +227,7 @@
     out[...] = self_product(total[...])
 
 
-def factor_kernel(gram, following, basis_out, inverse_out):
+def factor_kernel(gram, inverse_out):
     order = gram.shape[0]
     blocks = order // PANEL
     shape = (PANEL, order)
@@ -262,8 +261,11 @@
                 left[i] = left[i] - factor[i] * left_row
                 right[i] = right[i] - factor[i] * right_row
         inverse_out[b * PANEL : (b + 1) * PANEL, :] = right[b] * scale
-    basis_out[...] = lax.dot_general(
-        following[...], inverse_out[...], (((1,), (1,)), ((), ())), precision=HIGHEST, preferred_element_type=jnp.float32
+
+
+def basis_kernel(following, inverse, out):
+    out[...] = lax.dot_general(
+        following[...], inverse[...], (((1,), (1,)), ((), ())), precision=HIGHEST, preferred_element_type=jnp.float32
     )
 
 
@@ -465,13 +467,13 @@
             flops=6 * held_rows * vec * vec,
             name="owner_rows",
         )
-        gram_matrix, gs = tie((gram_matrix, gs))
         ps = list(row_step(True, gs, pieces, got, xs))
+        across = [flip(p, "row", row_bits[-1]) for p in ps]
         gram_matrix = sum_over(gram_matrix, "row", row_bits[:-1])
-        across = [flip(p, "row", row_bits[-1]) for p in ps]
-        gram_matrix = sum_over(gram_matrix, "col", col_bits[:2])
+        gram_matrix = sum_over(gram_matrix, "col", col_bits[0:1])
         gram_matrix, across = tie((gram_matrix, across))
         images = gather_rest(ps, across)
+        gram_matrix = sum_over(gram_matrix, "col", col_bits[1:2])
         gram_matrix = sum_over(gram_matrix, "col", col_bits[2:])
         gram_matrix = sum_over(gram_matrix, "row", row_bits[-1:])
         inner_local = call(
@@ -488,14 +490,15 @@
             name="inner_product",
         )
         inner_matrix = sum_over(inner_local, "col", col_bits)
-        basis_block, inverse = call(
-            factor_kernel,
-            [jax.ShapeDtypeStruct(start_block.shape, jnp.float32), square],
+        inverse = call(factor_kernel, square, [VMEM], VMEM, [gram_matrix], flops=4 * vec**3, name="factor")
+        basis_block = call(
+            basis_kernel,
+            jax.ShapeDtypeStruct(start_block.shape, jnp.float32),
             [VMEM] * 2,
-            [VMEM] * 2,
-            [gram_matrix, following],
+            VMEM,
+            [following, inverse],
             flops=12 * held_rows * vec * vec,
-            name="factor_and_basis",
+            name="basis",
         )
         projected = call(project_kernel, square, [VMEM] * 2, VMEM, [inverse, inner_matrix], name="project")
         return (basis_block, projected)

time: 218 us -> 216 us (level)
  waiting for transfers between devices: 105 us -> 102 us
    ppermute x31, waiting for transfers between devices: 39 us -> 36.7 us  [flip(): return lax.ppermute(value, axis, [(i, i ^ bit) for i in range(size)])]
    pallas_call x29 -> x30, Pallas kernels: 33.8 us -> 33.8 us  [call(): pl.pallas_call(kernel, out_shape=out_shape, in_specs=in_specs, out_specs=...]
  transfers between devices with their start and end apart: 79 -> 79, of which waited for: 45 -> 45; matrix products, arithmetic and copies ran while one was open for 0% -> 1% of each run, Pallas kernels for 10% -> 12%
where the time goes in v3:
time: 216 us
  waiting for transfers between devices  102 us (47%)
  starting transfers between devices  73.2 us (34%)
  Pallas kernels  33.8 us (16%)
  between operations  3.01 us (1%)
    ppermute x48, waiting for transfers between devices, forward(): lax.ppermute(value, 'col', [(col, ring[(k + step) % n_col]) for k, col in...  65.7 us
    ppermute x48, starting transfers between devices, forward(): lax.ppermute(value, 'col', [(col, ring[(k + step) % n_col]) for k, col in...  50.1 us
    ppermute x31, waiting for transfers between devices, flip(): return lax.ppermute(value, axis, [(i, i ^ bit) for i in range(size)])  36.7 us
    pallas_call x30, Pallas kernels, call(): pl.pallas_call(kernel, out_shape=out_shape, in_specs=in_specs, out_specs=...  33.8 us
    ppermute x31, starting transfers between devices, flip(): return lax.ppermute(value, axis, [(i, i ^ bit) for i in range(size)])  23.1 us
  transfers between devices with their start and end apart: 79, of which 45 were waited for; matrix products, arithmetic and copies ran while one was open for 1% of the time, Pallas kernels for 12%

profile of v3, /device:TPU:0, one launch (start us, length us, event | category | flops | bytes accessed | tf_op | source)
XLA Modules:
  0.0 215.6 jit_solution(11249507701682296047)
XLA Ops:
  1.9 3.0 %collective-permute-start = (s32[2]{0:T(128)S(1)}, s32[2]{0:T(128)S(1)}, u32[]{:S(2)}, u32[]{:S(2)}) collective-permute-start(s32[2]{0:T(128)S(1)} %compare_select_fusion.1), channel_id=1, source_target_pairs={{0,1},{1,0},{2,3},{3,2},{4,5},{5,4},{6,7},{7,6},{8,9},{9,8},{10,11... | collective-permute-start | bytes 32 | tf_op jit(solution)/shard_map/tables/ppermute | solution.py:304
  6.5 2.1 collective-permute-start.1
  10.2 3.0 %collective-permute-start.2 = (s32[8]{0:T(128)S(1)}, s32[8]{0:T(128)S(1)}, u32[]{:S(2)}, u32[]{:S(2)}) collective-permute-start(s32[8]{0:T(128)S(1)} %pad_add_fusion.1), channel_id=1, source_target_pairs={{0,4},{1,5},{2,6},{3,7},{4,0},{5,1},{6,2},{7,3},{8,12},{9,13},{10,... | collective-permute-start | bytes 104 | tf_op jit(solution)/shard_map/tables/ppermute | solution.py:304
  29.7 2.8 %collective-permute-done.18.refs_0_ = f32[512,128]{1,0:T(8,128)S(1)} collective-permute-done((f32[512,128]{1,0:T(8,128)S(1)}, f32[512,128]{1,0:T(8,128)S(1)}, u32[]{:S(2)}, u32[]{:S(2)}) %collective-permute-start.18) | collective-permute-done | bytes 262176 | tf_op jit(solution)/shard_map/ppermute | solution.py:295
  35.8 2.3 %collective-permute-done.10.refs_0_ = f32[512,128]{1,0:T(8,128)S(1)} collective-permute-done((f32[512,128]{1,0:T(8,128)S(1)}, f32[512,128]{1,0:T(8,128)S(1)}, u32[]{:S(2)}, u32[]{:S(2)}) %collective-permute-start.10) | collective-permute-done | bytes 262176 | tf_op jit(solution)/shard_map/ppermute | solution.py:295
  51.3 3.1 %collective-permute-done.20.refs_1_ = f32[512,128]{1,0:T(8,128)S(1)} collective-permute-done((f32[512,128]{1,0:T(8,128)S(1)}, f32[512,128]{1,0:T(8,128)S(1)}, u32[]{:S(2)}, u32[]{:S(2)}) %collective-permute-start.20) | collective-permute-done | bytes 262176 | tf_op jit(solution)/shard_map/ppermute | solution.py:295
  54.4 2.2 %collective-permute-done.16.refs_0_ = f32[512,128]{1,0:T(8,128)S(1)} collective-permute-done((f32[512,128]{1,0:T(8,128)S(1)}, f32[512,128]{1,0:T(8,128)S(1)}, u32[]{:S(2)}, u32[]{:S(2)}) %collective-permute-start.16) | collective-permute-done | bytes 262176 | tf_op jit(solution)/shard_map/ppermute | solution.py:295
  64.2 5.5 %collective-permute-done.23.refs_4_ = f32[512,128]{1,0:T(8,128)S(1)} collective-permute-done((f32[512,128]{1,0:T(8,128)S(1)}, f32[512,128]{1,0:T(8,128)S(1)}, u32[]{:S(2)}, u32[]{:S(2)}) %collective-permute-start.23) | collective-permute-done | bytes 262176 | tf_op jit(solution)/shard_map/ppermute | solution.py:304
  78.0 3.7 %collective-permute-done.28.refs_9_ = f32[512,128]{1,0:T(8,128)S(1)} collective-permute-done((f32[512,128]{1,0:T(8,128)S(1)}, f32[512,128]{1,0:T(8,128)S(1)}, u32[]{:S(2)}, u32[]{:S(2)}) %collective-permute-start.28) | collective-permute-done | bytes 262176 | tf_op jit(solution)/shard_map/ppermute | solution.py:295
  83.8 3.6 %collective-permute-done.30.refs_11_ = f32[512,128]{1,0:T(8,128)S(1)} collective-permute-done((f32[512,128]{1,0:T(8,128)S(1)}, f32[512,128]{1,0:T(8,128)S(1)}, u32[]{:S(2)}, u32[]{:S(2)}) %collective-permute-start.30) | collective-permute-done | bytes 262176 | tf_op jit(solution)/shard_map/ppermute | solution.py:295
  89.4 3.6 %collective-permute-done.32.refs_13_ = f32[512,128]{1,0:T(8,128)S(1)} collective-permute-done((f32[512,128]{1,0:T(8,128)S(1)}, f32[512,128]{1,0:T(8,128)S(1)}, u32[]{:S(2)}, u32[]{:S(2)}) %collective-permute-start.32) | collective-permute-done | bytes 262176 | tf_op jit(solution)/shard_map/ppermute | solution.py:295
  95.0 3.6 %collective-permute-done.34.refs_15_ = f32[512,128]{1,0:T(8,128)S(1)} collective-permute-done((f32[512,128]{1,0:T(8,128)S(1)}, f32[512,128]{1,0:T(8,128)S(1)}, u32[]{:S(2)}, u32[]{:S(2)}) %collective-permute-start.34) | collective-permute-done | bytes 262176 | tf_op jit(solution)/shard_map/ppermute | solution.py:295
  100.6 3.6 %collective-permute-done.36.refs_17_ = f32[512,128]{1,0:T(8,128)S(1)} collective-permute-done((f32[512,128]{1,0:T(8,128)S(1)}, f32[512,128]{1,0:T(8,128)S(1)}, u32[]{:S(2)}, u32[]{:S(2)}) %collective-permute-start.36) | collective-permute-done | bytes 262176 | tf_op jit(solution)/shard_map/ppermute | solution.py:295
  106.4 3.5 %collective-permute-done.38.refs_19_ = f32[512,128]{1,0:T(8,128)S(1)} collective-permute-done((f32[512,128]{1,0:T(8,128)S(1)}, f32[512,128]{1,0:T(8,128)S(1)}, u32[]{:S(2)}, u32[]{:S(2)}) %collective-permute-start.38) | collective-permute-done | bytes 262176 | tf_op jit(solution)/shard_map/ppermute | solution.py:295
  116.5 2.2 %row_product.2 = (f32[512,128]{1,0:T(8,128)S(1)}, f32[512,128]{1,0:T(8,128)S(1)}) custom-call(s32[16]{0:T(128)S(1)} %pad_add_fusion.2.table, s32[10]{0:T(128)S(1)} %constant_dynamic-update-slice_fusion.places, f32[2]{0:T(128)S(1)} %pad_maximum_fusion.scalars, bf16[512,512]{1,0:T(8,128)(2,1)S(1)} %get-tuple-element.56.high_t.refs_0_, ...), custom_call_target="tpu_custom_call" | custom-call | flops 402653184 | bytes 6815856 | tf_op jit(solution)/shard_map/row_product/pallas_call | solution.py:20
  121.3 6.7 %collective-permute-done.45.refs_5_ = f32[512,128]{1,0:T(8,128)S(1)} collective-permute-done((f32[512,128]{1,0:T(8,128)S(1)}, f32[512,128]{1,0:T(8,128)S(1)}, u32[]{:S(2)}, u32[]{:S(2)}) %collective-permute-start.45) | collective-permute-done | bytes 262176 | tf_op jit(solution)/shard_map/ppermute | solution.py:304
  128.0 3.1 %collective-permute-done.46.refs_6_ = f32[512,128]{1,0:T(8,128)S(1)} collective-permute-done((f32[512,128]{1,0:T(8,128)S(1)}, f32[512,128]{1,0:T(8,128)S(1)}, u32[]{:S(2)}, u32[]{:S(2)}) %collective-permute-start.46) | collective-permute-done | bytes 262176 | tf_op jit(solution)/shard_map/ppermute | solution.py:304
  139.5 3.7 %collective-permute-done.50.refs_3_.refs_9_ = f32[512,128]{1,0:T(8,128)S(1)} collective-permute-done((f32[512,128]{1,0:T(8,128)S(1)}, f32[512,128]{1,0:T(8,128)S(1)}, u32[]{:S(2)}, u32[]{:S(2)}) %collective-permute-start.50) | collective-permute-done | bytes 262176 | tf_op jit(solution)/shard_map/ppermute | solution.py:295
  145.3 3.6 %collective-permute-done.52.refs_5_.refs_11_ = f32[512,128]{1,0:T(8,128)S(1)} collective-permute-done((f32[512,128]{1,0:T(8,128)S(1)}, f32[512,128]{1,0:T(8,128)S(1)}, u32[]{:S(2)}, u32[]{:S(2)}) %collective-permute-start.52) | collective-permute-done | bytes 262176 | tf_op jit(solution)/shard_map/ppermute | solution.py:295
  151.0 3.6 %collective-permute-done.54.refs_7_.refs_13_ = f32[512,128]{1,0:T(8,128)S(1)} collective-permute-done((f32[512,128]{1,0:T(8,128)S(1)}, f32[512,128]{1,0:T(8,128)S(1)}, u32[]{:S(2)}, u32[]{:S(2)}) %collective-permute-start.54) | collective-permute-done | bytes 262176 | tf_op jit(solution)/shard_map/ppermute | solution.py:295
  156.6 3.6 %collective-permute-done.56.refs_9_.refs_15_ = f32[512,128]{1,0:T(8,128)S(1)} collective-permute-done((f32[512,128]{1,0:T(8,128)S(1)}, f32[512,128]{1,0:T(8,128)S(1)}, u32[]{:S(2)}, u32[]{:S(2)}) %collective-permute-start.56) | collective-permute-done | bytes 262176 | tf_op jit(solution)/shard_map/ppermute | solution.py:295
  162.2 3.6 %collective-permute-done.58.refs_11_.refs_17_ = f32[512,128]{1,0:T(8,128)S(1)} collective-permute-done((f32[512,128]{1,0:T(8,128)S(1)}, f32[512,128]{1,0:T(8,128)S(1)}, u32[]{:S(2)}, u32[]{:S(2)}) %collective-permute-start.58) | collective-permute-done | bytes 262176 | tf_op jit(solution)/shard_map/ppermute | solution.py:295
  167.9 3.5 %collective-permute-done.60.refs_13_.refs_19_ = f32[512,128]{1,0:T(8,128)S(1)} collective-permute-done((f32[512,128]{1,0:T(8,128)S(1)}, f32[512,128]{1,0:T(8,128)S(1)}, u32[]{:S(2)}, u32[]{:S(2)}) %collective-permute-start.60) | collective-permute-done | bytes 262176 | tf_op jit(solution)/shard_map/ppermute | solution.py:295
  177.9 2.2 %row_product.3 = (f32[512,128]{1,0:T(8,128)S(1)}, f32[512,128]{1,0:T(8,128)S(1)}) custom-call(s32[16]{0:T(128)S(1)} %pad_add_fusion.2.table, s32[10]{0:T(128)S(1)} %constant_dynamic-update-slice_fusion.places, f32[2]{0:T(128)S(1)} %pad_maximum_fusion.scalars, bf16[512,512]{1,0:T(8,128)(2,1)S(1)} %get-tuple-element.56.high_t.refs_0_, ...), custom_call_target="tpu_custom_call" | custom-call | flops 402653184 | bytes 6815856 | tf_op jit(solution)/shard_map/row_product/pallas_call | solution.py:20
  182.3 2.0 owner_rows.1
  185.6 2.0 collective-permute-start.66
  190.1 2.2 %collective-permute-done.68.refs_5_ = f32[512,128]{1,0:T(8,128)S(1)} collective-permute-done((f32[512,128]{1,0:T(8,128)S(1)}, f32[512,128]{1,0:T(8,128)S(1)}, u32[]{:S(2)}, u32[]{:S(2)}) %collective-permute-start.68) | collective-permute-done | bytes 262176 | tf_op jit(solution)/shard_map/ppermute | solution.py:304
  194.2 2.3 %inner_product.1 = f32[128,128]{1,0:T(8,128)S(1)} custom-call(s32[8]{0:T(128)S(1)} %pad_add_fusion.4.columns, s32[1]{0:T(128)} %bitcast.6.place, f32[512,128]{1,0:T(8,128)S(1)} %get-tuple-element.71.refs_0_, f32[512,128]{1,0:T(8,128)S(1)} %get-tuple-element.72.refs_1_, f32[512,128]{1,0:T(8,128)S(1)} %collective-permute-done.72.refs_2_, ...), custom_call_target="tpu_custom_call" | custom-call | flops 402653184 | bytes 2097188 | tf_op jit(solution)/shard_map/inner_product/pallas_call | solution.py:20
  198.2 2.6 %collective-permute-done.76 = f32[128,128]{1,0:T(8,128)S(1)} collective-permute-done((f32[128,128]{1,0:T(8,128)S(1)}, f32[128,128]{1,0:T(8,128)S(1)}, u32[]{:S(2)}, u32[]{:S(2)}) %collective-permute-start.76) | collective-permute-done | bytes 65568 | tf_op jit(solution)/shard_map/ppermute | solution.py:304
  201.5 2.7 %collective-permute-done.70 = f32[128,128]{1,0:T(8,128)S(1)} collective-permute-done((f32[128,128]{1,0:T(8,128)S(1)}, f32[128,128]{1,0:T(8,128)S(1)}, u32[]{:S(2)}, u32[]{:S(2)}) %collective-permute-start.70) | collective-permute-done | bytes 65568 | tf_op jit(solution)/shard_map/ppermute | solution.py:304
  205.5 3.0 %collective-permute-done.71 = f32[128,128]{1,0:T(8,128)S(1)} collective-permute-done((f32[128,128]{1,0:T(8,128)S(1)}, f32[128,128]{1,0:T(8,128)S(1)}, u32[]{:S(2)}, u32[]{:S(2)}) %collective-permute-start.71) | collective-permute-done | bytes 65568 | tf_op jit(solution)/shard_map/ppermute | solution.py:304
  208.5 4.0 %factor.1.inverse = f32[128,128]{1,0:T(8,128)S(1)} custom-call(f32[128,128]{1,0:T(8,128)S(1)} %add.36.gram), custom_call_target="tpu_custom_call" | custom-call | flops 8388608 | bytes 65536 | tf_op jit(solution)/shard_map/factor/pallas_call | solution.py:20
  (190 shorter events, 110.9 us)
Async XLA Ops:
  27.0 11.1 %collective-permute-start.10 = (f32[512,128]{1,0:T(8,128)S(1)}, f32[512,128]{1,0:T(8,128)S(1)}, u32[]{:S(2)}, u32[]{:S(2)}) collective-permute-start(f32[512,128]{1,0:T(8,128)S(1)} %pick_rows.21), channel_id=1, source_target_pairs={{0,1},{2,0},{4,2},{6,4},{7,6},{5,7},{3,5},{1,3},{8,9},{10,8},{12,1... | collective-permute-start | bytes 786440 | tf_op jit(solution)/shard_map/ppermute | solution.py:295
  29.5 11.2 %collective-permute-start.4 = (f32[512,128]{1,0:T(8,128)S(1)}, f32[512,128]{1,0:T(8,128)S(1)}, u32[]{:S(2)}, u32[]{:S(2)}) collective-permute-start(f32[512,128]{1,0:T(8,128)S(1)} %pick_rows.17), channel_id=1, source_target_pairs={{0,2},{2,4},{4,6},{6,7},{7,5},{5,3},{3,1},{1,0},{8,10},{10,12},{12... | collective-permute-start | bytes 786440 | tf_op jit(solution)/shard_map/ppermute | solution.py:295
  33.1 11.4 %collective-permute-start.19 = (f32[512,128]{1,0:T(8,128)S(1)}, f32[512,128]{1,0:T(8,128)S(1)}, u32[]{:S(2)}, u32[]{:S(2)}) collective-permute-start(f32[512,128]{1,0:T(8,128)S(1)} %pick_rows.30), channel_id=1, source_target_pairs={{0,1},{2,0},{4,2},{6,4},{7,6},{5,7},{3,5},{1,3},{8,9},{10,8},{12,1... | collective-permute-start | bytes 786440 | tf_op jit(solution)/shard_map/ppermute | solution.py:295
  35.6 11.1 %collective-permute-start.15 = (f32[512,128]{1,0:T(8,128)S(1)}, f32[512,128]{1,0:T(8,128)S(1)}, u32[]{:S(2)}, u32[]{:S(2)}) collective-permute-start(f32[512,128]{1,0:T(8,128)S(1)} %pick_rows.26), channel_id=1, source_target_pairs={{0,2},{2,4},{4,6},{6,7},{7,5},{5,3},{3,1},{1,0},{8,10},{10,12},{12... | collective-permute-start | bytes 786440 | tf_op jit(solution)/shard_map/ppermute | solution.py:295
  48.6 10.7 %collective-permute-start.12 = (f32[512,128]{1,0:T(8,128)S(1)}, f32[512,128]{1,0:T(8,128)S(1)}, u32[]{:S(2)}, u32[]{:S(2)}) collective-permute-start(f32[512,128]{1,0:T(8,128)S(1)} %pick_rows.23), channel_id=1, source_target_pairs={{0,1},{2,0},{4,2},{6,4},{7,6},{5,7},{3,5},{1,3},{8,9},{10,8},{12,1... | collective-permute-start | bytes 786440 | tf_op jit(solution)/shard_map/ppermute | solution.py:295
  50.7 10.4 %collective-permute-start.8 = (f32[512,128]{1,0:T(8,128)S(1)}, f32[512,128]{1,0:T(8,128)S(1)}, u32[]{:S(2)}, u32[]{:S(2)}) collective-permute-start(f32[512,128]{1,0:T(8,128)S(1)} %pick_rows.19), channel_id=1, source_target_pairs={{0,2},{2,4},{4,6},{6,7},{7,5},{5,3},{3,1},{1,0},{8,10},{10,12},{12... | collective-permute-start | bytes 786440 | tf_op jit(solution)/shard_map/ppermute | solution.py:295
  75.9 11.4 %collective-permute-start.30 = (f32[512,128]{1,0:T(8,128)S(1)}, f32[512,128]{1,0:T(8,128)S(1)}, u32[]{:S(2)}, u32[]{:S(2)}) collective-permute-start(f32[512,128]{1,0:T(8,128)S(1)} %column_product.5.refs_5_.refs_0_), channel_id=1, source_target_pairs={{0,1},{2,0},{4,2},{6,4},{7,6},{5,7},{3,5},{1,3},{8,9},{10,8},{12,1... | collective-permute-start | bytes 786440 | tf_op jit(solution)/shard_map/ppermute | solution.py:295
  77.5 11.4 %collective-permute-start.29 = (f32[512,128]{1,0:T(8,128)S(1)}, f32[512,128]{1,0:T(8,128)S(1)}, u32[]{:S(2)}, u32[]{:S(2)}) collective-permute-start(f32[512,128]{1,0:T(8,128)S(1)} %column_product.5.refs_5_.refs_0_), channel_id=1, source_target_pairs={{0,2},{2,4},{4,6},{6,7},{7,5},{5,3},{3,1},{1,0},{8,10},{10,12},{12... | collective-permute-start | bytes 786440 | tf_op jit(solution)/shard_map/ppermute | solution.py:295
  81.7 11.2 %collective-permute-start.32 = (f32[512,128]{1,0:T(8,128)S(1)}, f32[512,128]{1,0:T(8,128)S(1)}, u32[]{:S(2)}, u32[]{:S(2)}) collective-permute-start(f32[512,128]{1,0:T(8,128)S(1)} %collective-permute-done.28.refs_9_), channel_id=1, source_target_pairs={{0,1},{2,0},{4,2},{6,4},{7,6},{5,7},{3,5},{1,3},{8,9},{10,8},{12,1... | collective-permute-start | bytes 786440 | tf_op jit(solution)/shard_map/ppermute | solution.py:295
  83.3 11.2 %collective-permute-start.31 = (f32[512,128]{1,0:T(8,128)S(1)}, f32[512,128]{1,0:T(8,128)S(1)}, u32[]{:S(2)}, u32[]{:S(2)}) collective-permute-start(f32[512,128]{1,0:T(8,128)S(1)} %collective-permute-done.27.refs_8_), channel_id=1, source_target_pairs={{0,2},{2,4},{4,6},{6,7},{7,5},{5,3},{3,1},{1,0},{8,10},{10,12},{12... | collective-permute-start | bytes 786440 | tf_op jit(solution)/shard_map/ppermute | solution.py:295
  87.3 11.2 %collective-permute-start.34 = (f32[512,128]{1,0:T(8,128)S(1)}, f32[512,128]{1,0:T(8,128)S(1)}, u32[]{:S(2)}, u32[]{:S(2)}) collective-permute-start(f32[512,128]{1,0:T(8,128)S(1)} %collective-permute-done.30.refs_11_), channel_id=1, source_target_pairs={{0,1},{2,0},{4,2},{6,4},{7,6},{5,7},{3,5},{1,3},{8,9},{10,8},{12,1... | collective-permute-start | bytes 786440 | tf_op jit(solution)/shard_map/ppermute | solution.py:295
  89.0 11.2 %collective-permute-start.33 = (f32[512,128]{1,0:T(8,128)S(1)}, f32[512,128]{1,0:T(8,128)S(1)}, u32[]{:S(2)}, u32[]{:S(2)}) collective-permute-start(f32[512,128]{1,0:T(8,128)S(1)} %collective-permute-done.29.refs_10_), channel_id=1, source_target_pairs={{0,2},{2,4},{4,6},{6,7},{7,5},{5,3},{3,1},{1,0},{8,10},{10,12},{12... | collective-permute-start | bytes 786440 | tf_op jit(solution)/shard_map/ppermute | solution.py:295
  93.0 11.2 %collective-permute-start.36 = (f32[512,128]{1,0:T(8,128)S(1)}, f32[512,128]{1,0:T(8,128)S(1)}, u32[]{:S(2)}, u32[]{:S(2)}) collective-permute-start(f32[512,128]{1,0:T(8,128)S(1)} %collective-permute-done.32.refs_13_), channel_id=1, source_target_pairs={{0,1},{2,0},{4,2},{6,4},{7,6},{5,7},{3,5},{1,3},{8,9},{10,8},{12,1... | collective-permute-start | bytes 786440 | tf_op jit(solution)/shard_map/ppermute | solution.py:295
  94.6 11.3 %collective-permute-start.35 = (f32[512,128]{1,0:T(8,128)S(1)}, f32[512,128]{1,0:T(8,128)S(1)}, u32[]{:S(2)}, u32[]{:S(2)}) collective-permute-start(f32[512,128]{1,0:T(8,128)S(1)} %collective-permute-done.31.refs_12_), channel_id=1, source_target_pairs={{0,2},{2,4},{4,6},{6,7},{7,5},{5,3},{3,1},{1,0},{8,10},{10,12},{12... | collective-permute-start | bytes 786440 | tf_op jit(solution)/shard_map/ppermute | solution.py:295
  98.6 11.2 %collective-permute-start.38 = (f32[512,128]{1,0:T(8,128)S(1)}, f32[512,128]{1,0:T(8,128)S(1)}, u32[]{:S(2)}, u32[]{:S(2)}) collective-permute-start(f32[512,128]{1,0:T(8,128)S(1)} %collective-permute-done.34.refs_15_), channel_id=1, source_target_pairs={{0,1},{2,0},{4,2},{6,4},{7,6},{5,7},{3,5},{1,3},{8,9},{10,8},{12,1... | collective-permute-start | bytes 786440 | tf_op jit(solution)/shard_map/ppermute | solution.py:295
  100.2 11.3 %collective-permute-start.37 = (f32[512,128]{1,0:T(8,128)S(1)}, f32[512,128]{1,0:T(8,128)S(1)}, u32[]{:S(2)}, u32[]{:S(2)}) collective-permute-start(f32[512,128]{1,0:T(8,128)S(1)} %collective-permute-done.33.refs_14_), channel_id=1, source_target_pairs={{0,2},{2,4},{4,6},{6,7},{7,5},{5,3},{3,1},{1,0},{8,10},{10,12},{12... | collective-permute-start | bytes 786440 | tf_op jit(solution)/shard_map/ppermute | solution.py:295
  119.3 11.8 %collective-permute-start.46 = (f32[512,128]{1,0:T(8,128)S(1)}, f32[512,128]{1,0:T(8,128)S(1)}, u32[]{:S(2)}, u32[]{:S(2)}) collective-permute-start(f32[512,128]{1,0:T(8,128)S(1)} %get-tuple-element.68.refs_2_.refs_1_), channel_id=1, source_target_pairs={{0,16},{8,24},{16,0},{24,8},{1,17},{9,25},{17,1},{25,9},{2,18},{10... | collective-permute-start | bytes 786440 | tf_op jit(solution)/shard_map/ppermute | solution.py:304
  120.8 10.3 %collective-permute-start.43 = (f32[512,128]{1,0:T(8,128)S(1)}, f32[512,128]{1,0:T(8,128)S(1)}, u32[]{:S(2)}, u32[]{:S(2)}) collective-permute-start(f32[512,128]{1,0:T(8,128)S(1)} %get-tuple-element.67.refs_1_.refs_2_), channel_id=1, source_target_pairs={{0,8},{8,0},{16,24},{24,16},{1,9},{9,1},{17,25},{25,17},{2,10},{10... | collective-permute-start | bytes 786440 | tf_op jit(solution)/shard_map/ppermute | solution.py:304
  120.8 10.3 %collective-permute-start.44 = (f32[512,128]{1,0:T(8,128)S(1)}, f32[512,128]{1,0:T(8,128)S(1)}, u32[]{:S(2)}, u32[]{:S(2)}) collective-permute-start(f32[512,128]{1,0:T(8,128)S(1)} %get-tuple-element.68.refs_2_.refs_1_), channel_id=1, source_target_pairs={{0,8},{8,0},{16,24},{24,16},{1,9},{9,1},{17,25},{25,17},{2,10},{10... | collective-permute-start | bytes 786440 | tf_op jit(solution)/shard_map/ppermute | solution.py:304
  137.5 11.4 %collective-permute-start.52 = (f32[512,128]{1,0:T(8,128)S(1)}, f32[512,128]{1,0:T(8,128)S(1)}, u32[]{:S(2)}, u32[]{:S(2)}) collective-permute-start(f32[512,128]{1,0:T(8,128)S(1)} %column_product.7.refs_1_.refs_5_), channel_id=1, source_target_pairs={{0,1},{2,0},{4,2},{6,4},{7,6},{5,7},{3,5},{1,3},{8,9},{10,8},{12,1... | collective-permute-start | bytes 786440 | tf_op jit(solution)/shard_map/ppermute | solution.py:295
  138.9 11.5 %collective-permute-start.51 = (f32[512,128]{1,0:T(8,128)S(1)}, f32[512,128]{1,0:T(8,128)S(1)}, u32[]{:S(2)}, u32[]{:S(2)}) collective-permute-start(f32[512,128]{1,0:T(8,128)S(1)} %column_product.7.refs_1_.refs_5_), channel_id=1, source_target_pairs={{0,2},{2,4},{4,6},{6,7},{7,5},{5,3},{3,1},{1,0},{8,10},{10,12},{12... | collective-permute-start | bytes 786440 | tf_op jit(solution)/shard_map/ppermute | solution.py:295
  143.3 11.2 %collective-permute-start.54 = (f32[512,128]{1,0:T(8,128)S(1)}, f32[512,128]{1,0:T(8,128)S(1)}, u32[]{:S(2)}, u32[]{:S(2)}) collective-permute-start(f32[512,128]{1,0:T(8,128)S(1)} %collective-permute-done.50.refs_3_.refs_9_), channel_id=1, source_target_pairs={{0,1},{2,0},{4,2},{6,4},{7,6},{5,7},{3,5},{1,3},{8,9},{10,8},{12,1... | collective-permute-start | bytes 786440 | tf_op jit(solution)/shard_map/ppermute | solution.py:295
  144.8 11.2 %collective-permute-start.53 = (f32[512,128]{1,0:T(8,128)S(1)}, f32[512,128]{1,0:T(8,128)S(1)}, u32[]{:S(2)}, u32[]{:S(2)}) collective-permute-start(f32[512,128]{1,0:T(8,128)S(1)} %collective-permute-done.49.refs_2_.refs_8_), channel_id=1, source_target_pairs={{0,2},{2,4},{4,6},{6,7},{7,5},{5,3},{3,1},{1,0},{8,10},{10,12},{12... | collective-permute-start | bytes 786440 | tf_op jit(solution)/shard_map/ppermute | solution.py:295
  148.9 11.2 %collective-permute-start.56 = (f32[512,128]{1,0:T(8,128)S(1)}, f32[512,128]{1,0:T(8,128)S(1)}, u32[]{:S(2)}, u32[]{:S(2)}) collective-permute-start(f32[512,128]{1,0:T(8,128)S(1)} %collective-permute-done.52.refs_5_.refs_11_), channel_id=1, source_target_pairs={{0,1},{2,0},{4,2},{6,4},{7,6},{5,7},{3,5},{1,3},{8,9},{10,8},{12,1... | collective-permute-start | bytes 786440 | tf_op jit(solution)/shard_map/ppermute | solution.py:295
  150.4 11.2 %collective-permute-start.55 = (f32[512,128]{1,0:T(8,128)S(1)}, f32[512,128]{1,0:T(8,128)S(1)}, u32[]{:S(2)}, u32[]{:S(2)}) collective-permute-start(f32[512,128]{1,0:T(8,128)S(1)} %collective-permute-done.51.refs_4_.refs_10_), channel_id=1, source_target_pairs={{0,2},{2,4},{4,6},{6,7},{7,5},{5,3},{3,1},{1,0},{8,10},{10,12},{12... | collective-permute-start | bytes 786440 | tf_op jit(solution)/shard_map/ppermute | solution.py:295
  154.5 11.2 %collective-permute-start.58 = (f32[512,128]{1,0:T(8,128)S(1)}, f32[512,128]{1,0:T(8,128)S(1)}, u32[]{:S(2)}, u32[]{:S(2)}) collective-permute-start(f32[512,128]{1,0:T(8,128)S(1)} %collective-permute-done.54.refs_7_.refs_13_), channel_id=1, source_target_pairs={{0,1},{2,0},{4,2},{6,4},{7,6},{5,7},{3,5},{1,3},{8,9},{10,8},{12,1... | collective-permute-start | bytes 786440 | tf_op jit(solution)/shard_map/ppermute | solution.py:295
  156.0 11.3 %collective-permute-start.57 = (f32[512,128]{1,0:T(8,128)S(1)}, f32[512,128]{1,0:T(8,128)S(1)}, u32[]{:S(2)}, u32[]{:S(2)}) collective-permute-start(f32[512,128]{1,0:T(8,128)S(1)} %collective-permute-done.53.refs_6_.refs_12_), channel_id=1, source_target_pairs={{0,2},{2,4},{4,6},{6,7},{7,5},{5,3},{3,1},{1,0},{8,10},{10,12},{12... | collective-permute-start | bytes 786440 | tf_op jit(solution)/shard_map/ppermute | solution.py:295
  160.1 11.2 %collective-permute-start.60 = (f32[512,128]{1,0:T(8,128)S(1)}, f32[512,128]{1,0:T(8,128)S(1)}, u32[]{:S(2)}, u32[]{:S(2)}) collective-permute-start(f32[512,128]{1,0:T(8,128)S(1)} %collective-permute-done.56.refs_9_.refs_15_), channel_id=1, source_target_pairs={{0,1},{2,0},{4,2},{6,4},{7,6},{5,7},{3,5},{1,3},{8,9},{10,8},{12,1... | collective-permute-start | bytes 786440 | tf_op jit(solution)/shard_map/ppermute | solution.py:295
  161.6 11.3 %collective-permute-start.59 = (f32[512,128]{1,0:T(8,128)S(1)}, f32[512,128]{1,0:T(8,128)S(1)}, u32[]{:S(2)}, u32[]{:S(2)}) collective-permute-start(f32[512,128]{1,0:T(8,128)S(1)} %collective-permute-done.55.refs_8_.refs_14_), channel_id=1, source_target_pairs={{0,2},{2,4},{4,6},{6,7},{7,5},{5,3},{3,1},{1,0},{8,10},{10,12},{12... | collective-permute-start | bytes 786440 | tf_op jit(solution)/shard_map/ppermute | solution.py:295
  180.2 9.9 %collective-permute-start.67 = (f32[512,128]{1,0:T(8,128)S(1)}, f32[512,128]{1,0:T(8,128)S(1)}, u32[]{:S(2)}, u32[]{:S(2)}) collective-permute-start(f32[512,128]{1,0:T(8,128)S(1)} %get-tuple-element.71.refs_0_), channel_id=1, source_target_pairs={{0,16},{8,24},{16,0},{24,8},{1,17},{9,25},{17,1},{25,9},{2,18},{10... | collective-permute-start | bytes 786440 | tf_op jit(solution)/shard_map/ppermute | solution.py:304
  180.7 11.6 %collective-permute-start.68 = (f32[512,128]{1,0:T(8,128)S(1)}, f32[512,128]{1,0:T(8,128)S(1)}, u32[]{:S(2)}, u32[]{:S(2)}) collective-permute-start(f32[512,128]{1,0:T(8,128)S(1)} %get-tuple-element.72.refs_1_), channel_id=1, source_target_pairs={{0,16},{8,24},{16,0},{24,8},{1,17},{9,25},{17,1},{25,9},{2,18},{10... | collective-permute-start | bytes 786440 | tf_op jit(solution)/shard_map/ppermute | solution.py:304
  205.1 9.4 %collective-permute-start.78 = (f32[128,128]{1,0:T(8,128)S(1)}, f32[128,128]{1,0:T(8,128)S(1)}, u32[]{:S(2)}, u32[]{:S(2)}) collective-permute-start(f32[128,128]{1,0:T(8,128)S(1)} %add.38), channel_id=1, source_target_pairs={{0,4},{1,5},{2,6},{3,7},{4,0},{5,1},{6,2},{7,3},{8,12},{9,13},{10,... | collective-permute-start | bytes 196616 | tf_op jit(solution)/shard_map/ppermute | solution.py:304
  (51 other events, 310.3 us)

commit v4 on v3

--- a/solution.py
+++ b/solution.py
@@ -124,11 +124,13 @@
     q_out[...] = q
 
 
-def row_kernel(slots, pieces, last, table, places, scalars, *refs):
+def row_kernel(slots, own, pieces, last, table, places, scalars, *refs):
     refs = list(refs)
-    high_t, low_t, mine, vectors = [[refs.pop(0) for _ in range(slots)] for _ in range(4)]
-    arrived, p_out, (total, landing, sems) = refs[: len(pieces)], refs[len(pieces) : -3], refs[-3:]
+    high_t, low_t, vectors = [refs.pop(0) for _ in range(3)]
+    mine = [refs.pop(0) for _ in range(slots)]
+    arrived, (p_out, total, landing, sems) = refs[: len(pieces)], refs[len(pieces) :]
     center, radius = scalars[0], scalars[1]
+    wanted = table[own]
     rows = [table_row(table, places, entry, slots, slot) for entry, slot, _ in pieces]
 
     def copy(b):
@@ -136,40 +138,31 @@
 
     def each(action):
         for b in range(len(pieces)):
-            hit = rows[b] < -1
-            for s in range(slots):
-                hit = hit | ((rows[b] == table[s]) & (rows[b] >= 0))
-
-            @pl.when(hit)
+
+            @pl.when((rows[b] == wanted) & (wanted >= 0))
             def _():
                 action(b)
 
     each(lambda b: copy(b).start())
-    for s in range(slots):
-        total[s] = mine[s][...]
-        for t in range(slots):
-            if t != s:
-
-                @pl.when((table[t] == table[s]) & (table[s] >= 0))
-                def _():
-                    total[s] += mine[t][...]
+    total[...] = mine[own][...]
+    for t in range(slots):
+        if t != own:
+
+            @pl.when((table[t] == wanted) & (wanted >= 0))
+            def _():
+                total[...] += mine[t][...]
 
     def add(b):
         copy(b).wait()
         first, count = pieces[b][2], arrived[b].shape[0]
-        for s in range(slots):
-
-            @pl.when(rows[b] == table[s])
-            def _():
-                total[s, first : first + count, :] += landing[b, :count, :]
+        total[first : first + count, :] += landing[b, :count, :]
 
     each(add)
-    for s in range(slots):
-        if last:
-            y = total[s] + (2.0 * (center / radius) * (center / radius) - 1.0) * vectors[s][...]
-        else:
-            y = (total[s] - center * vectors[s][...]) / radius
-        p_out[s][...] = dot3(high_t[s][...], low_t[s][...], y)
+    if last:
+        y = total[...] + (2.0 * (center / radius) * (center / radius) - 1.0) * vectors[...]
+    else:
+        y = (total[...] - center * vectors[...]) / radius
+    p_out[...] = dot3(high_t[...], low_t[...], y)
 
 
 def owner_kernel(slots, pieces, unit, per_block, table, places, scalars, start, *refs):
@@ -264,16 +257,12 @@
 
 
 def basis_kernel(following, inverse, out):
-    out[...] = lax.dot_general(
-        following[...], inverse[...], (((1,), (1,)), ((), ())), precision=HIGHEST, preferred_element_type=jnp.float32
-    )
+    out[...] = dot3(*split(following[...]), inverse[...].T)
 
 
 def project_kernel(inverse, inner, out):
-    half = jnp.dot(inverse[...], inner[...], precision=HIGHEST, preferred_element_type=jnp.float32)
-    out[...] = lax.dot_general(
-        half, inverse[...], (((1,), (1,)), ((), ())), precision=HIGHEST, preferred_element_type=jnp.float32
-    )
+    half = dot3(*split(inverse[...]), inner[...])
+    out[...] = dot3(*split(half), inverse[...].T)
 
 
 def solution(mesh):
@@ -431,20 +420,23 @@
             return out
 
         def row_step(last, mine, pieces, got, vectors):
-            return call(
-                functools.partial(row_kernel, slots, pieces, last),
-                [chunk] * slots,
-                [SMEM] * 3 + [VMEM] * (4 * slots) + [ANY] * len(got),
-                [VMEM] * slots,
-                [table, places, scalars] + high_t + low_t + mine + vectors + got,
-                scratch=[
-                    pltpu.VMEM((slots, size, vec), jnp.float32),
-                    pltpu.VMEM((len(got), size, vec), jnp.float32),
-                    pltpu.SemaphoreType.DMA((len(got),)),
-                ],
-                flops=flops * slots,
-                name="row_product",
-            )
+            return [
+                call(
+                    functools.partial(row_kernel, slots, slot, pieces, last),
+                    chunk,
+                    [SMEM] * 3 + [VMEM] * (3 + slots) + [ANY] * len(got),
+                    VMEM,
+                    [table, places, scalars, high_t[slot], low_t[slot], vectors[slot]] + mine + got,
+                    scratch=[
+                        pltpu.VMEM(chunk.shape, jnp.float32),
+                        pltpu.VMEM((len(got), size, vec), jnp.float32),
+                        pltpu.SemaphoreType.DMA((len(got),)),
+                    ],
+                    flops=flops,
+                    name="row_product",
+                )
+                for slot in range(slots)
+            ]
 
         xs, ps = zip(*[first_step(slot) for slot in range(slots)])
         xs, ps = list(xs), list(ps)

time: 216 us -> 214 us (level)
  waiting for transfers between devices: 102 us -> 99.3 us
    ppermute x31, waiting for transfers between devices: 36.7 us -> 33.5 us  [flip(): return lax.ppermute(value, axis, [(i, i ^ bit) for i in range(size)])]
    pallas_call x30 -> x32, Pallas kernels: 33.8 us -> 35.3 us  [call(): pl.pallas_call(kernel, out_shape=out_shape, in_specs=in_specs, out_specs=...]
  transfers between devices with their start and end apart: 79 -> 79, of which waited for: 45 -> 45; matrix products, arithmetic and copies ran while one was open for 1% -> 1% of each run, Pallas kernels for 12% -> 13%
where the time goes in v4:
time: 214 us
  waiting for transfers between devices  99.3 us (46%)
  starting transfers between devices  73 us (34%)
  Pallas kernels  35.3 us (16%)
  between operations  3.02 us (1%)
    ppermute x48, waiting for transfers between devices, forward(): lax.ppermute(value, 'col', [(col, ring[(k + step) % n_col]) for k, col in...  65.8 us
    ppermute x48, starting transfers between devices, forward(): lax.ppermute(value, 'col', [(col, ring[(k + step) % n_col]) for k, col in...  50.1 us
    pallas_call x32, Pallas kernels, call(): pl.pallas_call(kernel, out_shape=out_shape, in_specs=in_specs, out_specs=...  35.3 us
    ppermute x31, waiting for transfers between devices, flip(): return lax.ppermute(value, axis, [(i, i ^ bit) for i in range(size)])  33.5 us
    ppermute x31, starting transfers between devices, flip(): return lax.ppermute(value, axis, [(i, i ^ bit) for i in range(size)])  23 us
  transfers between devices with their start and end apart: 79, of which 45 were waited for; matrix products, arithmetic and copies ran while one was open for 1% of the time, Pallas kernels for 13%

profile of v4, /device:TPU:0, one launch (start us, length us, event | category | flops | bytes accessed | tf_op | source)
XLA Modules:
  0.0 213.9 jit_solution(16741315433261852216)
XLA Ops:
  1.9 3.0 %collective-permute-start = (s32[2]{0:T(128)S(1)}, s32[2]{0:T(128)S(1)}, u32[]{:S(2)}, u32[]{:S(2)}) collective-permute-start(s32[2]{0:T(128)S(1)} %compare_select_fusion.1), channel_id=1, source_target_pairs={{0,1},{1,0},{2,3},{3,2},{4,5},{5,4},{6,7},{7,6},{8,9},{9,8},{10,11... | collective-permute-start | bytes 32 | tf_op jit(solution)/shard_map/tables/ppermute | solution.py:293
  6.5 2.1 collective-permute-start.1
  10.2 3.0 %collective-permute-start.2 = (s32[8]{0:T(128)S(1)}, s32[8]{0:T(128)S(1)}, u32[]{:S(2)}, u32[]{:S(2)}) collective-permute-start(s32[8]{0:T(128)S(1)} %pad_add_fusion.1), channel_id=1, source_target_pairs={{0,4},{1,5},{2,6},{3,7},{4,0},{5,1},{6,2},{7,3},{8,12},{9,13},{10,... | collective-permute-start | bytes 104 | tf_op jit(solution)/shard_map/tables/ppermute | solution.py:293
  16.6 1.9 collective-permute-start.17
  19.9 1.9 collective-permute-start.9
  23.2 1.9 collective-permute-start.18
  29.7 2.8 %collective-permute-done.18.refs_0_ = f32[512,128]{1,0:T(8,128)S(1)} collective-permute-done((f32[512,128]{1,0:T(8,128)S(1)}, f32[512,128]{1,0:T(8,128)S(1)}, u32[]{:S(2)}, u32[]{:S(2)}) %collective-permute-start.18) | collective-permute-done | bytes 262176 | tf_op jit(solution)/shard_map/ppermute | solution.py:284
  35.8 2.3 %collective-permute-done.10.refs_0_ = f32[512,128]{1,0:T(8,128)S(1)} collective-permute-done((f32[512,128]{1,0:T(8,128)S(1)}, f32[512,128]{1,0:T(8,128)S(1)}, u32[]{:S(2)}, u32[]{:S(2)}) %collective-permute-start.10) | collective-permute-done | bytes 262176 | tf_op jit(solution)/shard_map/ppermute | solution.py:284
  51.3 3.1 %collective-permute-done.20.refs_1_ = f32[512,128]{1,0:T(8,128)S(1)} collective-permute-done((f32[512,128]{1,0:T(8,128)S(1)}, f32[512,128]{1,0:T(8,128)S(1)}, u32[]{:S(2)}, u32[]{:S(2)}) %collective-permute-start.20) | collective-permute-done | bytes 262176 | tf_op jit(solution)/shard_map/ppermute | solution.py:284
  54.4 2.2 %collective-permute-done.16.refs_0_ = f32[512,128]{1,0:T(8,128)S(1)} collective-permute-done((f32[512,128]{1,0:T(8,128)S(1)}, f32[512,128]{1,0:T(8,128)S(1)}, u32[]{:S(2)}, u32[]{:S(2)}) %collective-permute-start.16) | collective-permute-done | bytes 262176 | tf_op jit(solution)/shard_map/ppermute | solution.py:284
  64.2 5.5 %collective-permute-done.23.refs_4_ = f32[512,128]{1,0:T(8,128)S(1)} collective-permute-done((f32[512,128]{1,0:T(8,128)S(1)}, f32[512,128]{1,0:T(8,128)S(1)}, u32[]{:S(2)}, u32[]{:S(2)}) %collective-permute-start.23) | collective-permute-done | bytes 262176 | tf_op jit(solution)/shard_map/ppermute | solution.py:293
  78.0 3.8 %collective-permute-done.28.refs_6_ = f32[512,128]{1,0:T(8,128)S(1)} collective-permute-done((f32[512,128]{1,0:T(8,128)S(1)}, f32[512,128]{1,0:T(8,128)S(1)}, u32[]{:S(2)}, u32[]{:S(2)}) %collective-permute-start.28) | collective-permute-done | bytes 262176 | tf_op jit(solution)/shard_map/ppermute | solution.py:284
  83.9 3.6 %collective-permute-done.30.refs_8_ = f32[512,128]{1,0:T(8,128)S(1)} collective-permute-done((f32[512,128]{1,0:T(8,128)S(1)}, f32[512,128]{1,0:T(8,128)S(1)}, u32[]{:S(2)}, u32[]{:S(2)}) %collective-permute-start.30) | collective-permute-done | bytes 262176 | tf_op jit(solution)/shard_map/ppermute | solution.py:284
  89.5 3.6 %collective-permute-done.32.refs_10_ = f32[512,128]{1,0:T(8,128)S(1)} collective-permute-done((f32[512,128]{1,0:T(8,128)S(1)}, f32[512,128]{1,0:T(8,128)S(1)}, u32[]{:S(2)}, u32[]{:S(2)}) %collective-permute-start.32) | collective-permute-done | bytes 262176 | tf_op jit(solution)/shard_map/ppermute | solution.py:284
  95.1 3.6 %collective-permute-done.34.refs_12_ = f32[512,128]{1,0:T(8,128)S(1)} collective-permute-done((f32[512,128]{1,0:T(8,128)S(1)}, f32[512,128]{1,0:T(8,128)S(1)}, u32[]{:S(2)}, u32[]{:S(2)}) %collective-permute-start.34) | collective-permute-done | bytes 262176 | tf_op jit(solution)/shard_map/ppermute | solution.py:284
  100.7 3.6 %collective-permute-done.36.refs_14_ = f32[512,128]{1,0:T(8,128)S(1)} collective-permute-done((f32[512,128]{1,0:T(8,128)S(1)}, f32[512,128]{1,0:T(8,128)S(1)}, u32[]{:S(2)}, u32[]{:S(2)}) %collective-permute-start.36) | collective-permute-done | bytes 262176 | tf_op jit(solution)/shard_map/ppermute | solution.py:284
  106.4 3.5 %collective-permute-done.38.refs_16_ = f32[512,128]{1,0:T(8,128)S(1)} collective-permute-done((f32[512,128]{1,0:T(8,128)S(1)}, f32[512,128]{1,0:T(8,128)S(1)}, u32[]{:S(2)}, u32[]{:S(2)}) %collective-permute-start.38) | collective-permute-done | bytes 262176 | tf_op jit(solution)/shard_map/ppermute | solution.py:284
  122.2 5.1 %collective-permute-done.45.refs_5_ = f32[512,128]{1,0:T(8,128)S(1)} collective-permute-done((f32[512,128]{1,0:T(8,128)S(1)}, f32[512,128]{1,0:T(8,128)S(1)}, u32[]{:S(2)}, u32[]{:S(2)}) %collective-permute-start.45) | collective-permute-done | bytes 262176 | tf_op jit(solution)/shard_map/ppermute | solution.py:293
  127.4 3.0 %collective-permute-done.46.refs_6_ = f32[512,128]{1,0:T(8,128)S(1)} collective-permute-done((f32[512,128]{1,0:T(8,128)S(1)}, f32[512,128]{1,0:T(8,128)S(1)}, u32[]{:S(2)}, u32[]{:S(2)}) %collective-permute-start.46) | collective-permute-done | bytes 262176 | tf_op jit(solution)/shard_map/ppermute | solution.py:293
  138.8 3.8 %collective-permute-done.50.refs_3_.refs_6_ = f32[512,128]{1,0:T(8,128)S(1)} collective-permute-done((f32[512,128]{1,0:T(8,128)S(1)}, f32[512,128]{1,0:T(8,128)S(1)}, u32[]{:S(2)}, u32[]{:S(2)}) %collective-permute-start.50) | collective-permute-done | bytes 262176 | tf_op jit(solution)/shard_map/ppermute | solution.py:284
  144.6 3.5 %collective-permute-done.52.refs_5_.refs_8_ = f32[512,128]{1,0:T(8,128)S(1)} collective-permute-done((f32[512,128]{1,0:T(8,128)S(1)}, f32[512,128]{1,0:T(8,128)S(1)}, u32[]{:S(2)}, u32[]{:S(2)}) %collective-permute-start.52) | collective-permute-done | bytes 262176 | tf_op jit(solution)/shard_map/ppermute | solution.py:284
  150.3 3.5 %collective-permute-done.54.refs_7_.refs_10_ = f32[512,128]{1,0:T(8,128)S(1)} collective-permute-done((f32[512,128]{1,0:T(8,128)S(1)}, f32[512,128]{1,0:T(8,128)S(1)}, u32[]{:S(2)}, u32[]{:S(2)}) %collective-permute-start.54) | collective-permute-done | bytes 262176 | tf_op jit(solution)/shard_map/ppermute | solution.py:284
  155.9 3.5 %collective-permute-done.56.refs_9_.refs_12_ = f32[512,128]{1,0:T(8,128)S(1)} collective-permute-done((f32[512,128]{1,0:T(8,128)S(1)}, f32[512,128]{1,0:T(8,128)S(1)}, u32[]{:S(2)}, u32[]{:S(2)}) %collective-permute-start.56) | collective-permute-done | bytes 262176 | tf_op jit(solution)/shard_map/ppermute | solution.py:284
  161.5 3.5 %collective-permute-done.58.refs_11_.refs_14_ = f32[512,128]{1,0:T(8,128)S(1)} collective-permute-done((f32[512,128]{1,0:T(8,128)S(1)}, f32[512,128]{1,0:T(8,128)S(1)}, u32[]{:S(2)}, u32[]{:S(2)}) %collective-permute-start.58) | collective-permute-done | bytes 262176 | tf_op jit(solution)/shard_map/ppermute | solution.py:284
  167.2 3.5 %collective-permute-done.60.refs_13_.refs_16_ = f32[512,128]{1,0:T(8,128)S(1)} collective-permute-done((f32[512,128]{1,0:T(8,128)S(1)}, f32[512,128]{1,0:T(8,128)S(1)}, u32[]{:S(2)}, u32[]{:S(2)}) %collective-permute-start.60) | collective-permute-done | bytes 262176 | tf_op jit(solution)/shard_map/ppermute | solution.py:284
  182.5 2.3 %owner_rows.1 = (f32[2048,128]{1,0:T(8,128)S(1)}, f32[128,128]{1,0:T(8,128)S(1)}) custom-call(s32[16]{0:T(128)S(1)} %pad_add_fusion.2.table, s32[10]{0:T(128)S(1)} %constant_dynamic-update-slice_fusion.places, f32[2]{0:T(128)S(1)} %pad_maximum_fusion.scalars, f32[2048,128]{1,0:T(8,128)S(1)} %copy-done.1, f32[512,128]{1,0:T(8,128)S(1)} %column_product.6.refs_0_.refs_3_, ...), custom_call_target="tpu_custom_call" | custom-call | flops 201326592 | bytes 5242992 | tf_op jit(solution)/shard_map/owner_rows/pallas_call | solution.py:20
  188.0 2.5 %collective-permute-done.66 = f32[128,128]{1,0:T(8,128)S(1)} collective-permute-done((f32[128,128]{1,0:T(8,128)S(1)}, f32[128,128]{1,0:T(8,128)S(1)}, u32[]{:S(2)}, u32[]{:S(2)}) %collective-permute-start.66) | collective-permute-done | bytes 65568 | tf_op jit(solution)/shard_map/ppermute | solution.py:293
  192.8 2.2 %inner_product.1 = f32[128,128]{1,0:T(8,128)S(1)} custom-call(s32[8]{0:T(128)S(1)} %pad_add_fusion.4.columns, s32[1]{0:T(128)} %bitcast.6.place, f32[512,128]{1,0:T(8,128)S(1)} %row_product.6.refs_0_, f32[512,128]{1,0:T(8,128)S(1)} %row_product.7.refs_1_, f32[512,128]{1,0:T(8,128)S(1)} %collective-permute-done.72.refs_2_, ...), custom_call_target="tpu_custom_call" | custom-call | flops 402653184 | bytes 2097188 | tf_op jit(solution)/shard_map/inner_product/pallas_call | solution.py:20
  196.8 2.5 %collective-permute-done.76 = f32[128,128]{1,0:T(8,128)S(1)} collective-permute-done((f32[128,128]{1,0:T(8,128)S(1)}, f32[128,128]{1,0:T(8,128)S(1)}, u32[]{:S(2)}, u32[]{:S(2)}) %collective-permute-start.76) | collective-permute-done | bytes 65568 | tf_op jit(solution)/shard_map/ppermute | solution.py:293
  200.1 2.8 %collective-permute-done.70 = f32[128,128]{1,0:T(8,128)S(1)} collective-permute-done((f32[128,128]{1,0:T(8,128)S(1)}, f32[128,128]{1,0:T(8,128)S(1)}, u32[]{:S(2)}, u32[]{:S(2)}) %collective-permute-start.70) | collective-permute-done | bytes 65568 | tf_op jit(solution)/shard_map/ppermute | solution.py:293
  204.1 3.1 %collective-permute-done.71 = f32[128,128]{1,0:T(8,128)S(1)} collective-permute-done((f32[128,128]{1,0:T(8,128)S(1)}, f32[128,128]{1,0:T(8,128)S(1)}, u32[]{:S(2)}, u32[]{:S(2)}) %collective-permute-start.71) | collective-permute-done | bytes 65568 | tf_op jit(solution)/shard_map/ppermute | solution.py:293
  207.2 4.0 %factor.1.inverse = f32[128,128]{1,0:T(8,128)S(1)} custom-call(f32[128,128]{1,0:T(8,128)S(1)} %add.36.gram), custom_call_target="tpu_custom_call" | custom-call | flops 8388608 | bytes 65536 | tf_op jit(solution)/shard_map/factor/pallas_call | solution.py:20
  (192 shorter events, 110.7 us)
Async XLA Ops:
  23.2 9.3 %collective-permute-start.18 = (f32[512,128]{1,0:T(8,128)S(1)}, f32[512,128]{1,0:T(8,128)S(1)}, u32[]{:S(2)}, u32[]{:S(2)}) collective-permute-start(f32[512,128]{1,0:T(8,128)S(1)} %pick_rows.29), channel_id=1, source_target_pairs={{0,1},{2,0},{4,2},{6,4},{7,6},{5,7},{3,5},{1,3},{8,9},{10,8},{12,1... | collective-permute-start | bytes 786440 | tf_op jit(solution)/shard_map/ppermute | solution.py:284
  25.7 9.3 %collective-permute-start.14 = (f32[512,128]{1,0:T(8,128)S(1)}, f32[512,128]{1,0:T(8,128)S(1)}, u32[]{:S(2)}, u32[]{:S(2)}) collective-permute-start(f32[512,128]{1,0:T(8,128)S(1)} %pick_rows.25), channel_id=1, source_target_pairs={{0,2},{2,4},{4,6},{6,7},{7,5},{5,3},{3,1},{1,0},{8,10},{10,12},{12... | collective-permute-start | bytes 786440 | tf_op jit(solution)/shard_map/ppermute | solution.py:284
  27.0 11.1 %collective-permute-start.10 = (f32[512,128]{1,0:T(8,128)S(1)}, f32[512,128]{1,0:T(8,128)S(1)}, u32[]{:S(2)}, u32[]{:S(2)}) collective-permute-start(f32[512,128]{1,0:T(8,128)S(1)} %pick_rows.21), channel_id=1, source_target_pairs={{0,1},{2,0},{4,2},{6,4},{7,6},{5,7},{3,5},{1,3},{8,9},{10,8},{12,1... | collective-permute-start | bytes 786440 | tf_op jit(solution)/shard_map/ppermute | solution.py:284
  29.5 11.2 %collective-permute-start.4 = (f32[512,128]{1,0:T(8,128)S(1)}, f32[512,128]{1,0:T(8,128)S(1)}, u32[]{:S(2)}, u32[]{:S(2)}) collective-permute-start(f32[512,128]{1,0:T(8,128)S(1)} %pick_rows.17), channel_id=1, source_target_pairs={{0,2},{2,4},{4,6},{6,7},{7,5},{5,3},{3,1},{1,0},{8,10},{10,12},{12... | collective-permute-start | bytes 786440 | tf_op jit(solution)/shard_map/ppermute | solution.py:284
  33.1 11.5 %collective-permute-start.19 = (f32[512,128]{1,0:T(8,128)S(1)}, f32[512,128]{1,0:T(8,128)S(1)}, u32[]{:S(2)}, u32[]{:S(2)}) collective-permute-start(f32[512,128]{1,0:T(8,128)S(1)} %pick_rows.30), channel_id=1, source_target_pairs={{0,1},{2,0},{4,2},{6,4},{7,6},{5,7},{3,5},{1,3},{8,9},{10,8},{12,1... | collective-permute-start | bytes 786440 | tf_op jit(solution)/shard_map/ppermute | solution.py:284
  35.6 11.1 %collective-permute-start.15 = (f32[512,128]{1,0:T(8,128)S(1)}, f32[512,128]{1,0:T(8,128)S(1)}, u32[]{:S(2)}, u32[]{:S(2)}) collective-permute-start(f32[512,128]{1,0:T(8,128)S(1)} %pick_rows.26), channel_id=1, source_target_pairs={{0,2},{2,4},{4,6},{6,7},{7,5},{5,3},{3,1},{1,0},{8,10},{10,12},{12... | collective-permute-start | bytes 786440 | tf_op jit(solution)/shard_map/ppermute | solution.py:284
  48.6 10.7 %collective-permute-start.12 = (f32[512,128]{1,0:T(8,128)S(1)}, f32[512,128]{1,0:T(8,128)S(1)}, u32[]{:S(2)}, u32[]{:S(2)}) collective-permute-start(f32[512,128]{1,0:T(8,128)S(1)} %pick_rows.23), channel_id=1, source_target_pairs={{0,1},{2,0},{4,2},{6,4},{7,6},{5,7},{3,5},{1,3},{8,9},{10,8},{12,1... | collective-permute-start | bytes 786440 | tf_op jit(solution)/shard_map/ppermute | solution.py:284
  50.7 10.4 %collective-permute-start.8 = (f32[512,128]{1,0:T(8,128)S(1)}, f32[512,128]{1,0:T(8,128)S(1)}, u32[]{:S(2)}, u32[]{:S(2)}) collective-permute-start(f32[512,128]{1,0:T(8,128)S(1)} %pick_rows.19), channel_id=1, source_target_pairs={{0,2},{2,4},{4,6},{6,7},{7,5},{5,3},{3,1},{1,0},{8,10},{10,12},{12... | collective-permute-start | bytes 786440 | tf_op jit(solution)/shard_map/ppermute | solution.py:284
  76.0 11.5 %collective-permute-start.30 = (f32[512,128]{1,0:T(8,128)S(1)}, f32[512,128]{1,0:T(8,128)S(1)}, u32[]{:S(2)}, u32[]{:S(2)}) collective-permute-start(f32[512,128]{1,0:T(8,128)S(1)} %column_product.5.refs_4_.refs_0_), channel_id=1, source_target_pairs={{0,1},{2,0},{4,2},{6,4},{7,6},{5,7},{3,5},{1,3},{8,9},{10,8},{12,1... | collective-permute-start | bytes 786440 | tf_op jit(solution)/shard_map/ppermute | solution.py:284
  77.6 11.4 %collective-permute-start.29 = (f32[512,128]{1,0:T(8,128)S(1)}, f32[512,128]{1,0:T(8,128)S(1)}, u32[]{:S(2)}, u32[]{:S(2)}) collective-permute-start(f32[512,128]{1,0:T(8,128)S(1)} %column_product.5.refs_4_.refs_0_), channel_id=1, source_target_pairs={{0,2},{2,4},{4,6},{6,7},{7,5},{5,3},{3,1},{1,0},{8,10},{10,12},{12... | collective-permute-start | bytes 786440 | tf_op jit(solution)/shard_map/ppermute | solution.py:284
  81.8 11.2 %collective-permute-start.32 = (f32[512,128]{1,0:T(8,128)S(1)}, f32[512,128]{1,0:T(8,128)S(1)}, u32[]{:S(2)}, u32[]{:S(2)}) collective-permute-start(f32[512,128]{1,0:T(8,128)S(1)} %collective-permute-done.28.refs_6_), channel_id=1, source_target_pairs={{0,1},{2,0},{4,2},{6,4},{7,6},{5,7},{3,5},{1,3},{8,9},{10,8},{12,1... | collective-permute-start | bytes 786440 | tf_op jit(solution)/shard_map/ppermute | solution.py:284
  83.4 11.2 %collective-permute-start.31 = (f32[512,128]{1,0:T(8,128)S(1)}, f32[512,128]{1,0:T(8,128)S(1)}, u32[]{:S(2)}, u32[]{:S(2)}) collective-permute-start(f32[512,128]{1,0:T(8,128)S(1)} %collective-permute-done.27.refs_5_), channel_id=1, source_target_pairs={{0,2},{2,4},{4,6},{6,7},{7,5},{5,3},{3,1},{1,0},{8,10},{10,12},{12... | collective-permute-start | bytes 786440 | tf_op jit(solution)/shard_map/ppermute | solution.py:284
  87.4 11.2 %collective-permute-start.34 = (f32[512,128]{1,0:T(8,128)S(1)}, f32[512,128]{1,0:T(8,128)S(1)}, u32[]{:S(2)}, u32[]{:S(2)}) collective-permute-start(f32[512,128]{1,0:T(8,128)S(1)} %collective-permute-done.30.refs_8_), channel_id=1, source_target_pairs={{0,1},{2,0},{4,2},{6,4},{7,6},{5,7},{3,5},{1,3},{8,9},{10,8},{12,1... | collective-permute-start | bytes 786440 | tf_op jit(solution)/shard_map/ppermute | solution.py:284
  89.0 11.2 %collective-permute-start.33 = (f32[512,128]{1,0:T(8,128)S(1)}, f32[512,128]{1,0:T(8,128)S(1)}, u32[]{:S(2)}, u32[]{:S(2)}) collective-permute-start(f32[512,128]{1,0:T(8,128)S(1)} %collective-permute-done.29.refs_7_), channel_id=1, source_target_pairs={{0,2},{2,4},{4,6},{6,7},{7,5},{5,3},{3,1},{1,0},{8,10},{10,12},{12... | collective-permute-start | bytes 786440 | tf_op jit(solution)/shard_map/ppermute | solution.py:284
  93.0 11.2 %collective-permute-start.36 = (f32[512,128]{1,0:T(8,128)S(1)}, f32[512,128]{1,0:T(8,128)S(1)}, u32[]{:S(2)}, u32[]{:S(2)}) collective-permute-start(f32[512,128]{1,0:T(8,128)S(1)} %collective-permute-done.32.refs_10_), channel_id=1, source_target_pairs={{0,1},{2,0},{4,2},{6,4},{7,6},{5,7},{3,5},{1,3},{8,9},{10,8},{12,1... | collective-permute-start | bytes 786440 | tf_op jit(solution)/shard_map/ppermute | solution.py:284
  94.6 11.3 %collective-permute-start.35 = (f32[512,128]{1,0:T(8,128)S(1)}, f32[512,128]{1,0:T(8,128)S(1)}, u32[]{:S(2)}, u32[]{:S(2)}) collective-permute-start(f32[512,128]{1,0:T(8,128)S(1)} %collective-permute-done.31.refs_9_), channel_id=1, source_target_pairs={{0,2},{2,4},{4,6},{6,7},{7,5},{5,3},{3,1},{1,0},{8,10},{10,12},{12... | collective-permute-start | bytes 786440 | tf_op jit(solution)/shard_map/ppermute | solution.py:284
  98.7 11.2 %collective-permute-start.38 = (f32[512,128]{1,0:T(8,128)S(1)}, f32[512,128]{1,0:T(8,128)S(1)}, u32[]{:S(2)}, u32[]{:S(2)}) collective-permute-start(f32[512,128]{1,0:T(8,128)S(1)} %collective-permute-done.34.refs_12_), channel_id=1, source_target_pairs={{0,1},{2,0},{4,2},{6,4},{7,6},{5,7},{3,5},{1,3},{8,9},{10,8},{12,1... | collective-permute-start | bytes 786440 | tf_op jit(solution)/shard_map/ppermute | solution.py:284
  100.2 11.3 %collective-permute-start.37 = (f32[512,128]{1,0:T(8,128)S(1)}, f32[512,128]{1,0:T(8,128)S(1)}, u32[]{:S(2)}, u32[]{:S(2)}) collective-permute-start(f32[512,128]{1,0:T(8,128)S(1)} %collective-permute-done.33.refs_11_), channel_id=1, source_target_pairs={{0,2},{2,4},{4,6},{6,7},{7,5},{5,3},{3,1},{1,0},{8,10},{10,12},{12... | collective-permute-start | bytes 786440 | tf_op jit(solution)/shard_map/ppermute | solution.py:284
  118.0 9.3 %collective-permute-start.45 = (f32[512,128]{1,0:T(8,128)S(1)}, f32[512,128]{1,0:T(8,128)S(1)}, u32[]{:S(2)}, u32[]{:S(2)}) collective-permute-start(f32[512,128]{1,0:T(8,128)S(1)} %row_product.4.refs_1_.refs_2_), channel_id=1, source_target_pairs={{0,16},{8,24},{16,0},{24,8},{1,17},{9,25},{17,1},{25,9},{2,18},{10... | collective-permute-start | bytes 786440 | tf_op jit(solution)/shard_map/ppermute | solution.py:293
  120.1 10.2 %collective-permute-start.46 = (f32[512,128]{1,0:T(8,128)S(1)}, f32[512,128]{1,0:T(8,128)S(1)}, u32[]{:S(2)}, u32[]{:S(2)}) collective-permute-start(f32[512,128]{1,0:T(8,128)S(1)} %row_product.5.refs_2_.refs_1_), channel_id=1, source_target_pairs={{0,16},{8,24},{16,0},{24,8},{1,17},{9,25},{17,1},{25,9},{2,18},{10... | collective-permute-start | bytes 786440 | tf_op jit(solution)/shard_map/ppermute | solution.py:293
  136.7 11.5 %collective-permute-start.52 = (f32[512,128]{1,0:T(8,128)S(1)}, f32[512,128]{1,0:T(8,128)S(1)}, u32[]{:S(2)}, u32[]{:S(2)}) collective-permute-start(f32[512,128]{1,0:T(8,128)S(1)} %column_product.7.refs_1_.refs_4_), channel_id=1, source_target_pairs={{0,1},{2,0},{4,2},{6,4},{7,6},{5,7},{3,5},{1,3},{8,9},{10,8},{12,1... | collective-permute-start | bytes 786440 | tf_op jit(solution)/shard_map/ppermute | solution.py:284
  138.3 11.5 %collective-permute-start.51 = (f32[512,128]{1,0:T(8,128)S(1)}, f32[512,128]{1,0:T(8,128)S(1)}, u32[]{:S(2)}, u32[]{:S(2)}) collective-permute-start(f32[512,128]{1,0:T(8,128)S(1)} %column_product.7.refs_1_.refs_4_), channel_id=1, source_target_pairs={{0,2},{2,4},{4,6},{6,7},{7,5},{5,3},{3,1},{1,0},{8,10},{10,12},{12... | collective-permute-start | bytes 786440 | tf_op jit(solution)/shard_map/ppermute | solution.py:284
  142.6 11.2 %collective-permute-start.54 = (f32[512,128]{1,0:T(8,128)S(1)}, f32[512,128]{1,0:T(8,128)S(1)}, u32[]{:S(2)}, u32[]{:S(2)}) collective-permute-start(f32[512,128]{1,0:T(8,128)S(1)} %collective-permute-done.50.refs_3_.refs_6_), channel_id=1, source_target_pairs={{0,1},{2,0},{4,2},{6,4},{7,6},{5,7},{3,5},{1,3},{8,9},{10,8},{12,1... | collective-permute-start | bytes 786440 | tf_op jit(solution)/shard_map/ppermute | solution.py:284
  144.1 11.2 %collective-permute-start.53 = (f32[512,128]{1,0:T(8,128)S(1)}, f32[512,128]{1,0:T(8,128)S(1)}, u32[]{:S(2)}, u32[]{:S(2)}) collective-permute-start(f32[512,128]{1,0:T(8,128)S(1)} %collective-permute-done.49.refs_2_.refs_5_), channel_id=1, source_target_pairs={{0,2},{2,4},{4,6},{6,7},{7,5},{5,3},{3,1},{1,0},{8,10},{10,12},{12... | collective-permute-start | bytes 786440 | tf_op jit(solution)/shard_map/ppermute | solution.py:284
  148.2 11.2 %collective-permute-start.56 = (f32[512,128]{1,0:T(8,128)S(1)}, f32[512,128]{1,0:T(8,128)S(1)}, u32[]{:S(2)}, u32[]{:S(2)}) collective-permute-start(f32[512,128]{1,0:T(8,128)S(1)} %collective-permute-done.52.refs_5_.refs_8_), channel_id=1, source_target_pairs={{0,1},{2,0},{4,2},{6,4},{7,6},{5,7},{3,5},{1,3},{8,9},{10,8},{12,1... | collective-permute-start | bytes 786440 | tf_op jit(solution)/shard_map/ppermute | solution.py:284
  149.8 11.2 %collective-permute-start.55 = (f32[512,128]{1,0:T(8,128)S(1)}, f32[512,128]{1,0:T(8,128)S(1)}, u32[]{:S(2)}, u32[]{:S(2)}) collective-permute-start(f32[512,128]{1,0:T(8,128)S(1)} %collective-permute-done.51.refs_4_.refs_7_), channel_id=1, source_target_pairs={{0,2},{2,4},{4,6},{6,7},{7,5},{5,3},{3,1},{1,0},{8,10},{10,12},{12... | collective-permute-start | bytes 786440 | tf_op jit(solution)/shard_map/ppermute | solution.py:284
  153.8 11.2 %collective-permute-start.58 = (f32[512,128]{1,0:T(8,128)S(1)}, f32[512,128]{1,0:T(8,128)S(1)}, u32[]{:S(2)}, u32[]{:S(2)}) collective-permute-start(f32[512,128]{1,0:T(8,128)S(1)} %collective-permute-done.54.refs_7_.refs_10_), channel_id=1, source_target_pairs={{0,1},{2,0},{4,2},{6,4},{7,6},{5,7},{3,5},{1,3},{8,9},{10,8},{12,1... | collective-permute-start | bytes 786440 | tf_op jit(solution)/shard_map/ppermute | solution.py:284
  155.4 11.3 %collective-permute-start.57 = (f32[512,128]{1,0:T(8,128)S(1)}, f32[512,128]{1,0:T(8,128)S(1)}, u32[]{:S(2)}, u32[]{:S(2)}) collective-permute-start(f32[512,128]{1,0:T(8,128)S(1)} %collective-permute-done.53.refs_6_.refs_9_), channel_id=1, source_target_pairs={{0,2},{2,4},{4,6},{6,7},{7,5},{5,3},{3,1},{1,0},{8,10},{10,12},{12... | collective-permute-start | bytes 786440 | tf_op jit(solution)/shard_map/ppermute | solution.py:284
  159.4 11.2 %collective-permute-start.60 = (f32[512,128]{1,0:T(8,128)S(1)}, f32[512,128]{1,0:T(8,128)S(1)}, u32[]{:S(2)}, u32[]{:S(2)}) collective-permute-start(f32[512,128]{1,0:T(8,128)S(1)} %collective-permute-done.56.refs_9_.refs_12_), channel_id=1, source_target_pairs={{0,1},{2,0},{4,2},{6,4},{7,6},{5,7},{3,5},{1,3},{8,9},{10,8},{12,1... | collective-permute-start | bytes 786440 | tf_op jit(solution)/shard_map/ppermute | solution.py:284
  161.0 11.3 %collective-permute-start.59 = (f32[512,128]{1,0:T(8,128)S(1)}, f32[512,128]{1,0:T(8,128)S(1)}, u32[]{:S(2)}, u32[]{:S(2)}) collective-permute-start(f32[512,128]{1,0:T(8,128)S(1)} %collective-permute-done.55.refs_8_.refs_11_), channel_id=1, source_target_pairs={{0,2},{2,4},{4,6},{6,7},{7,5},{5,3},{3,1},{1,0},{8,10},{10,12},{12... | collective-permute-start | bytes 786440 | tf_op jit(solution)/shard_map/ppermute | solution.py:284
  178.8 11.7 %collective-permute-start.67 = (f32[512,128]{1,0:T(8,128)S(1)}, f32[512,128]{1,0:T(8,128)S(1)}, u32[]{:S(2)}, u32[]{:S(2)}) collective-permute-start(f32[512,128]{1,0:T(8,128)S(1)} %row_product.6.refs_0_), channel_id=1, source_target_pairs={{0,16},{8,24},{16,0},{24,8},{1,17},{9,25},{17,1},{25,9},{2,18},{10... | collective-permute-start | bytes 786440 | tf_op jit(solution)/shard_map/ppermute | solution.py:293
  181.0 9.8 %collective-permute-start.68 = (f32[512,128]{1,0:T(8,128)S(1)}, f32[512,128]{1,0:T(8,128)S(1)}, u32[]{:S(2)}, u32[]{:S(2)}) collective-permute-start(f32[512,128]{1,0:T(8,128)S(1)} %row_product.7.refs_1_), channel_id=1, source_target_pairs={{0,16},{8,24},{16,0},{24,8},{1,17},{9,25},{17,1},{25,9},{2,18},{10... | collective-permute-start | bytes 786440 | tf_op jit(solution)/shard_map/ppermute | solution.py:293
  (51 other events, 306.2 us)

commit v5 on v4

--- a/solution.py
+++ b/solution.py
@@ -47,7 +47,7 @@
         return lax.dot_general(left, right, (((0,), (0,)), ((), ())), preferred_element_type=jnp.float32)
 
     mixed = dot(high, low)
-    return dot(high, high) + (dot(low, low) + (mixed + mixed.T))
+    return dot(high, high) + (mixed + mixed.T)
 
 
 def prepare_kernel(slots, values, *outs):

time: 214 us -> 214 us (level)
  no operation moved by 1% of the time
where the time goes in v5:
time: 214 us
  waiting for transfers between devices  99.5 us (46%)
  starting transfers between devices  73.3 us (34%)
  Pallas kernels  34.6 us (16%)
  between operations  3.02 us (1%)
    ppermute x48, waiting for transfers between devices, forward(): lax.ppermute(value, 'col', [(col, ring[(k + step) % n_col]) for k, col in...  65.9 us
    ppermute x48, starting transfers between devices, forward(): lax.ppermute(value, 'col', [(col, ring[(k + step) % n_col]) for k, col in...  50.1 us
    pallas_call x32, Pallas kernels, call(): pl.pallas_call(kernel, out_shape=out_shape, in_specs=in_specs, out_specs=...  34.6 us
    ppermute x31, waiting for transfers between devices, flip(): return lax.ppermute(value, axis, [(i, i ^ bit) for i in range(size)])  33.6 us
    ppermute x31, starting transfers between devices, flip(): return lax.ppermute(value, axis, [(i, i ^ bit) for i in range(size)])  23.2 us
  transfers between devices with their start and end apart: 79, of which 45 were waited for; matrix products, arithmetic and copies ran while one was open for 1% of the time, Pallas kernels for 13%

profile of v5, /device:TPU:0, one launch (start us, length us, event | category | flops | bytes accessed | tf_op | source)
XLA Modules:
  0.0 213.6 jit_solution(14696114778988660883)
XLA Ops:
  1.9 3.0 %collective-permute-start = (s32[2]{0:T(128)S(1)}, s32[2]{0:T(128)S(1)}, u32[]{:S(2)}, u32[]{:S(2)}) collective-permute-start(s32[2]{0:T(128)S(1)} %compare_select_fusion.1), channel_id=1, source_target_pairs={{0,1},{1,0},{2,3},{3,2},{4,5},{5,4},{6,7},{7,6},{8,9},{9,8},{10,11... | collective-permute-start | bytes 32 | tf_op jit(solution)/shard_map/tables/ppermute | solution.py:293
  6.5 2.1 collective-permute-start.1
  10.2 3.0 %collective-permute-start.2 = (s32[8]{0:T(128)S(1)}, s32[8]{0:T(128)S(1)}, u32[]{:S(2)}, u32[]{:S(2)}) collective-permute-start(s32[8]{0:T(128)S(1)} %pad_add_fusion.1), channel_id=1, source_target_pairs={{0,4},{1,5},{2,6},{3,7},{4,0},{5,1},{6,2},{7,3},{8,12},{9,13},{10,... | collective-permute-start | bytes 104 | tf_op jit(solution)/shard_map/tables/ppermute | solution.py:293
  16.6 1.9 collective-permute-start.17
  19.9 1.9 collective-permute-start.9
  23.2 1.9 collective-permute-start.18
  27.0 1.9 collective-permute-start.10
  29.7 2.8 %collective-permute-done.18.refs_0_ = f32[512,128]{1,0:T(8,128)S(1)} collective-permute-done((f32[512,128]{1,0:T(8,128)S(1)}, f32[512,128]{1,0:T(8,128)S(1)}, u32[]{:S(2)}, u32[]{:S(2)}) %collective-permute-start.18) | collective-permute-done | bytes 262176 | tf_op jit(solution)/shard_map/ppermute | solution.py:284
  35.8 2.3 %collective-permute-done.10.refs_0_ = f32[512,128]{1,0:T(8,128)S(1)} collective-permute-done((f32[512,128]{1,0:T(8,128)S(1)}, f32[512,128]{1,0:T(8,128)S(1)}, u32[]{:S(2)}, u32[]{:S(2)}) %collective-permute-start.10) | collective-permute-done | bytes 262176 | tf_op jit(solution)/shard_map/ppermute | solution.py:284
  51.3 3.1 %collective-permute-done.20.refs_1_ = f32[512,128]{1,0:T(8,128)S(1)} collective-permute-done((f32[512,128]{1,0:T(8,128)S(1)}, f32[512,128]{1,0:T(8,128)S(1)}, u32[]{:S(2)}, u32[]{:S(2)}) %collective-permute-start.20) | collective-permute-done | bytes 262176 | tf_op jit(solution)/shard_map/ppermute | solution.py:284
  54.4 2.2 %collective-permute-done.16.refs_0_ = f32[512,128]{1,0:T(8,128)S(1)} collective-permute-done((f32[512,128]{1,0:T(8,128)S(1)}, f32[512,128]{1,0:T(8,128)S(1)}, u32[]{:S(2)}, u32[]{:S(2)}) %collective-permute-start.16) | collective-permute-done | bytes 262176 | tf_op jit(solution)/shard_map/ppermute | solution.py:284
  64.2 5.5 %collective-permute-done.23.refs_4_ = f32[512,128]{1,0:T(8,128)S(1)} collective-permute-done((f32[512,128]{1,0:T(8,128)S(1)}, f32[512,128]{1,0:T(8,128)S(1)}, u32[]{:S(2)}, u32[]{:S(2)}) %collective-permute-start.23) | collective-permute-done | bytes 262176 | tf_op jit(solution)/shard_map/ppermute | solution.py:293
  78.0 3.8 %collective-permute-done.28.refs_6_ = f32[512,128]{1,0:T(8,128)S(1)} collective-permute-done((f32[512,128]{1,0:T(8,128)S(1)}, f32[512,128]{1,0:T(8,128)S(1)}, u32[]{:S(2)}, u32[]{:S(2)}) %collective-permute-start.28) | collective-permute-done | bytes 262176 | tf_op jit(solution)/shard_map/ppermute | solution.py:284
  83.8 3.5 %collective-permute-done.30.refs_8_ = f32[512,128]{1,0:T(8,128)S(1)} collective-permute-done((f32[512,128]{1,0:T(8,128)S(1)}, f32[512,128]{1,0:T(8,128)S(1)}, u32[]{:S(2)}, u32[]{:S(2)}) %collective-permute-start.30) | collective-permute-done | bytes 262176 | tf_op jit(solution)/shard_map/ppermute | solution.py:284
  89.5 3.5 %collective-permute-done.32.refs_10_ = f32[512,128]{1,0:T(8,128)S(1)} collective-permute-done((f32[512,128]{1,0:T(8,128)S(1)}, f32[512,128]{1,0:T(8,128)S(1)}, u32[]{:S(2)}, u32[]{:S(2)}) %collective-permute-start.32) | collective-permute-done | bytes 262176 | tf_op jit(solution)/shard_map/ppermute | solution.py:284
  95.1 3.5 %collective-permute-done.34.refs_12_ = f32[512,128]{1,0:T(8,128)S(1)} collective-permute-done((f32[512,128]{1,0:T(8,128)S(1)}, f32[512,128]{1,0:T(8,128)S(1)}, u32[]{:S(2)}, u32[]{:S(2)}) %collective-permute-start.34) | collective-permute-done | bytes 262176 | tf_op jit(solution)/shard_map/ppermute | solution.py:284
  100.7 3.5 %collective-permute-done.36.refs_14_ = f32[512,128]{1,0:T(8,128)S(1)} collective-permute-done((f32[512,128]{1,0:T(8,128)S(1)}, f32[512,128]{1,0:T(8,128)S(1)}, u32[]{:S(2)}, u32[]{:S(2)}) %collective-permute-start.36) | collective-permute-done | bytes 262176 | tf_op jit(solution)/shard_map/ppermute | solution.py:284
  106.4 3.5 %collective-permute-done.38.refs_16_ = f32[512,128]{1,0:T(8,128)S(1)} collective-permute-done((f32[512,128]{1,0:T(8,128)S(1)}, f32[512,128]{1,0:T(8,128)S(1)}, u32[]{:S(2)}, u32[]{:S(2)}) %collective-permute-start.38) | collective-permute-done | bytes 262176 | tf_op jit(solution)/shard_map/ppermute | solution.py:284
  122.2 5.1 %collective-permute-done.45.refs_5_ = f32[512,128]{1,0:T(8,128)S(1)} collective-permute-done((f32[512,128]{1,0:T(8,128)S(1)}, f32[512,128]{1,0:T(8,128)S(1)}, u32[]{:S(2)}, u32[]{:S(2)}) %collective-permute-start.45) | collective-permute-done | bytes 262176 | tf_op jit(solution)/shard_map/ppermute | solution.py:293
  127.4 2.9 %collective-permute-done.46.refs_6_ = f32[512,128]{1,0:T(8,128)S(1)} collective-permute-done((f32[512,128]{1,0:T(8,128)S(1)}, f32[512,128]{1,0:T(8,128)S(1)}, u32[]{:S(2)}, u32[]{:S(2)}) %collective-permute-start.46) | collective-permute-done | bytes 262176 | tf_op jit(solution)/shard_map/ppermute | solution.py:293
  138.7 3.8 %collective-permute-done.50.refs_3_.refs_6_ = f32[512,128]{1,0:T(8,128)S(1)} collective-permute-done((f32[512,128]{1,0:T(8,128)S(1)}, f32[512,128]{1,0:T(8,128)S(1)}, u32[]{:S(2)}, u32[]{:S(2)}) %collective-permute-start.50) | collective-permute-done | bytes 262176 | tf_op jit(solution)/shard_map/ppermute | solution.py:284
  144.6 3.6 %collective-permute-done.52.refs_5_.refs_8_ = f32[512,128]{1,0:T(8,128)S(1)} collective-permute-done((f32[512,128]{1,0:T(8,128)S(1)}, f32[512,128]{1,0:T(8,128)S(1)}, u32[]{:S(2)}, u32[]{:S(2)}) %collective-permute-start.52) | collective-permute-done | bytes 262176 | tf_op jit(solution)/shard_map/ppermute | solution.py:284
  150.2 3.6 %collective-permute-done.54.refs_7_.refs_10_ = f32[512,128]{1,0:T(8,128)S(1)} collective-permute-done((f32[512,128]{1,0:T(8,128)S(1)}, f32[512,128]{1,0:T(8,128)S(1)}, u32[]{:S(2)}, u32[]{:S(2)}) %collective-permute-start.54) | collective-permute-done | bytes 262176 | tf_op jit(solution)/shard_map/ppermute | solution.py:284
  155.8 3.6 %collective-permute-done.56.refs_9_.refs_12_ = f32[512,128]{1,0:T(8,128)S(1)} collective-permute-done((f32[512,128]{1,0:T(8,128)S(1)}, f32[512,128]{1,0:T(8,128)S(1)}, u32[]{:S(2)}, u32[]{:S(2)}) %collective-permute-start.56) | collective-permute-done | bytes 262176 | tf_op jit(solution)/shard_map/ppermute | solution.py:284
  161.4 3.6 %collective-permute-done.58.refs_11_.refs_14_ = f32[512,128]{1,0:T(8,128)S(1)} collective-permute-done((f32[512,128]{1,0:T(8,128)S(1)}, f32[512,128]{1,0:T(8,128)S(1)}, u32[]{:S(2)}, u32[]{:S(2)}) %collective-permute-start.58) | collective-permute-done | bytes 262176 | tf_op jit(solution)/shard_map/ppermute | solution.py:284
  167.1 3.5 %collective-permute-done.60.refs_13_.refs_16_ = f32[512,128]{1,0:T(8,128)S(1)} collective-permute-done((f32[512,128]{1,0:T(8,128)S(1)}, f32[512,128]{1,0:T(8,128)S(1)}, u32[]{:S(2)}, u32[]{:S(2)}) %collective-permute-start.60) | collective-permute-done | bytes 262176 | tf_op jit(solution)/shard_map/ppermute | solution.py:284
  187.9 2.2 %collective-permute-done.66 = f32[128,128]{1,0:T(8,128)S(1)} collective-permute-done((f32[128,128]{1,0:T(8,128)S(1)}, f32[128,128]{1,0:T(8,128)S(1)}, u32[]{:S(2)}, u32[]{:S(2)}) %collective-permute-start.66) | collective-permute-done | bytes 65568 | tf_op jit(solution)/shard_map/ppermute | solution.py:293
  192.8 2.0 inner_product.1
  196.6 2.5 %collective-permute-done.76 = f32[128,128]{1,0:T(8,128)S(1)} collective-permute-done((f32[128,128]{1,0:T(8,128)S(1)}, f32[128,128]{1,0:T(8,128)S(1)}, u32[]{:S(2)}, u32[]{:S(2)}) %collective-permute-start.76) | collective-permute-done | bytes 65568 | tf_op jit(solution)/shard_map/ppermute | solution.py:293
  199.8 2.8 %collective-permute-done.70 = f32[128,128]{1,0:T(8,128)S(1)} collective-permute-done((f32[128,128]{1,0:T(8,128)S(1)}, f32[128,128]{1,0:T(8,128)S(1)}, u32[]{:S(2)}, u32[]{:S(2)}) %collective-permute-start.70) | collective-permute-done | bytes 65568 | tf_op jit(solution)/shard_map/ppermute | solution.py:293
  203.9 3.0 %collective-permute-done.71 = f32[128,128]{1,0:T(8,128)S(1)} collective-permute-done((f32[128,128]{1,0:T(8,128)S(1)}, f32[128,128]{1,0:T(8,128)S(1)}, u32[]{:S(2)}, u32[]{:S(2)}) %collective-permute-start.71) | collective-permute-done | bytes 65568 | tf_op jit(solution)/shard_map/ppermute | solution.py:293
  206.9 4.0 %factor.1.inverse = f32[128,128]{1,0:T(8,128)S(1)} custom-call(f32[128,128]{1,0:T(8,128)S(1)} %add.36.gram), custom_call_target="tpu_custom_call" | custom-call | flops 8388608 | bytes 65536 | tf_op jit(solution)/shard_map/factor/pallas_call | solution.py:20
  (192 shorter events, 111.5 us)
Async XLA Ops:
  23.2 9.3 %collective-permute-start.18 = (f32[512,128]{1,0:T(8,128)S(1)}, f32[512,128]{1,0:T(8,128)S(1)}, u32[]{:S(2)}, u32[]{:S(2)}) collective-permute-start(f32[512,128]{1,0:T(8,128)S(1)} %pick_rows.29), channel_id=1, source_target_pairs={{0,1},{2,0},{4,2},{6,4},{7,6},{5,7},{3,5},{1,3},{8,9},{10,8},{12,1... | collective-permute-start | bytes 786440 | tf_op jit(solution)/shard_map/ppermute | solution.py:284
  25.7 9.3 %collective-permute-start.14 = (f32[512,128]{1,0:T(8,128)S(1)}, f32[512,128]{1,0:T(8,128)S(1)}, u32[]{:S(2)}, u32[]{:S(2)}) collective-permute-start(f32[512,128]{1,0:T(8,128)S(1)} %pick_rows.25), channel_id=1, source_target_pairs={{0,2},{2,4},{4,6},{6,7},{7,5},{5,3},{3,1},{1,0},{8,10},{10,12},{12... | collective-permute-start | bytes 786440 | tf_op jit(solution)/shard_map/ppermute | solution.py:284
  27.0 11.1 %collective-permute-start.10 = (f32[512,128]{1,0:T(8,128)S(1)}, f32[512,128]{1,0:T(8,128)S(1)}, u32[]{:S(2)}, u32[]{:S(2)}) collective-permute-start(f32[512,128]{1,0:T(8,128)S(1)} %pick_rows.21), channel_id=1, source_target_pairs={{0,1},{2,0},{4,2},{6,4},{7,6},{5,7},{3,5},{1,3},{8,9},{10,8},{12,1... | collective-permute-start | bytes 786440 | tf_op jit(solution)/shard_map/ppermute | solution.py:284
  29.5 11.2 %collective-permute-start.4 = (f32[512,128]{1,0:T(8,128)S(1)}, f32[512,128]{1,0:T(8,128)S(1)}, u32[]{:S(2)}, u32[]{:S(2)}) collective-permute-start(f32[512,128]{1,0:T(8,128)S(1)} %pick_rows.17), channel_id=1, source_target_pairs={{0,2},{2,4},{4,6},{6,7},{7,5},{5,3},{3,1},{1,0},{8,10},{10,12},{12... | collective-permute-start | bytes 786440 | tf_op jit(solution)/shard_map/ppermute | solution.py:284
  33.1 11.5 %collective-permute-start.19 = (f32[512,128]{1,0:T(8,128)S(1)}, f32[512,128]{1,0:T(8,128)S(1)}, u32[]{:S(2)}, u32[]{:S(2)}) collective-permute-start(f32[512,128]{1,0:T(8,128)S(1)} %pick_rows.30), channel_id=1, source_target_pairs={{0,1},{2,0},{4,2},{6,4},{7,6},{5,7},{3,5},{1,3},{8,9},{10,8},{12,1... | collective-permute-start | bytes 786440 | tf_op jit(solution)/shard_map/ppermute | solution.py:284
  35.6 11.1 %collective-permute-start.15 = (f32[512,128]{1,0:T(8,128)S(1)}, f32[512,128]{1,0:T(8,128)S(1)}, u32[]{:S(2)}, u32[]{:S(2)}) collective-permute-start(f32[512,128]{1,0:T(8,128)S(1)} %pick_rows.26), channel_id=1, source_target_pairs={{0,2},{2,4},{4,6},{6,7},{7,5},{5,3},{3,1},{1,0},{8,10},{10,12},{12... | collective-permute-start | bytes 786440 | tf_op jit(solution)/shard_map/ppermute | solution.py:284
  48.6 10.7 %collective-permute-start.12 = (f32[512,128]{1,0:T(8,128)S(1)}, f32[512,128]{1,0:T(8,128)S(1)}, u32[]{:S(2)}, u32[]{:S(2)}) collective-permute-start(f32[512,128]{1,0:T(8,128)S(1)} %pick_rows.23), channel_id=1, source_target_pairs={{0,1},{2,0},{4,2},{6,4},{7,6},{5,7},{3,5},{1,3},{8,9},{10,8},{12,1... | collective-permute-start | bytes 786440 | tf_op jit(solution)/shard_map/ppermute | solution.py:284
  50.7 10.4 %collective-permute-start.8 = (f32[512,128]{1,0:T(8,128)S(1)}, f32[512,128]{1,0:T(8,128)S(1)}, u32[]{:S(2)}, u32[]{:S(2)}) collective-permute-start(f32[512,128]{1,0:T(8,128)S(1)} %pick_rows.19), channel_id=1, source_target_pairs={{0,2},{2,4},{4,6},{6,7},{7,5},{5,3},{3,1},{1,0},{8,10},{10,12},{12... | collective-permute-start | bytes 786440 | tf_op jit(solution)/shard_map/ppermute | solution.py:284
  75.9 11.5 %collective-permute-start.30 = (f32[512,128]{1,0:T(8,128)S(1)}, f32[512,128]{1,0:T(8,128)S(1)}, u32[]{:S(2)}, u32[]{:S(2)}) collective-permute-start(f32[512,128]{1,0:T(8,128)S(1)} %column_product.5.refs_4_.refs_0_), channel_id=1, source_target_pairs={{0,1},{2,0},{4,2},{6,4},{7,6},{5,7},{3,5},{1,3},{8,9},{10,8},{12,1... | collective-permute-start | bytes 786440 | tf_op jit(solution)/shard_map/ppermute | solution.py:284
  77.6 11.4 %collective-permute-start.29 = (f32[512,128]{1,0:T(8,128)S(1)}, f32[512,128]{1,0:T(8,128)S(1)}, u32[]{:S(2)}, u32[]{:S(2)}) collective-permute-start(f32[512,128]{1,0:T(8,128)S(1)} %column_product.5.refs_4_.refs_0_), channel_id=1, source_target_pairs={{0,2},{2,4},{4,6},{6,7},{7,5},{5,3},{3,1},{1,0},{8,10},{10,12},{12... | collective-permute-start | bytes 786440 | tf_op jit(solution)/shard_map/ppermute | solution.py:284
  81.8 11.2 %collective-permute-start.32 = (f32[512,128]{1,0:T(8,128)S(1)}, f32[512,128]{1,0:T(8,128)S(1)}, u32[]{:S(2)}, u32[]{:S(2)}) collective-permute-start(f32[512,128]{1,0:T(8,128)S(1)} %collective-permute-done.28.refs_6_), channel_id=1, source_target_pairs={{0,1},{2,0},{4,2},{6,4},{7,6},{5,7},{3,5},{1,3},{8,9},{10,8},{12,1... | collective-permute-start | bytes 786440 | tf_op jit(solution)/shard_map/ppermute | solution.py:284
  83.4 11.2 %collective-permute-start.31 = (f32[512,128]{1,0:T(8,128)S(1)}, f32[512,128]{1,0:T(8,128)S(1)}, u32[]{:S(2)}, u32[]{:S(2)}) collective-permute-start(f32[512,128]{1,0:T(8,128)S(1)} %collective-permute-done.27.refs_5_), channel_id=1, source_target_pairs={{0,2},{2,4},{4,6},{6,7},{7,5},{5,3},{3,1},{1,0},{8,10},{10,12},{12... | collective-permute-start | bytes 786440 | tf_op jit(solution)/shard_map/ppermute | solution.py:284
  87.4 11.2 %collective-permute-start.34 = (f32[512,128]{1,0:T(8,128)S(1)}, f32[512,128]{1,0:T(8,128)S(1)}, u32[]{:S(2)}, u32[]{:S(2)}) collective-permute-start(f32[512,128]{1,0:T(8,128)S(1)} %collective-permute-done.30.refs_8_), channel_id=1, source_target_pairs={{0,1},{2,0},{4,2},{6,4},{7,6},{5,7},{3,5},{1,3},{8,9},{10,8},{12,1... | collective-permute-start | bytes 786440 | tf_op jit(solution)/shard_map/ppermute | solution.py:284
  89.0 11.2 %collective-permute-start.33 = (f32[512,128]{1,0:T(8,128)S(1)}, f32[512,128]{1,0:T(8,128)S(1)}, u32[]{:S(2)}, u32[]{:S(2)}) collective-permute-start(f32[512,128]{1,0:T(8,128)S(1)} %collective-permute-done.29.refs_7_), channel_id=1, source_target_pairs={{0,2},{2,4},{4,6},{6,7},{7,5},{5,3},{3,1},{1,0},{8,10},{10,12},{12... | collective-permute-start | bytes 786440 | tf_op jit(solution)/shard_map/ppermute | solution.py:284
  93.0 11.2 %collective-permute-start.36 = (f32[512,128]{1,0:T(8,128)S(1)}, f32[512,128]{1,0:T(8,128)S(1)}, u32[]{:S(2)}, u32[]{:S(2)}) collective-permute-start(f32[512,128]{1,0:T(8,128)S(1)} %collective-permute-done.32.refs_10_), channel_id=1, source_target_pairs={{0,1},{2,0},{4,2},{6,4},{7,6},{5,7},{3,5},{1,3},{8,9},{10,8},{12,1... | collective-permute-start | bytes 786440 | tf_op jit(solution)/shard_map/ppermute | solution.py:284
  94.6 11.3 %collective-permute-start.35 = (f32[512,128]{1,0:T(8,128)S(1)}, f32[512,128]{1,0:T(8,128)S(1)}, u32[]{:S(2)}, u32[]{:S(2)}) collective-permute-start(f32[512,128]{1,0:T(8,128)S(1)} %collective-permute-done.31.refs_9_), channel_id=1, source_target_pairs={{0,2},{2,4},{4,6},{6,7},{7,5},{5,3},{3,1},{1,0},{8,10},{10,12},{12... | collective-permute-start | bytes 786440 | tf_op jit(solution)/shard_map/ppermute | solution.py:284
  98.6 11.2 %collective-permute-start.38 = (f32[512,128]{1,0:T(8,128)S(1)}, f32[512,128]{1,0:T(8,128)S(1)}, u32[]{:S(2)}, u32[]{:S(2)}) collective-permute-start(f32[512,128]{1,0:T(8,128)S(1)} %collective-permute-done.34.refs_12_), channel_id=1, source_target_pairs={{0,1},{2,0},{4,2},{6,4},{7,6},{5,7},{3,5},{1,3},{8,9},{10,8},{12,1... | collective-permute-start | bytes 786440 | tf_op jit(solution)/shard_map/ppermute | solution.py:284
  100.2 11.3 %collective-permute-start.37 = (f32[512,128]{1,0:T(8,128)S(1)}, f32[512,128]{1,0:T(8,128)S(1)}, u32[]{:S(2)}, u32[]{:S(2)}) collective-permute-start(f32[512,128]{1,0:T(8,128)S(1)} %collective-permute-done.33.refs_11_), channel_id=1, source_target_pairs={{0,2},{2,4},{4,6},{6,7},{7,5},{5,3},{3,1},{1,0},{8,10},{10,12},{12... | collective-permute-start | bytes 786440 | tf_op jit(solution)/shard_map/ppermute | solution.py:284
  118.1 9.3 %collective-permute-start.45 = (f32[512,128]{1,0:T(8,128)S(1)}, f32[512,128]{1,0:T(8,128)S(1)}, u32[]{:S(2)}, u32[]{:S(2)}) collective-permute-start(f32[512,128]{1,0:T(8,128)S(1)} %row_product.4.refs_1_.refs_2_), channel_id=1, source_target_pairs={{0,16},{8,24},{16,0},{24,8},{1,17},{9,25},{17,1},{25,9},{2,18},{10... | collective-permute-start | bytes 786440 | tf_op jit(solution)/shard_map/ppermute | solution.py:293
  120.1 10.2 %collective-permute-start.46 = (f32[512,128]{1,0:T(8,128)S(1)}, f32[512,128]{1,0:T(8,128)S(1)}, u32[]{:S(2)}, u32[]{:S(2)}) collective-permute-start(f32[512,128]{1,0:T(8,128)S(1)} %row_product.5.refs_2_.refs_1_), channel_id=1, source_target_pairs={{0,16},{8,24},{16,0},{24,8},{1,17},{9,25},{17,1},{25,9},{2,18},{10... | collective-permute-start | bytes 786440 | tf_op jit(solution)/shard_map/ppermute | solution.py:293
  136.7 11.5 %collective-permute-start.52 = (f32[512,128]{1,0:T(8,128)S(1)}, f32[512,128]{1,0:T(8,128)S(1)}, u32[]{:S(2)}, u32[]{:S(2)}) collective-permute-start(f32[512,128]{1,0:T(8,128)S(1)} %column_product.7.refs_1_.refs_4_), channel_id=1, source_target_pairs={{0,1},{2,0},{4,2},{6,4},{7,6},{5,7},{3,5},{1,3},{8,9},{10,8},{12,1... | collective-permute-start | bytes 786440 | tf_op jit(solution)/shard_map/ppermute | solution.py:284
  138.3 11.5 %collective-permute-start.51 = (f32[512,128]{1,0:T(8,128)S(1)}, f32[512,128]{1,0:T(8,128)S(1)}, u32[]{:S(2)}, u32[]{:S(2)}) collective-permute-start(f32[512,128]{1,0:T(8,128)S(1)} %column_product.7.refs_1_.refs_4_), channel_id=1, source_target_pairs={{0,2},{2,4},{4,6},{6,7},{7,5},{5,3},{3,1},{1,0},{8,10},{10,12},{12... | collective-permute-start | bytes 786440 | tf_op jit(solution)/shard_map/ppermute | solution.py:284
  142.5 11.2 %collective-permute-start.54 = (f32[512,128]{1,0:T(8,128)S(1)}, f32[512,128]{1,0:T(8,128)S(1)}, u32[]{:S(2)}, u32[]{:S(2)}) collective-permute-start(f32[512,128]{1,0:T(8,128)S(1)} %collective-permute-done.50.refs_3_.refs_6_), channel_id=1, source_target_pairs={{0,1},{2,0},{4,2},{6,4},{7,6},{5,7},{3,5},{1,3},{8,9},{10,8},{12,1... | collective-permute-start | bytes 786440 | tf_op jit(solution)/shard_map/ppermute | solution.py:284
  144.1 11.2 %collective-permute-start.53 = (f32[512,128]{1,0:T(8,128)S(1)}, f32[512,128]{1,0:T(8,128)S(1)}, u32[]{:S(2)}, u32[]{:S(2)}) collective-permute-start(f32[512,128]{1,0:T(8,128)S(1)} %collective-permute-done.49.refs_2_.refs_5_), channel_id=1, source_target_pairs={{0,2},{2,4},{4,6},{6,7},{7,5},{5,3},{3,1},{1,0},{8,10},{10,12},{12... | collective-permute-start | bytes 786440 | tf_op jit(solution)/shard_map/ppermute | solution.py:284
  148.1 11.2 %collective-permute-start.56 = (f32[512,128]{1,0:T(8,128)S(1)}, f32[512,128]{1,0:T(8,128)S(1)}, u32[]{:S(2)}, u32[]{:S(2)}) collective-permute-start(f32[512,128]{1,0:T(8,128)S(1)} %collective-permute-done.52.refs_5_.refs_8_), channel_id=1, source_target_pairs={{0,1},{2,0},{4,2},{6,4},{7,6},{5,7},{3,5},{1,3},{8,9},{10,8},{12,1... | collective-permute-start | bytes 786440 | tf_op jit(solution)/shard_map/ppermute | solution.py:284
  149.8 11.2 %collective-permute-start.55 = (f32[512,128]{1,0:T(8,128)S(1)}, f32[512,128]{1,0:T(8,128)S(1)}, u32[]{:S(2)}, u32[]{:S(2)}) collective-permute-start(f32[512,128]{1,0:T(8,128)S(1)} %collective-permute-done.51.refs_4_.refs_7_), channel_id=1, source_target_pairs={{0,2},{2,4},{4,6},{6,7},{7,5},{5,3},{3,1},{1,0},{8,10},{10,12},{12... | collective-permute-start | bytes 786440 | tf_op jit(solution)/shard_map/ppermute | solution.py:284
  153.8 11.2 %collective-permute-start.58 = (f32[512,128]{1,0:T(8,128)S(1)}, f32[512,128]{1,0:T(8,128)S(1)}, u32[]{:S(2)}, u32[]{:S(2)}) collective-permute-start(f32[512,128]{1,0:T(8,128)S(1)} %collective-permute-done.54.refs_7_.refs_10_), channel_id=1, source_target_pairs={{0,1},{2,0},{4,2},{6,4},{7,6},{5,7},{3,5},{1,3},{8,9},{10,8},{12,1... | collective-permute-start | bytes 786440 | tf_op jit(solution)/shard_map/ppermute | solution.py:284
  155.4 11.3 %collective-permute-start.57 = (f32[512,128]{1,0:T(8,128)S(1)}, f32[512,128]{1,0:T(8,128)S(1)}, u32[]{:S(2)}, u32[]{:S(2)}) collective-permute-start(f32[512,128]{1,0:T(8,128)S(1)} %collective-permute-done.53.refs_6_.refs_9_), channel_id=1, source_target_pairs={{0,2},{2,4},{4,6},{6,7},{7,5},{5,3},{3,1},{1,0},{8,10},{10,12},{12... | collective-permute-start | bytes 786440 | tf_op jit(solution)/shard_map/ppermute | solution.py:284
  159.4 11.2 %collective-permute-start.60 = (f32[512,128]{1,0:T(8,128)S(1)}, f32[512,128]{1,0:T(8,128)S(1)}, u32[]{:S(2)}, u32[]{:S(2)}) collective-permute-start(f32[512,128]{1,0:T(8,128)S(1)} %collective-permute-done.56.refs_9_.refs_12_), channel_id=1, source_target_pairs={{0,1},{2,0},{4,2},{6,4},{7,6},{5,7},{3,5},{1,3},{8,9},{10,8},{12,1... | collective-permute-start | bytes 786440 | tf_op jit(solution)/shard_map/ppermute | solution.py:284
  161.0 11.3 %collective-permute-start.59 = (f32[512,128]{1,0:T(8,128)S(1)}, f32[512,128]{1,0:T(8,128)S(1)}, u32[]{:S(2)}, u32[]{:S(2)}) collective-permute-start(f32[512,128]{1,0:T(8,128)S(1)} %collective-permute-done.55.refs_8_.refs_11_), channel_id=1, source_target_pairs={{0,2},{2,4},{4,6},{6,7},{7,5},{5,3},{3,1},{1,0},{8,10},{10,12},{12... | collective-permute-start | bytes 786440 | tf_op jit(solution)/shard_map/ppermute | solution.py:284
  178.9 11.3 %collective-permute-start.67 = (f32[512,128]{1,0:T(8,128)S(1)}, f32[512,128]{1,0:T(8,128)S(1)}, u32[]{:S(2)}, u32[]{:S(2)}) collective-permute-start(f32[512,128]{1,0:T(8,128)S(1)} %row_product.6.refs_0_), channel_id=1, source_target_pairs={{0,16},{8,24},{16,0},{24,8},{1,17},{9,25},{17,1},{25,9},{2,18},{10... | collective-permute-start | bytes 786440 | tf_op jit(solution)/shard_map/ppermute | solution.py:293
  181.0 9.9 %collective-permute-start.68 = (f32[512,128]{1,0:T(8,128)S(1)}, f32[512,128]{1,0:T(8,128)S(1)}, u32[]{:S(2)}, u32[]{:S(2)}) collective-permute-start(f32[512,128]{1,0:T(8,128)S(1)} %row_product.7.refs_1_), channel_id=1, source_target_pairs={{0,16},{8,24},{16,0},{24,8},{1,17},{9,25},{17,1},{25,9},{2,18},{10... | collective-permute-start | bytes 786440 | tf_op jit(solution)/shard_map/ppermute | solution.py:293
  (51 other events, 306.0 us)
